TPU v7x, 256 devices: a whole 4x4x8 slice. The times are simulated.
256 devices in a mesh: ctx: 32 (over z, y_lo, core), tp: 8 (over y_hi, x).
Axes of the slice: x: 4, y: 4 (y_hi: 2, y_lo: 2; y = y_hi * 2 + y_lo), z: 8, core: 2. Of those that a mesh axis runs over, the one named last changes fastest.
Arguments:
- query_in: bfloat16 [8192, 8192], P('ctx', 'tp'), may hold values from -6 to 6
- key_in: bfloat16 [8192, 8192], P('ctx', 'tp'), may hold values from -6 to 6
- value_in: bfloat16 [8192, 8192], P('ctx', 'tp'), may hold values from -6 to 6
- cotangent: bfloat16 [8192, 8192], P('ctx', 'tp'), may hold values from -6 to 6
- short_weight: float32 [3, 3, 8192], P(None, None, 'tp'), may hold values from -3 to 3
- long_filter: bfloat16 [8192, 8192], P('ctx', 'tp'), may hold values from -1.5 to 1.5
Outputs:
- block_out: bfloat16 [8192, 8192], P('ctx', 'tp')
- grad_query: bfloat16 [8192, 8192], P('ctx', 'tp')
- grad_key: bfloat16 [8192, 8192], P('ctx', 'tp')
- grad_value: bfloat16 [8192, 8192], P('ctx', 'tp')
- grad_short: float32 [3, 3, 8192], P(None, None, 'tp')
- grad_filter: bfloat16 [8192, 8192], P('ctx', 'tp')
All inputs are finite; a program needn't handle non-finite values.
Results may differ from a plain program's by a relative error of at most 0.025.
Values may be sent and summed in bfloat16 or wider, within the bound.
No kernel may reach another device: no remote copies, remote signals or barrier semaphores. Data moves between devices by JAX's collectives and lax.ppermute only.
A program may use at most 64 MiB of HBM per device.

v0:
```python
import math

import jax
import jax.numpy as jnp
from jax import lax
from jax.sharding import PartitionSpec as P

S = 128


def from_behind(x, axis, by):
    count = lax.axis_size(axis)
    pairs = [(i, i + by) for i in range(count) if 0 <= i + by < count]
    return lax.ppermute(x, axis, pairs)


def phase_grid(left_index, right_index, period):
    product = left_index[:, None] * right_index[None, :] % period
    phases = 2.0 * math.pi / period * product.astype(jnp.float32)
    return (jnp.cos(phases), jnp.sin(phases))


def short_filter(extended, weights, local_rows):
    tap_count = weights.shape[0]
    result = jnp.zeros((local_rows, extended.shape[1]), jnp.float32)
    for lag_index in range(tap_count):
        offset_row = tap_count - 1 - lag_index
        result = result + weights[lag_index] * extended[
            offset_row : offset_row + local_rows
        ].astype(jnp.float32)
    return result


def filter_back(extended, weights, local_rows):
    tap_count = weights.shape[0]
    result = jnp.zeros((local_rows, extended.shape[1]), jnp.float32)
    for lag_index in range(tap_count):
        result = result + weights[lag_index] * extended[lag_index : lag_index + local_rows].astype(
            jnp.float32
        )
    return result


def weight_terms(grads, extended, tap_count, local_rows):
    grad_float = grads.astype(jnp.float32)
    terms = []
    for lag_index in range(tap_count):
        offset_row = tap_count - 1 - lag_index
        terms.append(
            jnp.sum(
                grad_float * extended[offset_row : offset_row + local_rows].astype(jnp.float32),
                axis=0,
            )
        )
    return jnp.stack(terms)


def spectral_product(spec_re, spec_im, filt_re, filt_im):
    spec_re = spec_re.astype(jnp.float32)
    spec_im = spec_im.astype(jnp.float32)
    prod_re = spec_re * filt_re - spec_im * filt_im
    prod_im = spec_re * filt_im + spec_im * filt_re
    return (prod_re.astype(jnp.bfloat16), prod_im.astype(jnp.bfloat16))


def on_device(query_in, key_in, value_in, cotangent, short_weight, long_filter):
    local_rows, channels = query_in.shape
    tap_count = short_weight.shape[1]
    rim_rows = tap_count - 1
    ctx_size = lax.axis_size("ctx")
    ctx_rank = lax.axis_index("ctx")
    length = local_rows * ctx_size
    fft_size = 2 * length
    inner_len = S
    outer_len = fft_size // inner_len
    half_rows = outer_len // 2
    inv_root = 1.0 / math.sqrt(length)
    outer_ids = jnp.arange(outer_len, dtype=jnp.int32)
    half_ids = jnp.arange(half_rows, dtype=jnp.int32)
    inner_ids = jnp.arange(inner_len, dtype=jnp.int32)
    cos_first, sin_first = phase_grid(outer_ids, half_ids, outer_len)
    cos_first = cos_first.astype(jnp.bfloat16)
    sin_first = sin_first.astype(jnp.bfloat16)
    cos_back, sin_back = phase_grid(half_ids, outer_ids, outer_len)
    cos_back = cos_back.astype(jnp.bfloat16)
    sin_back = sin_back.astype(jnp.bfloat16)
    cos_inner, sin_inner = phase_grid(inner_ids, inner_ids, inner_len)
    cos_inner = cos_inner.astype(jnp.bfloat16)
    sin_inner = sin_inner.astype(jnp.bfloat16)
    ahead = from_behind(
        (
            query_in[local_rows - rim_rows :],
            key_in[local_rows - rim_rows :],
            value_in[local_rows - rim_rows :],
        ),
        "ctx",
        1,
    )
    ext_query = jnp.concatenate([ahead[0], query_in], axis=0)
    ext_key = jnp.concatenate([ahead[1], key_in], axis=0)
    ext_value = jnp.concatenate([ahead[2], value_in], axis=0)
    q_short = short_filter(ext_query, short_weight[0], local_rows)
    k_short = short_filter(ext_key, short_weight[1], local_rows)
    v_short = short_filter(ext_value, short_weight[2], local_rows)
    mixed = (k_short * v_short).astype(jnp.bfloat16)
    inner_part = inner_len // ctx_size
    k_rows = outer_len // ctx_size
    row_ids = ctx_rank * k_rows + jnp.arange(k_rows, dtype=jnp.int32)
    fwd_cos, fwd_sin = phase_grid(
        outer_ids, ctx_rank * inner_part + jnp.arange(inner_part, dtype=jnp.int32), fft_size
    )
    fwd_cos = fwd_cos[:, :, None]
    fwd_sin = fwd_sin[:, :, None]
    inv_cos, inv_sin = phase_grid(row_ids, inner_ids, fft_size)
    inv_cos = inv_cos[:, :, None]
    inv_sin = inv_sin[:, :, None]

    def forward_transform(signal):
        grid_rows = signal.reshape(local_rows // inner_len, inner_len, channels)
        arrived = lax.all_to_all(grid_rows, "ctx", split_axis=1, concat_axis=0, tiled=True)
        flattened = arrived.reshape(half_rows, inner_part * channels)
        first_re = jnp.dot(cos_first, flattened, preferred_element_type=jnp.float32).reshape(
            outer_len, inner_part, channels
        )
        first_im = -jnp.dot(sin_first, flattened, preferred_element_type=jnp.float32).reshape(
            outer_len, inner_part, channels
        )
        twist_re = (first_re * fwd_cos + first_im * fwd_sin).astype(jnp.bfloat16)
        twist_im = (first_im * fwd_cos - first_re * fwd_sin).astype(jnp.bfloat16)
        spread = (
            lax.all_to_all(twist_re, "ctx", split_axis=0, concat_axis=1, tiled=True),
            lax.all_to_all(twist_im, "ctx", split_axis=0, concat_axis=1, tiled=True),
        )
        spec_re = jnp.einsum(
            "js,ksc->kjc", cos_inner, spread[0], preferred_element_type=jnp.float32
        ) + jnp.einsum("js,ksc->kjc", sin_inner, spread[1], preferred_element_type=jnp.float32)
        spec_im = jnp.einsum(
            "js,ksc->kjc", cos_inner, spread[1], preferred_element_type=jnp.float32
        ) - jnp.einsum("js,ksc->kjc", sin_inner, spread[0], preferred_element_type=jnp.float32)
        return (spec_re.astype(jnp.bfloat16), spec_im.astype(jnp.bfloat16))

    def inverse_transform(spec_re, spec_im):
        back_re = jnp.einsum(
            "sj,kjc->ksc", cos_inner, spec_re, preferred_element_type=jnp.float32
        ) - jnp.einsum("sj,kjc->ksc", sin_inner, spec_im, preferred_element_type=jnp.float32)
        back_im = jnp.einsum(
            "sj,kjc->ksc", cos_inner, spec_im, preferred_element_type=jnp.float32
        ) + jnp.einsum("sj,kjc->ksc", sin_inner, spec_re, preferred_element_type=jnp.float32)
        untw_re = (back_re * inv_cos - back_im * inv_sin).astype(jnp.bfloat16)
        untw_im = (back_im * inv_cos + back_re * inv_sin).astype(jnp.bfloat16)
        arrived = (
            lax.all_to_all(untw_re, "ctx", split_axis=1, concat_axis=0, tiled=True),
            lax.all_to_all(untw_im, "ctx", split_axis=1, concat_axis=0, tiled=True),
        )
        signal = jnp.dot(
            cos_back,
            arrived[0].reshape(outer_len, inner_part * channels),
            preferred_element_type=jnp.float32,
        ) - jnp.dot(
            sin_back,
            arrived[1].reshape(outer_len, inner_part * channels),
            preferred_element_type=jnp.float32,
        )
        signal = (
            (signal * (1.0 / fft_size))
            .astype(jnp.bfloat16)
            .reshape(half_rows, inner_part, channels)
        )
        returned = lax.all_to_all(signal, "ctx", split_axis=0, concat_axis=1, tiled=True)
        return returned.reshape(local_rows, channels)

    spec_h = forward_transform(long_filter)
    h_re = spec_h[0].astype(jnp.float32)
    h_im = spec_h[1].astype(jnp.float32)
    spec_x = forward_transform(mixed)
    product = spectral_product(spec_x[0], spec_x[1], h_re, h_im)
    conv = inverse_transform(product[0], product[1]).astype(jnp.float32)
    block_out = (q_short * conv).astype(jnp.bfloat16)
    cot_float = cotangent.astype(jnp.float32)
    gq_short = (cot_float * conv).astype(jnp.bfloat16)
    grad_conv = (cot_float * q_short).astype(jnp.bfloat16)
    spec_g = forward_transform(grad_conv)
    back_product = spectral_product(spec_g[0], spec_g[1], h_re, -h_im)
    grad_mixed = inverse_transform(back_product[0], back_product[1]).astype(jnp.float32)
    gk_short = (grad_mixed * v_short).astype(jnp.bfloat16)
    gv_short = (grad_mixed * k_short).astype(jnp.bfloat16)
    x_re = spec_x[0].astype(jnp.float32)
    x_im = spec_x[1].astype(jnp.float32)
    g_re = spec_g[0].astype(jnp.float32)
    g_im = spec_g[1].astype(jnp.float32)
    cross_re = ((g_re * x_re + g_im * x_im) * inv_root).astype(jnp.bfloat16)
    cross_im = ((g_im * x_re - g_re * x_im) * inv_root).astype(jnp.bfloat16)
    grad_filter = inverse_transform(cross_re, cross_im)
    behind = from_behind((gq_short[:rim_rows], gk_short[:rim_rows], gv_short[:rim_rows]), "ctx", -1)
    ext_gq = jnp.concatenate([gq_short, behind[0]], axis=0)
    ext_gk = jnp.concatenate([gk_short, behind[1]], axis=0)
    ext_gv = jnp.concatenate([gv_short, behind[2]], axis=0)
    grad_query = filter_back(ext_gq, short_weight[0], local_rows).astype(jnp.bfloat16)
    grad_key = filter_back(ext_gk, short_weight[1], local_rows).astype(jnp.bfloat16)
    grad_value = filter_back(ext_gv, short_weight[2], local_rows).astype(jnp.bfloat16)
    short_part = jnp.stack(
        [
            weight_terms(gq_short, ext_query, tap_count, local_rows),
            weight_terms(gk_short, ext_key, tap_count, local_rows),
            weight_terms(gv_short, ext_value, tap_count, local_rows),
        ]
    )
    short_total = lax.psum(short_part.astype(jnp.bfloat16), "ctx").astype(jnp.float32)
    grad_short = short_total * inv_root
    return (block_out, grad_query, grad_key, grad_value, grad_short, grad_filter)


def solution(mesh):
    in_specs = (
        P("ctx", "tp"),
        P("ctx", "tp"),
        P("ctx", "tp"),
        P("ctx", "tp"),
        P(None, None, "tp"),
        P("ctx", "tp"),
    )
    out_specs = (
        P("ctx", "tp"),
        P("ctx", "tp"),
        P("ctx", "tp"),
        P("ctx", "tp"),
        P(None, None, "tp"),
        P("ctx", "tp"),
    )
    return jax.shard_map(
        on_device, mesh=mesh, in_specs=in_specs, out_specs=out_specs, check_vma=False
    )
```

profile of v0, /device:TPU:1, one launch (start us, length us, event | category | flops | bytes accessed | tf_op | source)
XLA Modules:
  0.0 707.7 jit_solution(17484825310666465228)
XLA Ops:
  3.1 11.1 %all-to-all-start.3 = ((bf16[2,128,1024]{2,0,1:T(2,128)(2,1)}), bf16[2,128,1024]{2,0,1:T(2,128)(2,1)S(1)}, u32[]{:S(2)}, u32[]{:S(2)}) async-start(bf16[2,128,1024]{2,0,1:T(2,128)(2,1)} %copy.115), calls=%async_computation.3 | async-start | bytes 1048576 | tf_op jit(solution)/shard_map/all_to_all | solution.py:120
  23.2 7.8 %all-to-all-done.3 = bf16[2,128,1024]{2,0,1:T(2,128)(2,1)S(1)} async-done(((bf16[2,128,1024]{2,0,1:T(2,128)(2,1)}), bf16[2,128,1024]{2,0,1:T(2,128)(2,1)S(1)}, u32[]{:S(2)}, u32[]{:S(2)}) %all-to-all-start.3) | async-done | bytes 524320 | tf_op jit(solution)/shard_map/all_to_all | solution.py:120
  31.0 6.4 all-to-all-start
  43.7 10.4 %all-to-all-done = bf16[2,128,1024]{2,0,1:T(2,128)(2,1)S(1)} async-done(((bf16[2,128,1024]{2,0,1:T(2,128)(2,1)}), bf16[2,128,1024]{2,0,1:T(2,128)(2,1)S(1)}, u32[]{:S(2)}, u32[]{:S(2)}) %all-to-all-start) | async-done | bytes 524320 | tf_op jit(solution)/shard_map/all_to_all | solution.py:120
  54.1 6.2 all-to-all-start.9
  67.2 9.8 %all-to-all-done.9 = bf16[2,128,1024]{2,0,1:T(2,128)(2,1)} async-done(((bf16[2,128,1024]{2,0,1:T(2,128)(2,1)}), bf16[2,128,1024]{2,0,1:T(2,128)(2,1)}, u32[]{:S(2)}, u32[]{:S(2)}) %all-to-all-start.9) | async-done | bytes 524320 | tf_op jit(solution)/shard_map/all_to_all | solution.py:120
  94.0 26.4 %all-to-all-done.10 = bf16[128,4,1024]{2,1,0:T(4,128)(2,1)} async-done(((bf16[128,4,1024]{2,1,0:T(4,128)(2,1)}), bf16[128,4,1024]{2,1,0:T(4,128)(2,1)}, u32[]{:S(2)}, u32[]{:S(2)}) %all-to-all-start.10) | async-done | bytes 1048608 | tf_op jit(solution)/shard_map/all_to_all | solution.py:131
  128.1 26.4 %all-to-all-done.11 = bf16[128,4,1024]{2,1,0:T(4,128)(2,1)} async-done(((bf16[128,4,1024]{2,1,0:T(4,128)(2,1)}), bf16[128,4,1024]{2,1,0:T(4,128)(2,1)}, u32[]{:S(2)}, u32[]{:S(2)}) %all-to-all-start.11) | async-done | bytes 1048608 | tf_op jit(solution)/shard_map/all_to_all | solution.py:132
  162.0 26.4 %all-to-all-done.5 = bf16[128,4,1024]{2,1,0:T(4,128)(2,1)} async-done(((bf16[128,4,1024]{2,1,0:T(4,128)(2,1)}), bf16[128,4,1024]{2,1,0:T(4,128)(2,1)}, u32[]{:S(2)}, u32[]{:S(2)}) %all-to-all-start.5) | async-done | bytes 1048608 | tf_op jit(solution)/shard_map/all_to_all | solution.py:132
  195.2 26.4 %all-to-all-done.4 = bf16[128,4,1024]{2,1,0:T(4,128)(2,1)S(1)} async-done(((bf16[128,4,1024]{2,1,0:T(4,128)(2,1)}), bf16[128,4,1024]{2,1,0:T(4,128)(2,1)S(1)}, u32[]{:S(2)}, u32[]{:S(2)}) %all-to-all-start.4) | async-done | bytes 1048608 | tf_op jit(solution)/shard_map/all_to_all | solution.py:131
  228.3 26.4 %all-to-all-done.2 = bf16[128,4,1024]{2,1,0:T(4,128)(2,1)S(1)} async-done(((bf16[128,4,1024]{2,1,0:T(4,128)(2,1)}), bf16[128,4,1024]{2,1,0:T(4,128)(2,1)S(1)}, u32[]{:S(2)}, u32[]{:S(2)}) %all-to-all-start.2) | async-done | bytes 1048608 | tf_op jit(solution)/shard_map/all_to_all | solution.py:132
  280.4 8.2 %all-to-all-done.1 = bf16[128,4,1024]{2,1,0:T(4,128)(2,1)} async-done(((bf16[128,4,1024]{2,1,0:T(4,128)(2,1)}), bf16[128,4,1024]{2,1,0:T(4,128)(2,1)}, u32[]{:S(2)}, u32[]{:S(2)}) %all-to-all-start.1) | async-done | bytes 1048608 | tf_op jit(solution)/shard_map/all_to_all | solution.py:131
  326.1 26.5 %all-to-all-done.16 = bf16[4,128,1024]{2,0,1:T(4,128)(2,1)S(1)} async-done(((bf16[4,128,1024]{2,0,1:T(4,128)(2,1)}), bf16[4,128,1024]{2,0,1:T(4,128)(2,1)S(1)}, u32[]{:S(2)}, u32[]{:S(2)}) %all-to-all-start.16) | async-done | bytes 1048608 | tf_op jit(solution)/shard_map/all_to_all | solution.py:153
  359.3 26.5 %all-to-all-done.15 = bf16[4,128,1024]{2,0,1:T(4,128)(2,1)S(1)} async-done(((bf16[4,128,1024]{2,0,1:T(4,128)(2,1)}), bf16[4,128,1024]{2,0,1:T(4,128)(2,1)S(1)}, u32[]{:S(2)}, u32[]{:S(2)}) %all-to-all-start.15) | async-done | bytes 1048608 | tf_op jit(solution)/shard_map/all_to_all | solution.py:152
  393.4 25.5 %all-to-all-done.6 = bf16[4,128,1024]{2,0,1:T(4,128)(2,1)S(1)} async-done(((bf16[4,128,1024]{2,0,1:T(4,128)(2,1)}), bf16[4,128,1024]{2,0,1:T(4,128)(2,1)S(1)}, u32[]{:S(2)}, u32[]{:S(2)}) %all-to-all-start.6) | async-done | bytes 1048608 | tf_op jit(solution)/shard_map/all_to_all | solution.py:152
  426.6 25.5 %all-to-all-done.7 = bf16[4,128,1024]{2,0,1:T(4,128)(2,1)S(1)} async-done(((bf16[4,128,1024]{2,0,1:T(4,128)(2,1)}), bf16[4,128,1024]{2,0,1:T(4,128)(2,1)S(1)}, u32[]{:S(2)}, u32[]{:S(2)}) %all-to-all-start.7) | async-done | bytes 1048608 | tf_op jit(solution)/shard_map/all_to_all | solution.py:153
  460.8 25.5 %all-to-all-done.12 = bf16[4,128,1024]{2,0,1:T(4,128)(2,1)S(1)} async-done(((bf16[4,128,1024]{2,0,1:T(4,128)(2,1)}), bf16[4,128,1024]{2,0,1:T(4,128)(2,1)S(1)}, u32[]{:S(2)}, u32[]{:S(2)}) %all-to-all-start.12) | async-done | bytes 1048608 | tf_op jit(solution)/shard_map/all_to_all | solution.py:152
  486.3 6.0 all-to-all-start.13
  496.5 23.8 %all-to-all-done.13 = bf16[4,128,1024]{2,0,1:T(4,128)(2,1)} async-done(((bf16[4,128,1024]{2,0,1:T(4,128)(2,1)}), bf16[4,128,1024]{2,0,1:T(4,128)(2,1)}, u32[]{:S(2)}, u32[]{:S(2)}) %all-to-all-start.13) | async-done | bytes 1048608 | tf_op jit(solution)/shard_map/all_to_all | solution.py:153
  529.5 12.9 %all-to-all-done.17 = bf16[64,4,1024]{2,1,0:T(4,128)(2,1)S(1)} async-done(((bf16[64,4,1024]{2,1,0:T(4,128)(2,1)}), bf16[64,4,1024]{2,1,0:T(4,128)(2,1)S(1)}, u32[]{:S(2)}, u32[]{:S(2)}) %all-to-all-start.17) | async-done | bytes 524320 | tf_op jit(solution)/shard_map/all_to_all | solution.py:169
  552.3 12.0 %all-to-all-done.8 = bf16[64,4,1024]{2,1,0:T(4,128)(2,1)S(1)} async-done(((bf16[64,4,1024]{2,1,0:T(4,128)(2,1)}), bf16[64,4,1024]{2,1,0:T(4,128)(2,1)S(1)}, u32[]{:S(2)}, u32[]{:S(2)}) %all-to-all-start.8) | async-done | bytes 524320 | tf_op jit(solution)/shard_map/all_to_all | solution.py:169
  577.2 10.0 %all-to-all-done.14 = bf16[64,4,1024]{2,1,0:T(4,128)(2,1)} async-done(((bf16[64,4,1024]{2,1,0:T(4,128)(2,1)}), bf16[64,4,1024]{2,1,0:T(4,128)(2,1)}, u32[]{:S(2)}, u32[]{:S(2)}) %all-to-all-start.14) | async-done | bytes 524320 | tf_op jit(solution)/shard_map/all_to_all | solution.py:169
  597.4 100.5 %psum.7 = bf16[3,3,1024]{2,1,0:T(4,128)(2,1)S(1)} all-reduce(bf16[3,3,1024]{2,1,0:T(4,128)(2,1)S(1)} %pad_maximum_fusion.6), channel_id=1, replica_groups=mesh['ctx'=32,'tp'=8] {'ctx'}, use_global_device_ids=true, to_apply=%region_9.10 | all-reduce | flops 9216 | bytes 36864 | tf_op jit(solution)/shard_map/psum | solution.py:208
  697.9 6.3 collective-permute-start.4
  (192 shorter events, 212.7 us)
Async XLA Ops:
  3.1 27.9 %all-to-all-start.3 = ((bf16[2,128,1024]{2,0,1:T(2,128)(2,1)}), bf16[2,128,1024]{2,0,1:T(2,128)(2,1)S(1)}, u32[]{:S(2)}, u32[]{:S(2)}) async-start(bf16[2,128,1024]{2,0,1:T(2,128)(2,1)} %copy.115), calls=%async_computation.3 | async-start | bytes 1048576 | tf_op jit(solution)/shard_map/all_to_all | solution.py:120
  14.3 5.8 collective-permute-start.2
  18.0 3.1 collective-permute-start.1
  31.0 23.1 %all-to-all-start = ((bf16[2,128,1024]{2,0,1:T(2,128)(2,1)}), bf16[2,128,1024]{2,0,1:T(2,128)(2,1)S(1)}, u32[]{:S(2)}, u32[]{:S(2)}) async-start(bf16[2,128,1024]{2,0,1:T(2,128)(2,1)} %copy.105), calls=%async_computation | async-start | bytes 1048576 | tf_op jit(solution)/shard_map/all_to_all | solution.py:120
  37.4 4.3 collective-permute-start
  54.1 23.0 %all-to-all-start.9 = ((bf16[2,128,1024]{2,0,1:T(2,128)(2,1)}), bf16[2,128,1024]{2,0,1:T(2,128)(2,1)}, u32[]{:S(2)}, u32[]{:S(2)}) async-start(bf16[2,128,1024]{2,0,1:T(2,128)(2,1)} %copy.134), calls=%async_computation.9 | async-start | bytes 1048576 | tf_op jit(solution)/shard_map/all_to_all | solution.py:120
  86.4 34.0 %all-to-all-start.10 = ((bf16[128,4,1024]{2,1,0:T(4,128)(2,1)}), bf16[128,4,1024]{2,1,0:T(4,128)(2,1)}, u32[]{:S(2)}, u32[]{:S(2)}) async-start(bf16[128,4,1024]{2,1,0:T(4,128)(2,1)} %copy.138), calls=%async_computation.10 | async-start | bytes 2097152 | tf_op jit(solution)/shard_map/all_to_all | solution.py:131
  120.4 34.1 %all-to-all-start.11 = ((bf16[128,4,1024]{2,1,0:T(4,128)(2,1)}), bf16[128,4,1024]{2,1,0:T(4,128)(2,1)}, u32[]{:S(2)}, u32[]{:S(2)}) async-start(bf16[128,4,1024]{2,1,0:T(4,128)(2,1)} %copy.141), calls=%async_computation.11 | async-start | bytes 2097152 | tf_op jit(solution)/shard_map/all_to_all | solution.py:132
  154.5 33.9 %all-to-all-start.5 = ((bf16[128,4,1024]{2,1,0:T(4,128)(2,1)}), bf16[128,4,1024]{2,1,0:T(4,128)(2,1)}, u32[]{:S(2)}, u32[]{:S(2)}) async-start(bf16[128,4,1024]{2,1,0:T(4,128)(2,1)} %copy.122), calls=%async_computation.5 | async-start | bytes 2097152 | tf_op jit(solution)/shard_map/all_to_all | solution.py:132
  188.4 33.2 %all-to-all-start.4 = ((bf16[128,4,1024]{2,1,0:T(4,128)(2,1)}), bf16[128,4,1024]{2,1,0:T(4,128)(2,1)S(1)}, u32[]{:S(2)}, u32[]{:S(2)}) async-start(bf16[128,4,1024]{2,1,0:T(4,128)(2,1)} %copy.119), calls=%async_computation.4 | async-start | bytes 2097152 | tf_op jit(solution)/shard_map/all_to_all | solution.py:131
  221.6 33.2 %all-to-all-start.2 = ((bf16[128,4,1024]{2,1,0:T(4,128)(2,1)}), bf16[128,4,1024]{2,1,0:T(4,128)(2,1)S(1)}, u32[]{:S(2)}, u32[]{:S(2)}) async-start(bf16[128,4,1024]{2,1,0:T(4,128)(2,1)} %copy.112), calls=%async_computation.2 | async-start | bytes 2097152 | tf_op jit(solution)/shard_map/all_to_all | solution.py:132
  254.8 33.9 %all-to-all-start.1 = ((bf16[128,4,1024]{2,1,0:T(4,128)(2,1)}), bf16[128,4,1024]{2,1,0:T(4,128)(2,1)}, u32[]{:S(2)}, u32[]{:S(2)}) async-start(bf16[128,4,1024]{2,1,0:T(4,128)(2,1)} %copy.109), calls=%async_computation.1 | async-start | bytes 2097152 | tf_op jit(solution)/shard_map/all_to_all | solution.py:131
  319.4 33.2 %all-to-all-start.16 = ((bf16[4,128,1024]{2,0,1:T(4,128)(2,1)}), bf16[4,128,1024]{2,0,1:T(4,128)(2,1)S(1)}, u32[]{:S(2)}, u32[]{:S(2)}) async-start(bf16[4,128,1024]{2,0,1:T(4,128)(2,1)} %copy.153), calls=%async_computation.16 | async-start | bytes 2097152 | tf_op jit(solution)/shard_map/all_to_all | solution.py:153
  352.6 33.2 %all-to-all-start.15 = ((bf16[4,128,1024]{2,0,1:T(4,128)(2,1)}), bf16[4,128,1024]{2,0,1:T(4,128)(2,1)S(1)}, u32[]{:S(2)}, u32[]{:S(2)}) async-start(bf16[4,128,1024]{2,0,1:T(4,128)(2,1)} %copy.151), calls=%async_computation.15 | async-start | bytes 2097152 | tf_op jit(solution)/shard_map/all_to_all | solution.py:152
  385.8 33.2 %all-to-all-start.6 = ((bf16[4,128,1024]{2,0,1:T(4,128)(2,1)}), bf16[4,128,1024]{2,0,1:T(4,128)(2,1)S(1)}, u32[]{:S(2)}, u32[]{:S(2)}) async-start(bf16[4,128,1024]{2,0,1:T(4,128)(2,1)} %copy.129), calls=%async_computation.6 | async-start | bytes 2097152 | tf_op jit(solution)/shard_map/all_to_all | solution.py:152
  419.0 33.2 %all-to-all-start.7 = ((bf16[4,128,1024]{2,0,1:T(4,128)(2,1)}), bf16[4,128,1024]{2,0,1:T(4,128)(2,1)S(1)}, u32[]{:S(2)}, u32[]{:S(2)}) async-start(bf16[4,128,1024]{2,0,1:T(4,128)(2,1)} %copy.131), calls=%async_computation.7 | async-start | bytes 2097152 | tf_op jit(solution)/shard_map/all_to_all | solution.py:153
  453.1 33.2 %all-to-all-start.12 = ((bf16[4,128,1024]{2,0,1:T(4,128)(2,1)}), bf16[4,128,1024]{2,0,1:T(4,128)(2,1)S(1)}, u32[]{:S(2)}, u32[]{:S(2)}) async-start(bf16[4,128,1024]{2,0,1:T(4,128)(2,1)} %copy.146), calls=%async_computation.12 | async-start | bytes 2097152 | tf_op jit(solution)/shard_map/all_to_all | solution.py:152
  486.3 34.1 %all-to-all-start.13 = ((bf16[4,128,1024]{2,0,1:T(4,128)(2,1)}), bf16[4,128,1024]{2,0,1:T(4,128)(2,1)}, u32[]{:S(2)}, u32[]{:S(2)}) async-start(bf16[4,128,1024]{2,0,1:T(4,128)(2,1)} %copy.148), calls=%async_computation.13 | async-start | bytes 2097152 | tf_op jit(solution)/shard_map/all_to_all | solution.py:153
  520.3 22.0 %all-to-all-start.17 = ((bf16[64,4,1024]{2,1,0:T(4,128)(2,1)}), bf16[64,4,1024]{2,1,0:T(4,128)(2,1)S(1)}, u32[]{:S(2)}, u32[]{:S(2)}) async-start(bf16[64,4,1024]{2,1,0:T(4,128)(2,1)} %reshape.238), calls=%async_computation.17 | async-start | bytes 1048576 | tf_op jit(solution)/shard_map/all_to_all | solution.py:169
  542.4 21.9 %all-to-all-start.8 = ((bf16[64,4,1024]{2,1,0:T(4,128)(2,1)}), bf16[64,4,1024]{2,1,0:T(4,128)(2,1)S(1)}, u32[]{:S(2)}, u32[]{:S(2)}) async-start(bf16[64,4,1024]{2,1,0:T(4,128)(2,1)} %reshape.230), calls=%async_computation.8 | async-start | bytes 1048576 | tf_op jit(solution)/shard_map/all_to_all | solution.py:169
  564.3 22.9 %all-to-all-start.14 = ((bf16[64,4,1024]{2,1,0:T(4,128)(2,1)}), bf16[64,4,1024]{2,1,0:T(4,128)(2,1)}, u32[]{:S(2)}, u32[]{:S(2)}) async-start(bf16[64,4,1024]{2,1,0:T(4,128)(2,1)} %reshape.235), calls=%async_computation.14 | async-start | bytes 1048576 | tf_op jit(solution)/shard_map/all_to_all | solution.py:169
  574.9 129.3 %collective-permute-start.3 = (bf16[2,1024]{1,0:T(2,128)(2,1)S(1)}, bf16[2,1024]{1,0:T(2,128)(2,1)S(1)}, u32[]{:S(2)}, u32[]{:S(2)}) collective-permute-start(bf16[2,1024]{1,0:T(2,128)(2,1)S(1)} %slice.153), channel_id=1, source_target_pairs={{8,0},{16,8},{24,16},{32,24},{40,32},{48,40},{56,48},{64,56},{72,6... | collective-permute-start | bytes 12296 | tf_op jit(solution)/shard_map/ppermute | solution.py:14
  589.6 5.7 collective-permute-start.5
  697.9 8.2 %collective-permute-start.4 = (bf16[2,1024]{1,0:T(2,128)(2,1)S(1)}, bf16[2,1024]{1,0:T(2,128)(2,1)S(1)}, u32[]{:S(2)}, u32[]{:S(2)}) collective-permute-start(bf16[2,1024]{1,0:T(2,128)(2,1)S(1)} %slice.156), channel_id=1, source_target_pairs={{8,0},{16,8},{24,16},{32,24},{40,32},{48,40},{56,48},{64,56},{72,6... | collective-permute-start | bytes 12296 | tf_op jit(solution)/shard_map/ppermute | solution.py:14
  (25 other events, 402.0 us)
where the time goes:
time: 719 us; the launch traced here: 708 us
  waiting for transfers between devices  360 us (50%)
  starting transfers between devices  124 us (17%)
  blocking collectives  100 us (14%)
  local copies, waits for them, and re-layouts  72 us (10%)
  matrix products  37.4 us (5%)
  other arithmetic  11.1 us (2%)
    psum x1, blocking collectives, on_device(): lax.psum(short_part.astype(jnp.bfloat16), 'ctx').astype(jnp.float32)  100 us
    all_to_all x3, waiting for transfers between devices, forward_transform(): lax.all_to_all(twist_im, 'ctx', split_axis=0, concat_axis=1, tiled=True)  79.2 us
    all_to_all x3, waiting for transfers between devices, inverse_transform(): lax.all_to_all(untw_re, 'ctx', split_axis=1, concat_axis=0, tiled=True)  77.5 us
    all_to_all x3, waiting for transfers between devices, inverse_transform(): lax.all_to_all(untw_im, 'ctx', split_axis=1, concat_axis=0, tiled=True)  75.8 us
    all_to_all x3, waiting for transfers between devices, forward_transform(): lax.all_to_all(twist_re, 'ctx', split_axis=0, concat_axis=1, tiled=True)  61 us
    all_to_all x3, waiting for transfers between devices, inverse_transform(): lax.all_to_all(signal, 'ctx', split_axis=0, concat_axis=1, tiled=True)  34.8 us
    all_to_all x3, waiting for transfers between devices, forward_transform(): lax.all_to_all(grid_rows, 'ctx', split_axis=1, concat_axis=0, tiled=True)  28 us
    all_to_all x3, starting transfers between devices, forward_transform(): lax.all_to_all(grid_rows, 'ctx', split_axis=1, concat_axis=0, tiled=True)  23.7 us
  transfers between devices with their start and end apart: 24, of which 21 were waited for; matrix products, arithmetic and copies ran while one was open for 11% of the time, Pallas kernels for 0%

commit v1 on v0

v1 whole, which is shorter than its diff:
```python
import functools
import math

import jax
import jax.numpy as jnp
from jax import lax
from jax.experimental import pallas as pl
from jax.experimental.pallas import tpu as pltpu
from jax.sharding import PartitionSpec as P

BF = jnp.bfloat16
F32 = jnp.float32
LANES = 128
VMEM_LIMIT = 48 * 1024 * 1024


def angles(left, right, period):
    product = left[:, None] * right[None, :] % (4 * period)
    return (2.0 * math.pi / (4 * period)) * product.astype(F32)


def filter_taps(scratch, at, weights, base):
    rows = scratch.shape[0] - 8
    total = weights[base : base + 1, :] * scratch[pl.ds(at, rows), :]
    for lag in range(1, 3):
        total = total + weights[base + lag : base + lag + 1, :] * scratch[pl.ds(at - lag, rows), :]
    return total


def stage(scratch, ref, halo, first):
    scratch[pl.ds(0, 8), :] = jnp.zeros((8, scratch.shape[1]), F32)
    scratch[pl.ds(6, 2), :] = halo[first : first + 2, :]
    scratch[pl.ds(8, ref.shape[0]), :] = ref[...].astype(F32)


def put_transposed(signal, out_ref, slot):
    for b in range(signal.shape[0] // LANES):
        turned = jnp.transpose(signal[b * LANES : (b + 1) * LANES, :]).astype(BF)
        out_ref[:, slot, b] = turned.reshape(out_ref.shape[0], out_ref.shape[3], LANES)


def pack_filter_kernel(h_ref, out_ref):
    put_transposed(h_ref[...].astype(F32), out_ref, 0)


def pack_signals_kernel(q_ref, k_ref, v_ref, cot_ref, halo_ref, w_ref, buf_ref, out_ref, qs, ks, vs):
    del buf_ref
    halo = halo_ref[...]
    w = w_ref[...]
    stage(qs, q_ref, halo, 0)
    stage(ks, k_ref, halo, 2)
    stage(vs, v_ref, halo, 4)
    q_short = filter_taps(qs, 8, w, 0)
    k_short = filter_taps(ks, 8, w, 3)
    v_short = filter_taps(vs, 8, w, 6)
    put_transposed(k_short * v_short, out_ref, 0)
    put_transposed(cot_ref[...].astype(F32) * q_short, out_ref, 1)


def spectral_kernel(
    inv_root, scale, group, in_ref, a_ref, b_ref, w_ref, wi_ref, c_ref, s_ref, out1, out2, xin, xout
):
    sources, arrays, halves, chans, _ = in_ref.shape
    rows = sources * halves
    for a in range(arrays):
        xin[a] = in_ref[:, a].reshape(rows * chans, LANES).astype(F32)
    cos_t = c_ref[...]
    sin_t = s_ref[...]
    n1 = cos_t.shape[0]

    def step(g, carry):
        spectra = []
        for a in range(arrays):
            cols = jnp.concatenate(
                [
                    xin[a, pl.ds(g * group + i, rows, stride=chans), :].astype(BF)
                    for i in range(group)
                ],
                axis=1,
            )
            first = jnp.dot(a_ref[...], cols, preferred_element_type=F32)
            parts = []
            for i in range(group):
                y_re = first[:n1, i * LANES : (i + 1) * LANES]
                y_im = first[n1:, i * LANES : (i + 1) * LANES]
                z_re = y_re * cos_t + y_im * sin_t
                z_im = y_im * cos_t - y_re * sin_t
                parts.append(jnp.concatenate([z_re.astype(BF), z_im.astype(BF)], axis=1))
            spectra.append(
                jnp.dot(jnp.concatenate(parts, axis=0), w_ref[...], preferred_element_type=F32)
            )
        (x_re, x_im), (g_re, g_im), (h_re, h_im) = [
            (f[:, :LANES], f[:, LANES:]) for f in spectra
        ]
        products = (
            (x_re * h_re - x_im * h_im, x_re * h_im + x_im * h_re),
            (g_re * h_re + g_im * h_im, g_im * h_re - g_re * h_im),
            ((g_re * x_re + g_im * x_im) * inv_root, (g_im * x_re - g_re * x_im) * inv_root),
        )
        for a, (p_re, p_im) in enumerate(products):
            spec = jnp.concatenate([p_re.astype(BF), p_im.astype(BF)], axis=1)
            back = jnp.dot(spec, wi_ref[...], preferred_element_type=F32)
            parts = []
            for i in range(group):
                u_re = back[i * n1 : (i + 1) * n1, :LANES]
                u_im = back[i * n1 : (i + 1) * n1, LANES:]
                v_re = u_re * cos_t - u_im * sin_t
                v_im = u_im * cos_t + u_re * sin_t
                parts.append(jnp.concatenate([v_re.astype(BF), v_im.astype(BF)], axis=0))
            signal = jnp.dot(
                b_ref[...], jnp.concatenate(parts, axis=1), preferred_element_type=F32
            )
            signal = signal * scale
            for i in range(group):
                xout[a, pl.ds(g * group + i, rows, stride=chans), :] = signal[
                    :, i * LANES : (i + 1) * LANES
                ]
        return carry

    lax.fori_loop(0, chans // group, step, 0)
    for a in range(2):
        out1[:, a] = xout[a].astype(BF).reshape(sources, halves, chans, LANES)
    out2[...] = xout[2].astype(BF).reshape(sources, halves, chans, LANES)


def get_transposed(in_ref, slot):
    blocks = []
    for b in range(in_ref.shape[2]):
        tile = in_ref[:, slot, b].reshape(LANES, LANES).astype(F32)
        blocks.append(jnp.transpose(tile))
    return jnp.concatenate(blocks, axis=0)


def finish_kernel(
    q_ref,
    k_ref,
    v_ref,
    cot_ref,
    halo_ref,
    w_ref,
    in_ref,
    out_ref,
    gq_ref,
    gk_ref,
    gv_ref,
    sums_ref,
    edge_ref,
    qs,
    ks,
    vs,
    gs,
):
    halo = halo_ref[...]
    w = w_ref[...]
    rows = q_ref.shape[0]
    stage(qs, q_ref, halo, 0)
    stage(ks, k_ref, halo, 2)
    stage(vs, v_ref, halo, 4)
    sums_ref[...] = jnp.zeros(sums_ref.shape, F32)
    edge_ref[...] = jnp.zeros(edge_ref.shape, F32)

    def finish(index, grad, staged, out):
        grad = grad.astype(BF).astype(F32)
        edge_ref[4 * index : 4 * index + 2, :] = grad[:2]
        edge_ref[4 * index + 2 : 4 * index + 4, :] = grad[rows - 2 :]
        gs[pl.ds(0, rows), :] = grad
        gs[pl.ds(rows, 8), :] = jnp.zeros((8, LANES), F32)
        back = w[3 * index : 3 * index + 1, :] * grad
        for lag in range(1, 3):
            back = back + w[3 * index + lag : 3 * index + lag + 1, :] * gs[pl.ds(lag, rows), :]
        out[...] = back.astype(BF)
        for lag in range(3):
            sums_ref[3 * index + lag : 3 * index + lag + 1, :] = jnp.sum(
                grad * staged[pl.ds(8 - lag, rows), :], axis=0, keepdims=True
            )

    conv = get_transposed(in_ref, 0)
    out_ref[...] = (filter_taps(qs, 8, w, 0) * conv).astype(BF)
    finish(0, cot_ref[...].astype(F32) * conv, qs, gq_ref)
    grad_mixed = get_transposed(in_ref, 1)
    finish(1, grad_mixed * filter_taps(vs, 8, w, 6), ks, gk_ref)
    finish(2, grad_mixed * filter_taps(ks, 8, w, 3), vs, gv_ref)


def unpack_kernel(in_ref, out_ref):
    for b in range(in_ref.shape[1]):
        tile = in_ref[:, b].reshape(LANES, LANES).astype(F32)
        out_ref[b * LANES : (b + 1) * LANES, :] = jnp.transpose(tile).astype(BF)


def params(**more):
    return pltpu.CompilerParams(vmem_limit_bytes=VMEM_LIMIT, **more)


def on_device(query_in, key_in, value_in, cotangent, short_weight, long_filter):
    rows, channels = query_in.shape
    taps = short_weight.shape[1]
    rim = taps - 1
    ctx = lax.axis_size("ctx")
    length = rows * ctx
    inv_root = 1.0 / math.sqrt(length)
    own = channels // ctx
    halves = rows // LANES
    outer = length // LANES
    tiles = channels // LANES
    per_tile = LANES // own
    w9 = short_weight.reshape(3 * taps, channels)

    r = jnp.arange(outer, dtype=jnp.int32)
    k1 = 4 * jnp.arange(outer, dtype=jnp.int32) + 1
    s = jnp.arange(LANES, dtype=jnp.int32)
    theta = angles(r, k1, outer).T
    a_mat = jnp.concatenate([jnp.cos(theta), -jnp.sin(theta)], axis=0).astype(BF)
    b_mat = a_mat.T
    phi = angles(s, k1, length).T
    cos_t, sin_t = jnp.cos(phi), jnp.sin(phi)
    psi = angles(s, 4 * s, LANES)
    c2, s2 = jnp.cos(psi), jnp.sin(psi)
    w_mat = jnp.concatenate(
        [jnp.concatenate([c2, -s2], axis=1), jnp.concatenate([s2, c2], axis=1)], axis=0
    ).astype(BF)
    wi_mat = w_mat.T

    up = [(i, i + 1) for i in range(ctx - 1)]
    down = [(i + 1, i) for i in range(ctx - 1)]
    tails = jnp.concatenate([x[rows - rim :] for x in (query_in, key_in, value_in)], axis=0)
    halo = lax.ppermute(tails, "ctx", up)
    halo = jnp.pad(halo.astype(F32), ((0, 8 - 3 * rim), (0, 0)))

    block = lambda: pl.BlockSpec((rows, LANES), lambda j: (0, j))
    row_block = lambda n: pl.BlockSpec((n, LANES), lambda j: (0, j))
    buf_shape = jax.ShapeDtypeStruct((ctx, 3, halves, own, LANES), BF)
    packed = pl.pallas_call(
        pack_filter_kernel,
        grid=(tiles,),
        in_specs=[block()],
        out_specs=pl.BlockSpec((per_tile, 1, halves, own, LANES), lambda j: (j, 2, 0, 0, 0)),
        out_shape=buf_shape,
        compiler_params=params(),
        name="pack_filter",
    )(long_filter)
    packed = pl.pallas_call(
        pack_signals_kernel,
        grid=(tiles,),
        in_specs=[block()] * 4
        + [row_block(8), row_block(9), pl.BlockSpec(memory_space=pl.ANY)],
        out_specs=pl.BlockSpec((per_tile, 2, halves, own, LANES), lambda j: (j, 0, 0, 0, 0)),
        out_shape=buf_shape,
        scratch_shapes=[pltpu.VMEM((rows + 8, LANES), F32)] * 3,
        input_output_aliases={6: 0},
        compiler_params=params(),
        name="pack_signals",
    )(query_in, key_in, value_in, cotangent, halo, w9, packed)
    arrived = lax.all_to_all(packed, "ctx", split_axis=0, concat_axis=0, tiled=True)

    cblock = 16
    whole = lambda x: pl.BlockSpec(x.shape, lambda i: (0,) * x.ndim)
    consts = (a_mat, b_mat, w_mat, wi_mat, cos_t, sin_t)
    out1, out2 = pl.pallas_call(
        functools.partial(spectral_kernel, inv_root, 1.0 / length, 4),
        grid=(own // cblock,),
        in_specs=[pl.BlockSpec((ctx, 3, halves, cblock, LANES), lambda i: (0, 0, 0, i, 0))]
        + [whole(x) for x in consts],
        out_specs=[
            pl.BlockSpec((ctx, 2, halves, cblock, LANES), lambda i: (0, 0, 0, i, 0)),
            pl.BlockSpec((ctx, halves, cblock, LANES), lambda i: (0, 0, i, 0)),
        ],
        out_shape=[
            jax.ShapeDtypeStruct((ctx, 2, halves, own, LANES), BF),
            jax.ShapeDtypeStruct((ctx, halves, own, LANES), BF),
        ],
        scratch_shapes=[pltpu.VMEM((3, outer * cblock, LANES), F32)] * 2,
        compiler_params=params(),
        name="spectral",
    )(arrived, *consts)
    back1 = lax.all_to_all(out1, "ctx", split_axis=0, concat_axis=0, tiled=True)
    back2 = lax.all_to_all(out2, "ctx", split_axis=0, concat_axis=0, tiled=True)

    wide = jax.ShapeDtypeStruct((rows, channels), BF)
    block_out, grad_q, grad_k, grad_v, sums, edge = pl.pallas_call(
        finish_kernel,
        grid=(tiles,),
        in_specs=[block()] * 4
        + [
            row_block(8),
            row_block(9),
            pl.BlockSpec((per_tile, 2, halves, own, LANES), lambda j: (j, 0, 0, 0, 0)),
        ],
        out_specs=[block()] * 4 + [row_block(16), row_block(16)],
        out_shape=[wide] * 4 + [jax.ShapeDtypeStruct((16, channels), F32)] * 2,
        scratch_shapes=[pltpu.VMEM((rows + 8, LANES), F32)] * 4,
        compiler_params=params(),
        name="finish",
    )(query_in, key_in, value_in, cotangent, halo, w9, back1)

    edge = edge[:12].reshape(3, 4, channels)
    ahead = lax.ppermute(edge[:, :2].astype(BF), "ctx", down).astype(F32)
    last = edge[:, 2:]
    w3 = short_weight
    row0 = w3[:, 0] * last[:, 0] + w3[:, 1] * last[:, 1] + w3[:, 2] * ahead[:, 0]
    row1 = w3[:, 0] * last[:, 1] + w3[:, 1] * ahead[:, 0] + w3[:, 2] * ahead[:, 1]
    fixed = jnp.stack([row0, row1], axis=1).astype(BF)
    grad_q = grad_q.at[rows - rim :].set(fixed[0])
    grad_k = grad_k.at[rows - rim :].set(fixed[1])
    grad_v = grad_v.at[rows - rim :].set(fixed[2])

    terms = sums[:9].reshape(9, ctx, own).transpose(1, 0, 2).reshape(ctx, 9 * own)
    terms = lax.all_to_all(terms, "ctx", split_axis=0, concat_axis=0, tiled=True)
    total = jnp.sum(terms, axis=0, keepdims=True)
    total = lax.all_to_all(
        jnp.broadcast_to(total, (ctx, 9 * own)), "ctx", split_axis=0, concat_axis=0, tiled=True
    )
    grad_short = total.reshape(ctx, 9, own).transpose(1, 0, 2).reshape(3, taps, channels) * inv_root

    grad_filter = pl.pallas_call(
        unpack_kernel,
        grid=(tiles,),
        in_specs=[pl.BlockSpec((per_tile, halves, own, LANES), lambda j: (j, 0, 0, 0))],
        out_specs=block(),
        out_shape=wide,
        compiler_params=params(),
        name="unpack_filter",
    )(back2)
    return (block_out, grad_q, grad_k, grad_v, grad_short, grad_filter)


def solution(mesh):
    wide = P("ctx", "tp")
    taps = P(None, None, "tp")
    return jax.shard_map(
        on_device,
        mesh=mesh,
        in_specs=(wide, wide, wide, wide, taps, wide),
        out_specs=(wide, wide, wide, wide, taps, wide),
        check_vma=False,
    )
```

time: 719 us -> 163 us (0.23); the launches traced: 708 us -> 162 us
  waiting for transfers between devices: 360 us -> 58.2 us
  starting transfers between devices: 124 us -> 29.4 us
  blocking collectives: 100 us -> 32.4 us
  local copies, waits for them, and re-layouts: 72 us -> 11 us
  matrix products: 37.4 us -> 0 us
  Pallas kernels: 0 us -> 25.7 us
    all_to_all x18 -> x4, waiting for transfers between devices: 356 us -> 58.2 us  [the longest x1 33.8 us: on_device(): lax.all_to_all(packed, 'ctx', split_axis=0, concat_axis=0, tiled=True)]
    psum x1 -> x0, blocking collectives: 100 us -> none  [on_device(): lax.psum(short_part.astype(jnp.bfloat16), 'ctx').astype(jnp.float32)]
    all_to_all x18 -> x4, starting transfers between devices: 103 us -> 22.5 us  [the longest x1 9.08 us: on_device(): lax.all_to_all(packed, 'ctx', split_axis=0, concat_axis=0, tiled=True)]
    dot_general x36 -> x0, matrix products: 37.4 us -> none  [the longest x3 9.45 us: forward_transform(): jnp.dot(cos_first, flattened, preferred_element_type=jnp.float32)]
    all_to_all x0 -> x1, blocking collectives: none -> 32.4 us  [on_device(): back1 = lax.all_to_all(out1, 'ctx', split_axis=0, concat_axis=0, tiled=True)]
    all_to_all x22 -> x2, local copies, waits for them, and re-layouts: 32.2 us -> 0.85 us  [the longest x1 0.73 us: on_device(): lax.all_to_all(terms, 'ctx', split_axis=0, concat_axis=0, tiled=True)]
    pallas_call x0 -> x5, Pallas kernels: none -> 25.7 us  [the longest x1 10.3 us: on_device(): pl.pallas_call(functools.partial(spectral_kernel, inv_root, 1.0 / length,...]
    convert_element_type x14 -> x0, local copies, waits for them, and re-layouts: 24.6 us -> none  [the longest x3 7.07 us: inverse_transform(): untw_im = (back_im * inv_cos + back_re * inv_sin).astype(jnp.bfloat16)]
  transfers between devices with their start and end apart: 24 -> 6, of which waited for: 21 -> 4; matrix products, arithmetic and copies ran while one was open for 11% -> 4% of each run, Pallas kernels for 0% -> 7%
where the time goes in v1:
time: 163 us; the launch traced here: 162 us
  waiting for transfers between devices  58.2 us (36%)
  blocking collectives  32.4 us (20%)
  starting transfers between devices  29.4 us (18%)
  Pallas kernels  25.7 us (16%)
  local copies, waits for them, and re-layouts  11 us (7%)
  other arithmetic  4.41 us (3%)
    all_to_all x1, waiting for transfers between devices, on_device(): lax.all_to_all(packed, 'ctx', split_axis=0, concat_axis=0, tiled=True)  33.8 us
    all_to_all x1, blocking collectives, on_device(): back1 = lax.all_to_all(out1, 'ctx', split_axis=0, concat_axis=0, tiled=True)  32.4 us
    pallas_call x1, Pallas kernels, on_device(): pl.pallas_call(functools.partial(spectral_kernel, inv_root, 1.0 / length,...  10.3 us
    all_to_all x1, starting transfers between devices, on_device(): lax.all_to_all(packed, 'ctx', split_axis=0, concat_axis=0, tiled=True)  9.08 us
    all_to_all x1, waiting for transfers between devices, on_device(): back2 = lax.all_to_all(out2, 'ctx', split_axis=0, concat_axis=0, tiled=True)  8.54 us
    all_to_all x1, waiting for transfers between devices, on_device(): lax.all_to_all(terms, 'ctx', split_axis=0, concat_axis=0, tiled=True)  8.16 us
    all_to_all x1, waiting for transfers between devices, on_device(): lax.all_to_all(jnp.broadcast_to(total, (ctx, 9 * own)), 'ctx', split_axis...  7.64 us
    pallas_call x1, Pallas kernels, on_device(): pl.pallas_call(finish_kernel, grid=(tiles,), in_specs=[block()] * 4 + [ro...  5.19 us
  transfers between devices with their start and end apart: 6, of which 4 were waited for; matrix products, arithmetic and copies ran while one was open for 4% of the time, Pallas kernels for 7%

profile of v1, /device:TPU:1, one launch (start us, length us, event | category | flops | bytes accessed | tf_op | source)
XLA Modules:
  0.0 162.1 jit_solution(6899542715647703905)
XLA Ops:
  0.7 0.9 slice.108
  3.0 4.6 %collective-permute-start = (bf16[6,1024]{1,0:T(8,128)(2,1)S(1)}, bf16[6,1024]{1,0:T(8,128)(2,1)S(1)}, u32[]{:S(2)}, u32[]{:S(2)}) collective-permute-start(bf16[6,1024]{1,0:T(8,128)(2,1)S(1)} %pad_maximum_fusion), channel_id=1, source_target_pairs={{0,8},{8,16},{16,24},{24,32},{32,40},{40,48},{48,56},{56,64},{64,7... | collective-permute-start | bytes 36872 | tf_op jit(solution)/shard_map/ppermute | solution.py:227
  7.6 0.8 reshape.125.w_ref
  8.5 1.0 copy-done.6
  9.5 3.1 %pack_filter.1.buf_ref = bf16[32,3,2,32,128]{4,3,2,1,0:T(8,128)(2,1)} custom-call(bf16[256,1024]{1,0:T(8,128)(2,1)S(1)} %copy-done.6), custom_call_target="tpu_custom_call" | custom-call | tf_op jit(solution)/shard_map/pack_filter/pallas_call | solution.py:233
  12.7 4.1 %pack_signals.1 = bf16[32,3,2,32,128]{4,3,2,1,0:T(8,128)(2,1)} custom-call(bf16[256,1024]{1,0:T(8,128)(2,1)S(1)} %copy-done, bf16[256,1024]{1,0:T(8,128)(2,1)S(1)} %copy-done.1, bf16[256,1024]{1,0:T(8,128)(2,1)S(1)} %copy-done.2, bf16[256,1024]{1,0:T(8,128)(2,1)S(1)} %copy-done.3, ...), custom_call_target="tpu_custom_call", output_to_operand_aliasing={{}: (6, {})} | custom-call | tf_op jit(solution)/shard_map/pack_signals/pallas_call | solution.py:242
  16.8 9.1 %all-to-all-start = ((bf16[32,3,2,32,128]{4,3,2,1,0:T(8,128)(2,1)}), bf16[32,3,2,32,128]{4,3,2,1,0:T(8,128)(2,1)S(1)}, u32[]{:S(2)}, u32[]{:S(2)}) async-start(bf16[32,3,2,32,128]{4,3,2,1,0:T(8,128)(2,1)} %pack_signals.1), calls=%async_computation | async-start | bytes 3145728 | tf_op jit(solution)/shard_map/all_to_all | solution.py:254
  27.9 1.0 copy.23.w_ref
  28.9 0.8 fusion.32.b_ref
  29.7 1.5 fusion.20
  31.2 33.8 %all-to-all-done.in_ref = bf16[32,3,2,32,128]{4,3,2,1,0:T(8,128)(2,1)S(1)} async-done(((bf16[32,3,2,32,128]{4,3,2,1,0:T(8,128)(2,1)}), bf16[32,3,2,32,128]{4,3,2,1,0:T(8,128)(2,1)S(1)}, u32[]{:S(2)}, u32[]{:S(2)}) %all-to-all-start) | async-done | bytes 1572896 | tf_op jit(solution)/shard_map/all_to_all | solution.py:254
  65.0 0.8 copy-done.7
  66.6 10.3 %spectral.1 = (bf16[32,2,2,32,128]{4,3,2,1,0:T(8,128)(2,1)S(1)}, bf16[32,2,32,128]{3,2,1,0:T(8,128)(2,1)S(1)}) custom-call(bf16[32,3,2,32,128]{4,3,2,1,0:T(8,128)(2,1)S(1)} %all-to-all-done.in_ref, bf16[128,64]{1,0:T(8,128)(2,1)S(1)} %copy.22.a_ref, bf16[64,128]{1,0:T(8,128)(2,1)S(1)} %fusion.32.b_ref, bf16[256,256]{1,0:T(8,128)(2,1)S(1)} %copy.23.w_ref, ...), custom_call_target="tpu_custom_call" | custom-call | tf_op jit(solution)/shard_map/spectral/pallas_call | solution.py:259
  76.9 32.4 %all_to_all.30.in_ref = bf16[32,2,2,32,128]{4,3,2,1,0:T(8,128)(2,1)S(1)} all-to-all(bf16[32,2,2,32,128]{4,3,2,1,0:T(8,128)(2,1)S(1)} %get-tuple-element.50), channel_id=1, replica_groups=mesh['ctx'=32,'tp'=8] {'ctx'}, dimensions={0} | all-to-all | bytes 2097152 | tf_op jit(solution)/shard_map/all_to_all | solution.py:276
  109.3 4.8 %all-to-all-start.4 = ((bf16[32,2,32,128]{3,2,1,0:T(8,128)(2,1)}), bf16[32,2,32,128]{3,2,1,0:T(8,128)(2,1)S(1)}, u32[]{:S(2)}, u32[]{:S(2)}) async-start(bf16[32,2,32,128]{3,2,1,0:T(8,128)(2,1)} %copy-done.5), calls=%async_computation.4 | async-start | bytes 1048576 | tf_op jit(solution)/shard_map/all_to_all | solution.py:277
  114.0 1.0 copy-done.4
  115.1 5.2 %finish.1 = (bf16[256,1024]{1,0:T(8,128)(2,1)}, bf16[256,1024]{1,0:T(8,128)(2,1)}, bf16[256,1024]{1,0:T(8,128)(2,1)}, bf16[256,1024]{1,0:T(8,128)(2,1)}, f32[16,1024]{1,0:T(8,128)S(1)}, /*index=5*/f32[16,1024]{1,0:T(8,128)S(1)}) custom-call(bf16[256,1024]{1,0:T(8,128)(2,1)S(1)} %copy-done, bf16[256,1024]{1,0:T(8,128)(2,1)S(1)} %copy-done.1, ...), custom_call_target="tpu_custom_call" | custom-call | tf_op jit(solution)/shard_map/finish/pallas_call | solution.py:280
  120.3 2.3 %collective-permute-start.1 = (bf16[3,2,1024]{2,1,0:T(2,128)(2,1)S(1)}, bf16[3,2,1024]{2,1,0:T(2,128)(2,1)S(1)}, u32[]{:S(2)}, u32[]{:S(2)}) collective-permute-start(bf16[3,2,1024]{2,1,0:T(2,128)(2,1)S(1)} %slice.176), channel_id=1, source_target_pairs={{8,0},{16,8},{24,16},{32,24},{40,32},{48,40},{56,48},{64,56},{72,6... | collective-permute-start | bytes 36872 | tf_op jit(solution)/shard_map/ppermute | solution.py:297
  122.6 8.5 %all-to-all-done.4.in_ref = bf16[32,2,32,128]{3,2,1,0:T(8,128)(2,1)S(1)} async-done(((bf16[32,2,32,128]{3,2,1,0:T(8,128)(2,1)}), bf16[32,2,32,128]{3,2,1,0:T(8,128)(2,1)S(1)}, u32[]{:S(2)}, u32[]{:S(2)}) %all-to-all-start.4) | async-done | bytes 524320 | tf_op jit(solution)/shard_map/all_to_all | solution.py:277
  131.1 3.0 %unpack_filter.1 = bf16[256,1024]{1,0:T(8,128)(2,1)} custom-call(bf16[32,2,32,128]{3,2,1,0:T(8,128)(2,1)S(1)} %all-to-all-done.4.in_ref), custom_call_target="tpu_custom_call" | custom-call | tf_op jit(solution)/shard_map/unpack_filter/pallas_call | solution.py:315
  135.1 4.8 %all-to-all-start.2 = ((f32[32,1,288]{2,1,0:T(1,128)}), f32[32,1,288]{2,1,0:T(1,128)S(1)}, u32[]{:S(2)}, u32[]{:S(2)}) async-start(f32[32,1,288]{2,1,0:T(1,128)} %copy.25), calls=%async_computation.2 | async-start | bytes 98304 | tf_op jit(solution)/shard_map/all_to_all | solution.py:308
  140.0 8.2 %all-to-all-done.2 = f32[32,1,288]{2,1,0:T(1,128)S(1)} async-done(((f32[32,1,288]{2,1,0:T(1,128)}), f32[32,1,288]{2,1,0:T(1,128)S(1)}, u32[]{:S(2)}, u32[]{:S(2)}) %all-to-all-start.2) | async-done | bytes 36896 | tf_op jit(solution)/shard_map/all_to_all | solution.py:308
  148.9 3.9 %all-to-all-start.3 = ((f32[32,1,288]{2,1,0:T(1,128)}), f32[32,1,288]{2,1,0:T(1,128)S(1)}, u32[]{:S(2)}, u32[]{:S(2)}) async-start(f32[32,1,288]{2,1,0:T(1,128)} %broadcast_in_dim.2), calls=%async_computation.3 | async-start | bytes 98304 | tf_op jit(solution)/shard_map/all_to_all | solution.py:310
  153.4 7.6 %all-to-all-done.3 = f32[32,1,288]{2,1,0:T(1,128)S(1)} async-done(((f32[32,1,288]{2,1,0:T(1,128)}), f32[32,1,288]{2,1,0:T(1,128)S(1)}, u32[]{:S(2)}, u32[]{:S(2)}) %all-to-all-start.3) | async-done | bytes 36896 | tf_op jit(solution)/shard_map/all_to_all | solution.py:310
  (50 shorter events, 7.6 us)
Async XLA Ops:
  0.6 12.0 %copy-start = (bf16[256,1024]{1,0:T(8,128)(2,1)S(1)}, bf16[256,1024]{1,0:T(8,128)(2,1)}, u32[]{:S(2)}) copy-start(bf16[256,1024]{1,0:T(8,128)(2,1)} %q_ref.3) | copy-start | bytes 1572868
  0.6 12.0 %copy-start.1 = (bf16[256,1024]{1,0:T(8,128)(2,1)S(1)}, bf16[256,1024]{1,0:T(8,128)(2,1)}, u32[]{:S(2)}) copy-start(bf16[256,1024]{1,0:T(8,128)(2,1)} %k_ref.3) | copy-start | bytes 1572868
  0.7 12.0 %copy-start.2 = (bf16[256,1024]{1,0:T(8,128)(2,1)S(1)}, bf16[256,1024]{1,0:T(8,128)(2,1)}, u32[]{:S(2)}) copy-start(bf16[256,1024]{1,0:T(8,128)(2,1)} %v_ref.3) | copy-start | bytes 1572868
  0.7 12.0 %copy-start.3 = (bf16[256,1024]{1,0:T(8,128)(2,1)S(1)}, bf16[256,1024]{1,0:T(8,128)(2,1)}, u32[]{:S(2)}) copy-start(bf16[256,1024]{1,0:T(8,128)(2,1)} %cot_ref.3) | copy-start | bytes 1572868
  3.0 9.6 %collective-permute-start = (bf16[6,1024]{1,0:T(8,128)(2,1)S(1)}, bf16[6,1024]{1,0:T(8,128)(2,1)S(1)}, u32[]{:S(2)}, u32[]{:S(2)}) collective-permute-start(bf16[6,1024]{1,0:T(8,128)(2,1)S(1)} %pad_maximum_fusion), channel_id=1, source_target_pairs={{0,8},{8,16},{16,24},{24,32},{32,40},{40,48},{48,56},{56,64},{64,7... | collective-permute-start | bytes 36872 | tf_op jit(solution)/shard_map/ppermute | solution.py:227
  8.4 1.0 copy-start.6
  16.8 48.3 %all-to-all-start = ((bf16[32,3,2,32,128]{4,3,2,1,0:T(8,128)(2,1)}), bf16[32,3,2,32,128]{4,3,2,1,0:T(8,128)(2,1)S(1)}, u32[]{:S(2)}, u32[]{:S(2)}) async-start(bf16[32,3,2,32,128]{4,3,2,1,0:T(8,128)(2,1)} %pack_signals.1), calls=%async_computation | async-start | bytes 3145728 | tf_op jit(solution)/shard_map/all_to_all | solution.py:254
  25.9 0.5 copy-start.12
  26.0 0.6 copy-start.10
  26.0 0.6 copy-start.11
  65.0 0.8 copy-start.7
  65.8 0.8 copy-start.8
  76.8 32.4 %copy-start.5 = (bf16[32,2,32,128]{3,2,1,0:T(8,128)(2,1)}, bf16[32,2,32,128]{3,2,1,0:T(8,128)(2,1)S(1)}, u32[]{:S(2)}) copy-start(bf16[32,2,32,128]{3,2,1,0:T(8,128)(2,1)S(1)} %get-tuple-element.57) | copy-start | bytes 1572868
  109.3 21.8 %all-to-all-start.4 = ((bf16[32,2,32,128]{3,2,1,0:T(8,128)(2,1)}), bf16[32,2,32,128]{3,2,1,0:T(8,128)(2,1)S(1)}, u32[]{:S(2)}, u32[]{:S(2)}) async-start(bf16[32,2,32,128]{3,2,1,0:T(8,128)(2,1)} %copy-done.5), calls=%async_computation.4 | async-start | bytes 1048576 | tf_op jit(solution)/shard_map/all_to_all | solution.py:277
  114.0 1.0 copy-start.4
  120.3 19.7 %copy-start.9 = (f32[3,3,1024]{2,1,0:T(4,128)S(1)}, f32[3,3,1024]{2,1,0:T(4,128)}, u32[]{:S(2)}) copy-start(f32[3,3,1024]{2,1,0:T(4,128)} %param.16) | copy-start | bytes 110596
  120.3 19.6 %collective-permute-start.1 = (bf16[3,2,1024]{2,1,0:T(2,128)(2,1)S(1)}, bf16[3,2,1024]{2,1,0:T(2,128)(2,1)S(1)}, u32[]{:S(2)}, u32[]{:S(2)}) collective-permute-start(bf16[3,2,1024]{2,1,0:T(2,128)(2,1)S(1)} %slice.176), channel_id=1, source_target_pairs={{8,0},{16,8},{24,16},{32,24},{40,32},{48,40},{56,48},{64,56},{72,6... | collective-permute-start | bytes 36872 | tf_op jit(solution)/shard_map/ppermute | solution.py:297
  135.1 13.1 %all-to-all-start.2 = ((f32[32,1,288]{2,1,0:T(1,128)}), f32[32,1,288]{2,1,0:T(1,128)S(1)}, u32[]{:S(2)}, u32[]{:S(2)}) async-start(f32[32,1,288]{2,1,0:T(1,128)} %copy.25), calls=%async_computation.2 | async-start | bytes 98304 | tf_op jit(solution)/shard_map/all_to_all | solution.py:308
  148.9 12.2 %all-to-all-start.3 = ((f32[32,1,288]{2,1,0:T(1,128)}), f32[32,1,288]{2,1,0:T(1,128)S(1)}, u32[]{:S(2)}, u32[]{:S(2)}) async-start(f32[32,1,288]{2,1,0:T(1,128)} %broadcast_in_dim.2), calls=%async_computation.3 | async-start | bytes 98304 | tf_op jit(solution)/shard_map/all_to_all | solution.py:310

commit v2 on v1

v2 whole, which is shorter than its diff:
```python
import functools
import math

import jax
import jax.numpy as jnp
from jax import lax
from jax.experimental import pallas as pl
from jax.experimental.pallas import tpu as pltpu
from jax.sharding import PartitionSpec as P
import numpy as np

BF = jnp.bfloat16
F32 = jnp.float32
LANES = 128
VMEM_LIMIT = 48 * 1024 * 1024
OUTS = (2, 1)


def tables(outer, length):
    r = np.arange(outer)
    k1 = 4 * np.arange(outer) + 1
    s = np.arange(LANES)
    theta = (k1[:, None] * r[None, :] % (4 * outer)) * (2.0 * math.pi / (4 * outer))
    phi = (k1[:, None] * s[None, :] % (4 * length)) * (2.0 * math.pi / (4 * length))
    psi = (s[:, None] * s[None, :] % LANES) * (2.0 * math.pi / LANES)
    first = np.concatenate([np.cos(theta), -np.sin(theta)], axis=0)
    c2, s2 = np.cos(psi), np.sin(psi)
    second = np.block([[c2, -s2], [s2, c2]])
    last = first.T / length
    as_bf = lambda x: jnp.asarray(x.astype(np.float32), BF)
    turn = np.stack([np.cos(phi), np.sin(phi)]).astype(np.float32)
    return as_bf(first), as_bf(last), as_bf(second), as_bf(second.T), jnp.asarray(turn)


def lane_tiles(ref):
    return [slice(t * LANES, (t + 1) * LANES) for t in range(ref.shape[-1] // LANES)]


def filter_taps(scratch, at, rows, weights, stream):
    total = weights[stream, 0:1, :] * scratch[pl.ds(at, rows), :]
    for lag in range(1, 3):
        total = total + weights[stream, lag : lag + 1, :] * scratch[pl.ds(at - lag, rows), :]
    return total


def stage(scratch, signal, halo):
    scratch[pl.ds(6, 2), :] = halo
    scratch[pl.ds(8, signal.shape[0]), :] = signal.astype(F32)


def put_transposed(signal, out_ref, tile, slot):
    own = out_ref.shape[3]
    per = LANES // own
    for b in range(signal.shape[0] // LANES):
        turned = jnp.transpose(signal[b * LANES : (b + 1) * LANES, :]).astype(BF)
        out_ref[tile * per : (tile + 1) * per, slot, b] = turned.reshape(per, own, LANES)


def get_transposed(in_ref, tile, slot):
    per = LANES // in_ref.shape[3]
    blocks = []
    for b in range(in_ref.shape[2]):
        part = in_ref[tile * per : (tile + 1) * per, slot, b].reshape(LANES, LANES)
        blocks.append(jnp.transpose(part.astype(F32)))
    return jnp.concatenate(blocks, axis=0)


def tails_kernel(q_ref, k_ref, v_ref, out_ref):
    rows = [ref[...].astype(F32)[14:, :] for ref in (q_ref, k_ref, v_ref)]
    fill = jnp.zeros((10, out_ref.shape[1]), F32)
    out_ref[...] = jnp.concatenate(rows + [fill], axis=0).astype(BF)


def pack_filter_kernel(h_ref, out_ref):
    for t, at in enumerate(lane_tiles(h_ref)):
        put_transposed(h_ref[:, at].astype(F32), out_ref, t, 0)


def pack_signals_kernel(q_ref, k_ref, v_ref, cot_ref, halo_ref, w_ref, buf_ref, out_ref, qs, ks, vs):
    del buf_ref
    rows = q_ref.shape[0]
    for t, at in enumerate(lane_tiles(q_ref)):
        halo = halo_ref[:, at].astype(F32)
        w = w_ref[:, :, at]
        stage(qs, q_ref[:, at], halo[0:2])
        stage(ks, k_ref[:, at], halo[2:4])
        stage(vs, v_ref[:, at], halo[4:6])
        mixed = filter_taps(ks, 8, rows, w, 1) * filter_taps(vs, 8, rows, w, 2)
        put_transposed(mixed, out_ref, t, 0)
        grad_conv = cot_ref[:, at].astype(F32) * filter_taps(qs, 8, rows, w, 0)
        put_transposed(grad_conv, out_ref, t, 1)


def spectral_kernel(inv_root, in_ref, a_ref, b_ref, w_ref, wi_ref, turn_ref, *rest):
    outs, (xin, xout) = rest[:-2], rest[-2:]
    sources, arrays, halves, chans, _ = in_ref.shape
    rows = sources * halves
    for a in range(arrays):
        xin[a] = in_ref[:, a].reshape(rows * chans, LANES).astype(F32)
    cos_t = turn_ref[0]
    sin_t = turn_ref[1]
    n1 = cos_t.shape[0]
    tiles = [slice(i * LANES, (i + 1) * LANES) for i in range(chans)]

    spectra = []
    for a in range(arrays):
        cols = jnp.concatenate(
            [xin[a, pl.ds(i, rows, stride=chans), :].astype(BF) for i in range(chans)], axis=1
        )
        first = jnp.dot(a_ref[...], cols, preferred_element_type=F32)
        parts = []
        for at in tiles:
            y_re = first[:n1, at]
            y_im = first[n1:, at]
            z_re = y_re * cos_t + y_im * sin_t
            z_im = y_im * cos_t - y_re * sin_t
            parts.append(jnp.concatenate([z_re.astype(BF), z_im.astype(BF)], axis=1))
        spectra.append(
            jnp.dot(jnp.concatenate(parts, axis=0), w_ref[...], preferred_element_type=F32)
        )
    (x_re, x_im), (g_re, g_im), (h_re, h_im) = [(f[:, :LANES], f[:, LANES:]) for f in spectra]
    products = (
        (x_re * h_re - x_im * h_im, x_re * h_im + x_im * h_re),
        (g_re * h_re + g_im * h_im, g_im * h_re - g_re * h_im),
        ((g_re * x_re + g_im * x_im) * inv_root, (g_im * x_re - g_re * x_im) * inv_root),
    )
    for a, (p_re, p_im) in enumerate(products):
        spec = jnp.concatenate([p_re.astype(BF), p_im.astype(BF)], axis=1)
        back = jnp.dot(spec, wi_ref[...], preferred_element_type=F32)
        parts = []
        for i in range(chans):
            u_re = back[i * n1 : (i + 1) * n1, :LANES]
            u_im = back[i * n1 : (i + 1) * n1, LANES:]
            v_re = u_re * cos_t - u_im * sin_t
            v_im = u_im * cos_t + u_re * sin_t
            parts.append(jnp.concatenate([v_re.astype(BF), v_im.astype(BF)], axis=0))
        signal = jnp.dot(b_ref[...], jnp.concatenate(parts, axis=1), preferred_element_type=F32)
        for i, at in enumerate(tiles):
            xout[a, pl.ds(i, rows, stride=chans), :] = signal[:, at]
    slots = [(out, j) for out in outs for j in range(out.shape[1])]
    for a, (out, j) in enumerate(slots):
        out[:, j] = xout[a].astype(BF).reshape(sources, halves, chans, LANES)


def finish_kernel(
    q_ref,
    k_ref,
    v_ref,
    cot_ref,
    halo_ref,
    w_ref,
    in_ref,
    out_ref,
    gq_ref,
    gk_ref,
    gv_ref,
    sums_ref,
    last_ref,
    qs,
    ks,
    vs,
    gs,
):
    rows = q_ref.shape[0]
    gs[pl.ds(rows, 8), :] = jnp.zeros((8, LANES), F32)
    for t, at in enumerate(lane_tiles(q_ref)):
        halo = halo_ref[:, at].astype(F32)
        w = w_ref[:, :, at]
        stage(qs, q_ref[:, at], halo[0:2])
        stage(ks, k_ref[:, at], halo[2:4])
        stage(vs, v_ref[:, at], halo[4:6])
        sums = []
        firsts = []
        lasts = []

        def finish(index, grad, staged, out):
            grad = grad.astype(BF).astype(F32)
            firsts.append(grad[:2])
            gs[pl.ds(0, rows), :] = grad
            back = w[index, 0:1, :] * grad
            for lag in range(1, 3):
                back = back + w[index, lag : lag + 1, :] * gs[pl.ds(lag, rows), :]
            out[:, at] = back.astype(BF)
            lasts.append(back[rows - 2 :])
            for lag in range(3):
                sums.append(
                    jnp.sum(grad * staged[pl.ds(8 - lag, rows), :], axis=0, keepdims=True)
                )

        conv = get_transposed(in_ref, t, 0)
        out_ref[:, at] = (filter_taps(qs, 8, rows, w, 0) * conv).astype(BF)
        finish(0, cot_ref[:, at].astype(F32) * conv, qs, gq_ref)
        grad_mixed = get_transposed(in_ref, t, 1)
        finish(1, grad_mixed * filter_taps(vs, 8, rows, w, 2), ks, gk_ref)
        finish(2, grad_mixed * filter_taps(ks, 8, rows, w, 1), vs, gv_ref)
        fill = [jnp.zeros((1, LANES), F32)]
        sums_ref[:, at] = jnp.concatenate(sums + fill + firsts, axis=0).astype(BF)
        last_ref[:, at] = jnp.concatenate(lasts + 2 * fill, axis=0)


def rim_kernel(ahead_ref, last_ref, w_ref, gq_in, gk_in, gv_in, gq_out, gk_out, gv_out):
    row = lax.broadcasted_iota(jnp.int32, (16, ahead_ref.shape[1]), 0)
    ahead = ahead_ref[...].astype(F32)
    streams = ((gq_in, gq_out), (gk_in, gk_out), (gv_in, gv_out))
    for i, (before, after) in enumerate(streams):
        w1 = w_ref[i, 1:2, :]
        w2 = w_ref[i, 2:3, :]
        next0 = ahead[10 + 2 * i : 11 + 2 * i]
        next1 = ahead[11 + 2 * i : 12 + 2 * i]
        end0 = last_ref[2 * i : 2 * i + 1] + w2 * next0
        end1 = last_ref[2 * i + 1 : 2 * i + 2] + w1 * next0 + w2 * next1
        fixed = jnp.where(row == 14, end0, jnp.where(row == 15, end1, before[...].astype(F32)))
        after[...] = fixed.astype(BF)


def unpack_kernel(slot, in_ref, out_ref):
    for t, at in enumerate(lane_tiles(out_ref)):
        out_ref[:, at] = get_transposed(in_ref, t, slot).astype(BF)


def sum_over_ctx(terms):
    ctx = lax.axis_size("ctx")

    def moved(x, to):
        return lax.ppermute(x.astype(BF), "ctx", [(i, to(i)) for i in range(ctx)]).astype(F32)

    total = terms.astype(F32)
    near = [moved(total, lambda i, d=d: i ^ d) for d in (1, 2, 3)]
    total = lax.reduce_precision((total + near[0]) + (near[1] + near[2]), 8, 7)
    far = [moved(total, lambda i, d=d: (i + d) % ctx) for d in (ctx // 4, ctx // 2, 3 * ctx // 4)]
    total = lax.reduce_precision((total + far[1]) + (far[0] + far[2]), 8, 7)
    for d in (ctx // 8,):
        total = total + moved(total, lambda i: i ^ d)
    return total


def params(**more):
    return pltpu.CompilerParams(vmem_limit_bytes=VMEM_LIMIT, **more)


def on_device(query_in, key_in, value_in, cotangent, short_weight, long_filter):
    rows, channels = query_in.shape
    taps = short_weight.shape[1]
    ctx = lax.axis_size("ctx")
    length = rows * ctx
    inv_root = 1.0 / math.sqrt(length)
    own = channels // ctx
    halves = rows // LANES
    outer = length // LANES
    wide_step = 512
    steps = channels // wide_step
    per_step = wide_step // own
    consts = tables(outer, length)

    up = [(i, i + 1) for i in range(ctx - 1)]
    down = [(i + 1, i) for i in range(ctx - 1)]
    block = lambda: pl.BlockSpec((rows, wide_step), lambda j: (0, j))
    row_block = lambda n: pl.BlockSpec((n, wide_step), lambda j: (0, j))
    w_block = lambda: pl.BlockSpec((3, taps, wide_step), lambda j: (0, 0, j))
    end_block = lambda: pl.BlockSpec((16, channels), lambda j: (rows // 16 - 1, 0))
    small = lambda n: pl.BlockSpec((n, channels), lambda j: (0, 0))

    tails = pl.pallas_call(
        tails_kernel,
        grid=(1,),
        in_specs=[end_block()] * 3,
        out_specs=small(16),
        out_shape=jax.ShapeDtypeStruct((16, channels), BF),
        name="tails",
    )(query_in, key_in, value_in)
    halo = lax.ppermute(tails, "ctx", up)

    buf_shape = jax.ShapeDtypeStruct((ctx, 3, halves, own, LANES), BF)
    packed = pl.pallas_call(
        pack_filter_kernel,
        grid=(steps,),
        in_specs=[block()],
        out_specs=pl.BlockSpec((per_step, 1, halves, own, LANES), lambda j: (j, 2, 0, 0, 0)),
        out_shape=buf_shape,
        compiler_params=params(),
        name="pack_filter",
    )(long_filter)
    packed = pl.pallas_call(
        pack_signals_kernel,
        grid=(steps,),
        in_specs=[block()] * 4 + [row_block(16), w_block(), pl.BlockSpec(memory_space=pl.ANY)],
        out_specs=pl.BlockSpec((per_step, 2, halves, own, LANES), lambda j: (j, 0, 0, 0, 0)),
        out_shape=buf_shape,
        scratch_shapes=[pltpu.VMEM((rows + 8, LANES), F32)] * 3,
        input_output_aliases={6: 0},
        compiler_params=params(),
        name="pack_signals",
    )(query_in, key_in, value_in, cotangent, halo, short_weight, packed)
    arrived = lax.all_to_all(packed, "ctx", split_axis=0, concat_axis=0, tiled=True)

    cblock = 16
    whole = lambda x: pl.BlockSpec(x.shape, lambda i: (0,) * x.ndim)
    outs = OUTS
    back = pl.pallas_call(
        functools.partial(spectral_kernel, inv_root),
        grid=(own // cblock,),
        in_specs=[pl.BlockSpec((ctx, 3, halves, cblock, LANES), lambda i: (0, 0, 0, i, 0))]
        + [whole(x) for x in consts],
        out_specs=[
            pl.BlockSpec((ctx, n, halves, cblock, LANES), lambda i: (0, 0, 0, i, 0)) for n in outs
        ],
        out_shape=[jax.ShapeDtypeStruct((ctx, n, halves, own, LANES), BF) for n in outs],
        scratch_shapes=[pltpu.VMEM((3, outer * cblock, LANES), F32)] * 2,
        compiler_params=params(),
        name="spectral",
    )(arrived, *consts)
    back = [lax.all_to_all(x, "ctx", split_axis=0, concat_axis=0, tiled=True) for x in back]

    wide = jax.ShapeDtypeStruct((rows, channels), BF)
    message = lambda n, at: pl.BlockSpec(
        (per_step, n, halves, own, LANES), lambda j: (j, at, 0, 0, 0)
    )
    block_out, grad_q, grad_k, grad_v, sums, last = pl.pallas_call(
        finish_kernel,
        grid=(steps,),
        in_specs=[block()] * 4 + [row_block(16), w_block(), message(2, 0)],
        out_specs=[block()] * 4 + [row_block(16), row_block(8)],
        out_shape=[wide] * 4
        + [
            jax.ShapeDtypeStruct((16, channels), BF),
            jax.ShapeDtypeStruct((8, channels), F32),
        ],
        scratch_shapes=[pltpu.VMEM((rows + 8, LANES), F32)] * 4,
        compiler_params=params(),
        name="finish",
    )(query_in, key_in, value_in, cotangent, halo, short_weight, back[0])

    ahead = lax.ppermute(sums, "ctx", down)
    grad_q, grad_k, grad_v = pl.pallas_call(
        rim_kernel,
        grid=(1,),
        in_specs=[small(16), small(8), pl.BlockSpec((3, taps, channels), lambda j: (0, 0, 0))]
        + [end_block()] * 3,
        out_specs=[end_block()] * 3,
        out_shape=[wide] * 3,
        input_output_aliases={3: 0, 4: 1, 5: 2},
        compiler_params=params(),
        name="rims",
    )(ahead, last, short_weight, grad_q, grad_k, grad_v)

    total = sum_over_ctx(sums)
    grad_short = total[: 3 * taps].reshape(3, taps, channels) * inv_root

    slot = 2 if len(outs) == 1 else 0
    grad_filter = pl.pallas_call(
        functools.partial(unpack_kernel, 0),
        grid=(steps,),
        in_specs=[message(1, slot)],
        out_specs=block(),
        out_shape=wide,
        compiler_params=params(),
        name="unpack_filter",
    )(back[-1])
    return (block_out, grad_q, grad_k, grad_v, grad_short, grad_filter)


def solution(mesh):
    wide = P("ctx", "tp")
    taps = P(None, None, "tp")
    return jax.shard_map(
        on_device,
        mesh=mesh,
        in_specs=(wide, wide, wide, wide, taps, wide),
        out_specs=(wide, wide, wide, wide, taps, wide),
        check_vma=False,
    )
```

time: 163 us -> 131 us (0.80)
  waiting for transfers between devices: 58.2 us -> 3.72 us
  blocking collectives: 32.4 us -> 82.8 us
  Pallas kernels: 25.7 us -> 16.3 us
  local copies, waits for them, and re-layouts: 11 us -> 3.13 us
  starting transfers between devices: 29.4 us -> 24 us
  other arithmetic: 4.41 us -> 0.08 us
    all_to_all x4 -> x1, waiting for transfers between devices: 58.2 us -> 0.01 us  [on_device(): lax.all_to_all(x, 'ctx', split_axis=0, concat_axis=0, tiled=True)]
    all_to_all x1 -> x2, blocking collectives: 32.4 us -> 82.8 us  [the longest x1 50.9 us: on_device(): lax.all_to_all(packed, 'ctx', split_axis=0, concat_axis=0, tiled=True)]
    all_to_all x4 -> x1, starting transfers between devices: 22.5 us -> 4.75 us  [on_device(): lax.all_to_all(x, 'ctx', split_axis=0, concat_axis=0, tiled=True)]
    ppermute x1 -> x8, starting transfers between devices: 2.26 us -> 14.6 us  [the longest x7 11.4 us: moved(): lax.ppermute(x.astype(BF), 'ctx', [(i, to(i)) for i in range(ctx)])]
    pallas_call x5 -> x7, Pallas kernels: 25.7 us -> 16.3 us  [the longest x1 5.92 us: on_device(): pl.pallas_call(functools.partial(spectral_kernel, inv_root), grid=(own //...]
    ppermute x1 -> x8, waiting for transfers between devices: 0.01 us -> 3.72 us  [the longest x7 2.66 us: moved(): lax.ppermute(x.astype(BF), 'ctx', [(i, to(i)) for i in range(ctx)])]
    slice x4 -> x0, local copies, waits for them, and re-layouts: 2.32 us -> none  [the longest x3 2.31 us: on_device(): x[rows - rim:]]
    unnamed x26, local copies, waits for them, and re-layouts: 4.23 us -> 2.49 us
  transfers between devices with their start and end apart: 6 -> 10, of which waited for: 4 -> 3; matrix products, arithmetic and copies ran while one was open for 4% -> 0% of each run, Pallas kernels for 7% -> 6%
where the time goes in v2:
time: 131 us
  blocking collectives  82.8 us (63%)
  starting transfers between devices  24 us (18%)
  Pallas kernels  16.3 us (12%)
  waiting for transfers between devices  3.72 us (3%)
  local copies, waits for them, and re-layouts  3.13 us (2%)
    all_to_all x1, blocking collectives, on_device(): lax.all_to_all(packed, 'ctx', split_axis=0, concat_axis=0, tiled=True)  50.9 us
    all_to_all x1, blocking collectives, on_device(): lax.all_to_all(x, 'ctx', split_axis=0, concat_axis=0, tiled=True)  31.9 us
    ppermute x7, starting transfers between devices, moved(): lax.ppermute(x.astype(BF), 'ctx', [(i, to(i)) for i in range(ctx)])  11.4 us
    pallas_call x1, Pallas kernels, on_device(): pl.pallas_call(functools.partial(spectral_kernel, inv_root), grid=(own //...  5.92 us
    all_to_all x1, starting transfers between devices, on_device(): lax.all_to_all(x, 'ctx', split_axis=0, concat_axis=0, tiled=True)  4.75 us
    ppermute x1, starting transfers between devices, on_device(): halo = lax.ppermute(tails, 'ctx', up)  4.58 us
    pallas_call x1, Pallas kernels, on_device(): pl.pallas_call(finish_kernel, grid=(steps,), in_specs=[block()] * 4 + [ro...  4.54 us
    ppermute x1, starting transfers between devices, on_device(): ahead = lax.ppermute(sums, 'ctx', down)  3.26 us
  transfers between devices with their start and end apart: 10, of which 3 were waited for; matrix products, arithmetic and copies ran while one was open for 0% of the time, Pallas kernels for 6%

profile of v2, /device:TPU:1, one launch (start us, length us, event | category | flops | bytes accessed | tf_op | source)
XLA Modules:
  0.0 130.9 jit_solution(11196890377810304829)
XLA Ops:
  0.7 1.6 %tails.1 = bf16[16,1024]{1,0:T(8,128)(2,1)} custom-call(bf16[256,1024]{1,0:T(8,128)(2,1)} %q_ref.5, bf16[256,1024]{1,0:T(8,128)(2,1)} %k_ref.5, bf16[256,1024]{1,0:T(8,128)(2,1)} %v_ref.5), custom_call_target="tpu_custom_call" | custom-call | tf_op jit(solution)/shard_map/tails/pallas_call | solution.py:263
  2.2 4.6 %collective-permute-start = (bf16[16,1024]{1,0:T(8,128)(2,1)}, bf16[16,1024]{1,0:T(8,128)(2,1)S(1)}, u32[]{:S(2)}, u32[]{:S(2)}) collective-permute-start(bf16[16,1024]{1,0:T(8,128)(2,1)} %tails.1), channel_id=1, source_target_pairs={{0,8},{8,16},{16,24},{24,32},{32,40},{40,48},{48,56},{56,64},{64,7... | collective-permute-start | bytes 98312 | tf_op jit(solution)/shard_map/ppermute | solution.py:271
  6.8 1.0 copy-done.6
  7.9 0.4 pack_filter.1.buf_ref
  8.3 0.4 copy-done.7
  8.7 1.4 %pack_signals.1 = bf16[32,3,2,32,128]{4,3,2,1,0:T(8,128)(2,1)S(1)} custom-call(bf16[256,1024]{1,0:T(8,128)(2,1)S(1)} %copy-done, bf16[256,1024]{1,0:T(8,128)(2,1)S(1)} %copy-done.1, bf16[256,1024]{1,0:T(8,128)(2,1)S(1)} %copy-done.2, bf16[256,1024]{1,0:T(8,128)(2,1)S(1)} %copy-done.3, ...), custom_call_target="tpu_custom_call", output_to_operand_aliasing={{}: (6, {})} | custom-call | tf_op jit(solution)/shard_map/pack_signals/pallas_call | solution.py:283
  10.2 50.9 %all_to_all.15.in_ref = bf16[32,3,2,32,128]{4,3,2,1,0:T(8,128)(2,1)S(1)} all-to-all(bf16[32,3,2,32,128]{4,3,2,1,0:T(8,128)(2,1)S(1)} %pack_signals.1), channel_id=1, replica_groups=mesh['ctx'=32,'tp'=8] {'ctx'}, dimensions={0} | all-to-all | bytes 3145728 | tf_op jit(solution)/shard_map/all_to_all | solution.py:294
  61.1 5.9 %spectral.1 = (bf16[32,2,2,32,128]{4,3,2,1,0:T(8,128)(2,1)S(1)}, bf16[32,1,2,32,128]{4,3,2,1,0:T(8,128)(2,1)S(1)}) custom-call(bf16[32,3,2,32,128]{4,3,2,1,0:T(8,128)(2,1)S(1)} %all_to_all.15.in_ref, bf16[128,64]{1,0:T(8,128)(2,1)S(1)} %copy-done.11, bf16[64,128]{1,0:T(8,128)(2,1)S(1)} %copy-done.12, bf16[256,256]{1,0:T(8,128)(2,1)S(1)} %copy-done.8, ...), custom_call_target="tpu_custom_call" | custom-call | tf_op jit(solution)/shard_map/spectral/pallas_call | solution.py:299
  67.1 31.9 %all_to_all.16.in_ref = bf16[32,2,2,32,128]{4,3,2,1,0:T(8,128)(2,1)S(1)} all-to-all(bf16[32,2,2,32,128]{4,3,2,1,0:T(8,128)(2,1)S(1)} %get-tuple-element.17), channel_id=1, replica_groups=mesh['ctx'=32,'tp'=8] {'ctx'}, dimensions={0} | all-to-all | bytes 2097152 | tf_op jit(solution)/shard_map/all_to_all | solution.py:312
  99.0 4.8 %all-to-all-start.2 = ((bf16[32,1,2,32,128]{4,3,2,1,0:T(8,128)(2,1)}), bf16[32,1,2,32,128]{4,3,2,1,0:T(8,128)(2,1)S(1)}, u32[]{:S(2)}, u32[]{:S(2)}) async-start(bf16[32,1,2,32,128]{4,3,2,1,0:T(8,128)(2,1)} %copy-done.5), calls=%async_computation.2 | async-start | bytes 1048576 | tf_op jit(solution)/shard_map/all_to_all | solution.py:312
  103.7 1.0 copy-done.4
  104.8 4.5 %finish.1 = (bf16[256,1024]{1,0:T(8,128)(2,1)}, bf16[256,1024]{1,0:T(8,128)(2,1)}, bf16[256,1024]{1,0:T(8,128)(2,1)}, bf16[256,1024]{1,0:T(8,128)(2,1)}, bf16[16...) custom-call(bf16[256,1024]{1,0:T(8,128)(2,1)S(1)} %copy-done, bf16[256,1024]{1,0:T(8,128)(2,1)S(1)} %copy-done.1, ...), custom_call_target="tpu_custom_call" | custom-call | tf_op jit(solution)/shard_map/finish/pallas_call | solution.py:318
  109.3 1.6 %collective-permute-start.4 = (bf16[16,1024]{1,0:T(8,128)(2,1)S(1)}, bf16[16,1024]{1,0:T(8,128)(2,1)S(1)}, u32[]{:S(2)}, u32[]{:S(2)}) collective-permute-start(bf16[16,1024]{1,0:T(8,128)(2,1)S(1)} %get-tuple-element.19), channel_id=1, source_target_pairs={{0,24},{8,16},{16,8},{24,0},{32,56},{40,48},{48,40},{56,32},{64,88... | collective-permute-start | bytes 98312 | tf_op jit(solution)/shard_map/ppermute | solution.py:225
  111.0 0.4 collective-permute-start.2
  111.4 1.7 %collective-permute-done.4 = bf16[16,1024]{1,0:T(8,128)(2,1)S(1)} collective-permute-done((bf16[16,1024]{1,0:T(8,128)(2,1)S(1)}, bf16[16,1024]{1,0:T(8,128)(2,1)S(1)}, u32[]{:S(2)}, u32[]{:S(2)}) %collective-permute-start.4) | collective-permute-done | bytes 32800 | tf_op jit(solution)/shard_map/ppermute | solution.py:225
  113.1 0.9 collective-permute-done.3
  114.1 4.1 %collective-permute-start.7 = (bf16[16,1024]{1,0:T(8,128)(2,1)S(1)}, bf16[16,1024]{1,0:T(8,128)(2,1)S(1)}, u32[]{:S(2)}, u32[]{:S(2)}) collective-permute-start(bf16[16,1024]{1,0:T(8,128)(2,1)S(1)} %fusion.1), channel_id=1, source_target_pairs={{0,192},{8,200},{16,208},{24,216},{32,224},{40,232},{48,240},{56,2... | collective-permute-start | bytes 98312 | tf_op jit(solution)/shard_map/ppermute | solution.py:225
  118.2 5.0 %collective-permute-start.5 = (bf16[16,1024]{1,0:T(8,128)(2,1)S(1)}, bf16[16,1024]{1,0:T(8,128)(2,1)S(1)}, u32[]{:S(2)}, u32[]{:S(2)}) collective-permute-start(bf16[16,1024]{1,0:T(8,128)(2,1)S(1)} %fusion.1), channel_id=1, source_target_pairs={{0,128},{8,136},{16,144},{24,152},{32,160},{40,168},{48,176},{56,1... | collective-permute-start | bytes 98312 | tf_op jit(solution)/shard_map/ppermute | solution.py:225
  123.2 3.3 %collective-permute-start.1 = (bf16[16,1024]{1,0:T(8,128)(2,1)S(1)}, bf16[16,1024]{1,0:T(8,128)(2,1)S(1)}, u32[]{:S(2)}, u32[]{:S(2)}) collective-permute-start(bf16[16,1024]{1,0:T(8,128)(2,1)S(1)} %get-tuple-element.19), channel_id=1, source_target_pairs={{8,0},{16,8},{24,16},{32,24},{40,32},{48,40},{56,48},{64,56},{72,6... | collective-permute-start | bytes 98312 | tf_op jit(solution)/shard_map/ppermute | solution.py:333
  126.6 0.1 collective-permute-start.8
  126.7 1.0 unpack_filter.1
  127.7 1.1 collective-permute-done.1.ahead_ref
  128.8 1.4 %rims.1 = (bf16[256,1024]{1,0:T(8,128)(2,1)}, bf16[256,1024]{1,0:T(8,128)(2,1)}, bf16[256,1024]{1,0:T(8,128)(2,1)}) custom-call(bf16[16,1024]{1,0:T(8,128)(2,1)S(1)} %collective-permute-done.1.ahead_ref, f32[8,1024]{1,0:T(8,128)S(1)} %get-tuple-element.20.last_ref, ...), custom_call_target="tpu_custom_call", output_to_operand_aliasing={{0}: (3, {}), {1}: (4, {}), {2}: (5, {})} | custom-call | tf_op jit(solution)/shard_map/rims/pallas_call | solution.py:334
  130.2 0.6 mul.11
  (35 shorter events, 0.2 us)
Async XLA Ops:
  0.6 7.6 %copy-start = (bf16[256,1024]{1,0:T(8,128)(2,1)S(1)}, bf16[256,1024]{1,0:T(8,128)(2,1)}, u32[]{:S(2)}) copy-start(bf16[256,1024]{1,0:T(8,128)(2,1)} %q_ref.5) | copy-start | bytes 1572868
  0.6 7.6 %copy-start.1 = (bf16[256,1024]{1,0:T(8,128)(2,1)S(1)}, bf16[256,1024]{1,0:T(8,128)(2,1)}, u32[]{:S(2)}) copy-start(bf16[256,1024]{1,0:T(8,128)(2,1)} %k_ref.5) | copy-start | bytes 1572868
  0.7 7.6 %copy-start.2 = (bf16[256,1024]{1,0:T(8,128)(2,1)S(1)}, bf16[256,1024]{1,0:T(8,128)(2,1)}, u32[]{:S(2)}) copy-start(bf16[256,1024]{1,0:T(8,128)(2,1)} %v_ref.5) | copy-start | bytes 1572868
  0.7 7.6 %copy-start.3 = (bf16[256,1024]{1,0:T(8,128)(2,1)S(1)}, bf16[256,1024]{1,0:T(8,128)(2,1)}, u32[]{:S(2)}) copy-start(bf16[256,1024]{1,0:T(8,128)(2,1)} %cot_ref.3) | copy-start | bytes 1572868
  2.2 6.0 %collective-permute-start = (bf16[16,1024]{1,0:T(8,128)(2,1)}, bf16[16,1024]{1,0:T(8,128)(2,1)S(1)}, u32[]{:S(2)}, u32[]{:S(2)}) collective-permute-start(bf16[16,1024]{1,0:T(8,128)(2,1)} %tails.1), channel_id=1, source_target_pairs={{0,8},{8,16},{16,24},{24,32},{32,40},{40,48},{48,56},{56,64},{64,7... | collective-permute-start | bytes 98312 | tf_op jit(solution)/shard_map/ppermute | solution.py:271
  6.8 1.0 copy-start.6
  7.9 0.8 copy-start.7
  10.1 51.0 %copy-start.8 = (bf16[256,256]{1,0:T(8,128)(2,1)S(1)}, bf16[256,256]{1,0:T(8,128)(2,1)}, u32[]{:S(2)}) copy-start(bf16[256,256]{1,0:T(8,128)(2,1)} %constant.14.clone.w_ref) | copy-start | bytes 393220
  10.1 51.0 %copy-start.9 = (bf16[256,256]{1,0:T(8,128)(2,1)S(1)}, bf16[256,256]{1,0:T(8,128)(2,1)}, u32[]{:S(2)}) copy-start(bf16[256,256]{1,0:T(8,128)(2,1)} %constant.15.clone.wi_ref) | copy-start | bytes 393220
  10.1 51.0 %copy-start.10 = (f32[2,64,128]{2,1,0:T(8,128)S(1)}, f32[2,64,128]{2,1,0:T(8,128)}, u32[]{:S(2)}) copy-start(f32[2,64,128]{2,1,0:T(8,128)} %constant.16.clone.turn_ref) | copy-start | bytes 196612
  10.2 51.0 %copy-start.11 = (bf16[128,64]{1,0:T(8,128)(2,1)S(1)}, bf16[128,64]{1,0:T(8,128)(2,1)}, u32[]{:S(2)}) copy-start(bf16[128,64]{1,0:T(8,128)(2,1)} %constant.12.clone.a_ref) | copy-start | bytes 49156
  10.2 51.0 %copy-start.12 = (bf16[64,128]{1,0:T(8,128)(2,1)S(1)}, bf16[64,128]{1,0:T(8,128)(2,1)}, u32[]{:S(2)}) copy-start(bf16[64,128]{1,0:T(8,128)(2,1)} %constant.13.clone.b_ref) | copy-start | bytes 49156
  67.1 31.9 %copy-start.5 = (bf16[32,1,2,32,128]{4,3,2,1,0:T(8,128)(2,1)}, bf16[32,1,2,32,128]{4,3,2,1,0:T(8,128)(2,1)S(1)}, u32[]{:S(2)}) copy-start(bf16[32,1,2,32,128]{4,3,2,1,0:T(8,128)(2,1)S(1)} %get-tuple-element.27) | copy-start | bytes 1572868
  99.0 27.7 %all-to-all-start.2 = ((bf16[32,1,2,32,128]{4,3,2,1,0:T(8,128)(2,1)}), bf16[32,1,2,32,128]{4,3,2,1,0:T(8,128)(2,1)S(1)}, u32[]{:S(2)}, u32[]{:S(2)}) async-start(bf16[32,1,2,32,128]{4,3,2,1,0:T(8,128)(2,1)} %copy-done.5), calls=%async_computation.2 | async-start | bytes 1048576 | tf_op jit(solution)/shard_map/all_to_all | solution.py:312
  103.7 1.0 copy-start.4
  109.3 3.8 %collective-permute-start.4 = (bf16[16,1024]{1,0:T(8,128)(2,1)S(1)}, bf16[16,1024]{1,0:T(8,128)(2,1)S(1)}, u32[]{:S(2)}, u32[]{:S(2)}) collective-permute-start(bf16[16,1024]{1,0:T(8,128)(2,1)S(1)} %get-tuple-element.19), channel_id=1, source_target_pairs={{0,24},{8,16},{16,8},{24,0},{32,56},{40,48},{48,40},{56,32},{64,88... | collective-permute-start | bytes 98312 | tf_op jit(solution)/shard_map/ppermute | solution.py:225
  110.9 3.1 %collective-permute-start.3 = (bf16[16,1024]{1,0:T(8,128)(2,1)S(1)}, bf16[16,1024]{1,0:T(8,128)(2,1)S(1)}, u32[]{:S(2)}, u32[]{:S(2)}) collective-permute-start(bf16[16,1024]{1,0:T(8,128)(2,1)S(1)} %get-tuple-element.19), channel_id=1, source_target_pairs={{0,16},{8,24},{16,0},{24,8},{32,48},{40,56},{48,32},{56,40},{64,80... | collective-permute-start | bytes 98312 | tf_op jit(solution)/shard_map/ppermute | solution.py:225
  111.0 3.1 %collective-permute-start.2 = (bf16[16,1024]{1,0:T(8,128)(2,1)S(1)}, bf16[16,1024]{1,0:T(8,128)(2,1)S(1)}, u32[]{:S(2)}, u32[]{:S(2)}) collective-permute-start(bf16[16,1024]{1,0:T(8,128)(2,1)S(1)} %get-tuple-element.19), channel_id=1, source_target_pairs={{0,8},{8,0},{16,24},{24,16},{32,40},{40,32},{48,56},{56,48},{64,72... | collective-permute-start | bytes 98312 | tf_op jit(solution)/shard_map/ppermute | solution.py:225
  114.1 12.4 %collective-permute-start.7 = (bf16[16,1024]{1,0:T(8,128)(2,1)S(1)}, bf16[16,1024]{1,0:T(8,128)(2,1)S(1)}, u32[]{:S(2)}, u32[]{:S(2)}) collective-permute-start(bf16[16,1024]{1,0:T(8,128)(2,1)S(1)} %fusion.1), channel_id=1, source_target_pairs={{0,192},{8,200},{16,208},{24,216},{32,224},{40,232},{48,240},{56,2... | collective-permute-start | bytes 98312 | tf_op jit(solution)/shard_map/ppermute | solution.py:225
  118.2 8.3 %collective-permute-start.6 = (bf16[16,1024]{1,0:T(8,128)(2,1)S(1)}, bf16[16,1024]{1,0:T(8,128)(2,1)S(1)}, u32[]{:S(2)}, u32[]{:S(2)}) collective-permute-start(bf16[16,1024]{1,0:T(8,128)(2,1)S(1)} %fusion.1), channel_id=1, source_target_pairs={{0,64},{8,72},{16,80},{24,88},{32,96},{40,104},{48,112},{56,120},{... | collective-permute-start | bytes 98312 | tf_op jit(solution)/shard_map/ppermute | solution.py:225
  118.2 8.3 %collective-permute-start.5 = (bf16[16,1024]{1,0:T(8,128)(2,1)S(1)}, bf16[16,1024]{1,0:T(8,128)(2,1)S(1)}, u32[]{:S(2)}, u32[]{:S(2)}) collective-permute-start(bf16[16,1024]{1,0:T(8,128)(2,1)S(1)} %fusion.1), channel_id=1, source_target_pairs={{0,128},{8,136},{16,144},{24,152},{32,160},{40,168},{48,176},{56,1... | collective-permute-start | bytes 98312 | tf_op jit(solution)/shard_map/ppermute | solution.py:225
  123.2 5.5 %collective-permute-start.1 = (bf16[16,1024]{1,0:T(8,128)(2,1)S(1)}, bf16[16,1024]{1,0:T(8,128)(2,1)S(1)}, u32[]{:S(2)}, u32[]{:S(2)}) collective-permute-start(bf16[16,1024]{1,0:T(8,128)(2,1)S(1)} %get-tuple-element.19), channel_id=1, source_target_pairs={{8,0},{16,8},{24,16},{32,24},{40,32},{48,40},{56,48},{64,56},{72,6... | collective-permute-start | bytes 98312 | tf_op jit(solution)/shard_map/ppermute | solution.py:333
  126.6 3.6 %collective-permute-start.8 = (bf16[16,1024]{1,0:T(8,128)(2,1)S(1)}, bf16[16,1024]{1,0:T(8,128)(2,1)S(1)}, u32[]{:S(2)}, u32[]{:S(2)}) collective-permute-start(bf16[16,1024]{1,0:T(8,128)(2,1)S(1)} %get-tuple-element.28), channel_id=1, source_target_pairs={{0,32},{8,40},{16,48},{24,56},{32,0},{40,8},{48,16},{56,24},{64,96... | collective-permute-start | bytes 98312 | tf_op jit(solution)/shard_map/ppermute | solution.py:225

commit v3 on v2

v3 whole, which is shorter than its diff:
```python
import functools
import math

import jax
import jax.numpy as jnp
from jax import lax
from jax.experimental import pallas as pl
from jax.experimental.pallas import tpu as pltpu
from jax.sharding import PartitionSpec as P
import numpy as np

BF = jnp.bfloat16
F32 = jnp.float32
LANES = 128


def tables(outer, length):
    r = np.arange(outer)
    k1 = 4 * np.arange(outer) + 1
    s = np.arange(LANES)
    theta = (k1[:, None] * r[None, :] % (4 * outer)) * (2.0 * math.pi / (4 * outer))
    phi = (k1[:, None] * s[None, :] % (4 * length)) * (2.0 * math.pi / (4 * length))
    psi = (s[:, None] * s[None, :] % LANES) * (2.0 * math.pi / LANES)
    first = np.concatenate([np.cos(theta), -np.sin(theta)], axis=0)
    c2, s2 = np.cos(psi), np.sin(psi)
    second = np.block([[c2, -s2], [s2, c2]])
    last = first.T / length
    as_bf = lambda x: jnp.asarray(x.astype(np.float32), BF)
    turn = np.stack([np.cos(phi), np.sin(phi)]).astype(np.float32)
    return as_bf(first), as_bf(last), as_bf(second), as_bf(second.T), jnp.asarray(turn)


def lane_tiles(ref):
    return [slice(t * LANES, (t + 1) * LANES) for t in range(ref.shape[-1] // LANES)]


def filter_taps(scratch, at, rows, weights, stream):
    total = weights[stream, 0:1, :] * scratch[pl.ds(at, rows), :]
    for lag in range(1, 3):
        total = total + weights[stream, lag : lag + 1, :] * scratch[pl.ds(at - lag, rows), :]
    return total


def stage(scratch, signal, halo):
    scratch[pl.ds(6, 2), :] = halo
    scratch[pl.ds(8, signal.shape[0]), :] = signal.astype(F32)


def put_transposed(signal, out_ref, tile, slot):
    own = out_ref.shape[3]
    per = LANES // own
    for b in range(signal.shape[0] // LANES):
        turned = jnp.transpose(signal[b * LANES : (b + 1) * LANES, :]).astype(BF)
        out_ref[tile * per : (tile + 1) * per, slot, b] = turned.reshape(per, own, LANES)


def get_transposed(in_ref, tile, slot):
    per = LANES // in_ref.shape[3]
    blocks = []
    for b in range(in_ref.shape[2]):
        part = in_ref[tile * per : (tile + 1) * per, slot, b].reshape(LANES, LANES)
        blocks.append(jnp.transpose(part.astype(F32)))
    return jnp.concatenate(blocks, axis=0)


def tails_kernel(q_ref, k_ref, v_ref, out_ref):
    rows = [ref[...].astype(F32)[14:, :] for ref in (q_ref, k_ref, v_ref)]
    fill = jnp.zeros((10, out_ref.shape[1]), F32)
    out_ref[...] = jnp.concatenate(rows + [fill], axis=0).astype(BF)


def pack_filter_kernel(h_ref, out_ref):
    for t, at in enumerate(lane_tiles(h_ref)):
        put_transposed(h_ref[:, at].astype(F32), out_ref, t, 2)


def pack_signals_kernel(q_ref, k_ref, v_ref, cot_ref, halo_ref, w_ref, buf_ref, out_ref, qs, ks, vs):
    del buf_ref
    rows = q_ref.shape[0]
    for t, at in enumerate(lane_tiles(q_ref)):
        halo = halo_ref[:, at].astype(F32)
        w = w_ref[:, :, at]
        stage(qs, q_ref[:, at], halo[0:2])
        stage(ks, k_ref[:, at], halo[2:4])
        stage(vs, v_ref[:, at], halo[4:6])
        mixed = filter_taps(ks, 8, rows, w, 1) * filter_taps(vs, 8, rows, w, 2)
        put_transposed(mixed, out_ref, t, 0)
        grad_conv = cot_ref[:, at].astype(F32) * filter_taps(qs, 8, rows, w, 0)
        put_transposed(grad_conv, out_ref, t, 1)


def to_spectrum(signal, a_ref, w_ref, turn_ref):
    sources, halves, chans, _ = signal.shape
    n1 = turn_ref.shape[1]
    cos_t, sin_t = turn_ref[0], turn_ref[1]
    by_chan = jnp.swapaxes(signal.reshape(sources * halves, chans, LANES).astype(F32), 0, 1)
    by_chan = by_chan.astype(BF)
    cols = jnp.concatenate([by_chan[i] for i in range(chans)], axis=1)
    first = jnp.dot(a_ref[...], cols, preferred_element_type=F32)
    parts = []
    for i in range(chans):
        y_re = first[:n1, i * LANES : (i + 1) * LANES]
        y_im = first[n1:, i * LANES : (i + 1) * LANES]
        z_re = y_re * cos_t + y_im * sin_t
        z_im = y_im * cos_t - y_re * sin_t
        parts.append(jnp.concatenate([z_re.astype(BF), z_im.astype(BF)], axis=1))
    spec = jnp.dot(jnp.concatenate(parts, axis=0), w_ref[...], preferred_element_type=F32)
    return spec[:, :LANES], spec[:, LANES:]


def from_spectrum(spec, chans, b_ref, wi_ref, turn_ref):
    n1 = turn_ref.shape[1]
    cos_t, sin_t = turn_ref[0], turn_ref[1]
    back = jnp.dot(spec, wi_ref[...], preferred_element_type=F32)
    parts = []
    for i in range(chans):
        u_re = back[i * n1 : (i + 1) * n1, :LANES]
        u_im = back[i * n1 : (i + 1) * n1, LANES:]
        v_re = u_re * cos_t - u_im * sin_t
        v_im = u_im * cos_t + u_re * sin_t
        parts.append(jnp.concatenate([v_re.astype(BF), v_im.astype(BF)], axis=0))
    signal = jnp.dot(b_ref[...], jnp.concatenate(parts, axis=1), preferred_element_type=F32)
    stacked = jnp.stack([signal[:, i * LANES : (i + 1) * LANES] for i in range(chans)], axis=0)
    return jnp.swapaxes(stacked, 0, 1).astype(BF)


def spectral_kernel(
    inv_root, in_ref, a_ref, b_ref, w_ref, wi_ref, turn_ref, streams_ref, filters_ref
):
    sources, _, halves, own, _ = in_ref.shape
    chans = 16
    for first in range(0, own, chans):
        at = slice(first, first + chans)

        def put(out_ref, slot, re, im):
            spec = jnp.concatenate([re.astype(BF), im.astype(BF)], axis=1)
            signal = from_spectrum(spec, chans, b_ref, wi_ref, turn_ref)
            out_ref[:, slot, :, at] = signal.reshape(sources, halves, chans, LANES)

        x_re, x_im = to_spectrum(in_ref[:, 0, :, at], a_ref, w_ref, turn_ref)
        h_re, h_im = to_spectrum(in_ref[:, 2, :, at], a_ref, w_ref, turn_ref)
        put(streams_ref, 0, x_re * h_re - x_im * h_im, x_re * h_im + x_im * h_re)
        g_re, g_im = to_spectrum(in_ref[:, 1, :, at], a_ref, w_ref, turn_ref)
        put(streams_ref, 1, g_re * h_re + g_im * h_im, g_im * h_re - g_re * h_im)
        cross_re = (g_re * x_re + g_im * x_im) * inv_root
        cross_im = (g_im * x_re - g_re * x_im) * inv_root
        put(filters_ref, 0, cross_re, cross_im)


def local_terms(refs, halo_ref, w_ref, in_ref, scratch, t, at):
    q_ref, k_ref, v_ref, cot_ref = refs
    rows = q_ref.shape[0]
    halo = halo_ref[:, at].astype(F32)
    w = w_ref[:, :, at]
    for i, ref in enumerate((q_ref, k_ref, v_ref)):
        stage(scratch[i], ref[:, at], halo[2 * i : 2 * i + 2])
    conv = get_transposed(in_ref, t, 0)
    grad_mixed = get_transposed(in_ref, t, 1)
    grads = (
        cot_ref[:, at].astype(F32) * conv,
        grad_mixed * filter_taps(scratch[2], 8, rows, w, 2),
        grad_mixed * filter_taps(scratch[1], 8, rows, w, 1),
    )
    return w, conv, [grad.astype(BF).astype(F32) for grad in grads]


def sums_kernel(
    q_ref, k_ref, v_ref, cot_ref, halo_ref, w_ref, in_ref, sums_ref, qs, ks, vs
):
    refs = (q_ref, k_ref, v_ref, cot_ref)
    rows = q_ref.shape[0]
    for t, at in enumerate(lane_tiles(q_ref)):
        _, _, grads = local_terms(refs, halo_ref, w_ref, in_ref, (qs, ks, vs), t, at)
        out = []
        for grad, staged in zip(grads, (qs, ks, vs)):
            for lag in range(3):
                out.append(jnp.sum(grad * staged[pl.ds(8 - lag, rows), :], axis=0, keepdims=True))
        out.append(jnp.zeros((1, LANES), F32))
        out.extend(grad[:2] for grad in grads)
        sums_ref[:, at] = jnp.concatenate(out, axis=0).astype(BF)


def finish_kernel(
    q_ref,
    k_ref,
    v_ref,
    cot_ref,
    halo_ref,
    w_ref,
    in_ref,
    out_ref,
    gq_ref,
    gk_ref,
    gv_ref,
    last_ref,
    qs,
    ks,
    vs,
    gs,
):
    refs = (q_ref, k_ref, v_ref, cot_ref)
    rows = q_ref.shape[0]
    gs[pl.ds(rows, 8), :] = jnp.zeros((8, LANES), F32)
    for t, at in enumerate(lane_tiles(q_ref)):
        w, conv, grads = local_terms(refs, halo_ref, w_ref, in_ref, (qs, ks, vs), t, at)
        out_ref[:, at] = (filter_taps(qs, 8, rows, w, 0) * conv).astype(BF)
        lasts = []
        for i, (grad, out) in enumerate(zip(grads, (gq_ref, gk_ref, gv_ref))):
            gs[pl.ds(0, rows), :] = grad
            back = w[i, 0:1, :] * grad
            for lag in range(1, 3):
                back = back + w[i, lag : lag + 1, :] * gs[pl.ds(lag, rows), :]
            out[:, at] = back.astype(BF)
            lasts.append(back[rows - 2 :])
        lasts.append(jnp.zeros((2, LANES), F32))
        last_ref[:, at] = jnp.concatenate(lasts, axis=0)


def unpack_kernel(in_ref, out_ref):
    for t, at in enumerate(lane_tiles(out_ref)):
        out_ref[:, at] = get_transposed(in_ref, t, 0).astype(BF)


def close_kernel(
    inv_root,
    mine_ref,
    other_ref,
    near_ref,
    last_ref,
    w_ref,
    gq_in,
    gk_in,
    gv_in,
    short_ref,
    gq_out,
    gk_out,
    gv_out,
):
    mine = mine_ref[...]
    other = other_ref[...].astype(F32)
    total = (mine + other) * inv_root
    ahead = jnp.where(mine > 0.0, other, near_ref[...])
    row = lax.broadcasted_iota(jnp.int32, mine.shape, 0)
    streams = ((gq_in, gq_out), (gk_in, gk_out), (gv_in, gv_out))
    for i, (before, after) in enumerate(streams):
        short_ref[i] = total[3 * i : 3 * i + 3]
        w1 = w_ref[i, 1:2, :]
        w2 = w_ref[i, 2:3, :]
        next0 = ahead[10 + 2 * i : 11 + 2 * i]
        next1 = ahead[11 + 2 * i : 12 + 2 * i]
        end0 = last_ref[2 * i : 2 * i + 1] + w2 * next0
        end1 = last_ref[2 * i + 1 : 2 * i + 2] + w1 * next0 + w2 * next1
        fixed = jnp.where(row == 14, end0, jnp.where(row == 15, end1, before[...].astype(F32)))
        after[...] = fixed.astype(BF)


def sum_over_ctx(terms, beside):
    ctx = lax.axis_size("ctx")
    rank = lax.axis_index("ctx")
    slow, fast = rank // 4, rank % 4
    summed = lax.broadcasted_iota(jnp.int32, terms.shape, 0) < 10

    def moved(x, to):
        return lax.ppermute(x.astype(BF), "ctx", [(i, to(i)) for i in range(ctx)]).astype(F32)

    mine = terms.astype(F32)
    near = [moved(mine, lambda i, d=d: i ^ d) for d in (1, 2, 3)]
    total = lax.reduce_precision((mine + near[0]) + (near[1] + near[2]), 8, 7)
    heads = mine
    for d in (1, 2, 3):
        heads = jnp.where(fast == d, near[d - 1], heads)
    beyond = jnp.where(fast == 1, near[2], near[0])
    beyond = jnp.where(fast == 3, 0.0, beyond)
    total = jnp.where(summed, total, heads)
    total, beyond, beside = lax.optimization_barrier((total, beyond, beside))
    far = [moved(total, lambda i, d=d: (i + d) % ctx) for d in (ctx // 4, ctx // 2, 3 * ctx // 4)]
    heads = jnp.where(slow % 2 == 0, far[2], total)
    total = lax.reduce_precision((total + far[1]) + (far[0] + far[2]), 8, 7)
    other = lax.ppermute(
        jnp.where(summed, total, heads).astype(BF), "ctx", [(i, i ^ (ctx // 8)) for i in range(ctx)]
    )
    takes = jnp.where((fast == 3) & (rank < ctx - 1), 1.0, 0.0)
    return jnp.where(summed, total, takes), other, beyond, beside


def params(mib=32):
    return pltpu.CompilerParams(vmem_limit_bytes=mib * 1024 * 1024)


def on_device(query_in, key_in, value_in, cotangent, short_weight, long_filter):
    rows, channels = query_in.shape
    taps = short_weight.shape[1]
    ctx = lax.axis_size("ctx")
    length = rows * ctx
    inv_root = 1.0 / math.sqrt(length)
    own = channels // ctx
    halves = rows // LANES
    outer = length // LANES
    wide_step = 512
    steps = channels // wide_step
    per_step = wide_step // own
    consts = tables(outer, length)

    up = [(i, i + 1) for i in range(ctx - 1)]
    block = lambda: pl.BlockSpec((rows, wide_step), lambda j: (0, j))
    row_block = lambda n: pl.BlockSpec((n, wide_step), lambda j: (0, j))
    w_block = lambda: pl.BlockSpec((3, taps, wide_step), lambda j: (0, 0, j))
    end_block = lambda: pl.BlockSpec((16, channels), lambda j: (rows // 16 - 1, 0))
    small = lambda n: pl.BlockSpec((n, channels), lambda j: (0, 0))

    tails = pl.pallas_call(
        tails_kernel,
        grid=(1,),
        in_specs=[end_block()] * 3,
        out_specs=small(16),
        out_shape=jax.ShapeDtypeStruct((16, channels), BF),
        name="tails",
    )(query_in, key_in, value_in)
    halo = lax.ppermute(tails, "ctx", up)

    buf_shape = jax.ShapeDtypeStruct((ctx, 3, halves, own, LANES), BF)
    in_vmem = pl.BlockSpec(memory_space=pltpu.VMEM)
    packed = pl.pallas_call(
        pack_filter_kernel,
        in_specs=[in_vmem],
        out_specs=in_vmem,
        out_shape=buf_shape,
        compiler_params=params(),
        name="pack_filter",
    )(long_filter)
    packed = pl.pallas_call(
        pack_signals_kernel,
        in_specs=[in_vmem] * 7,
        out_specs=in_vmem,
        out_shape=buf_shape,
        scratch_shapes=[pltpu.VMEM((rows + 8, LANES), F32)] * 3,
        input_output_aliases={6: 0},
        compiler_params=params(),
        name="pack_signals",
    )(query_in, key_in, value_in, cotangent, halo, short_weight, packed)
    arrived = lax.all_to_all(packed, "ctx", split_axis=0, concat_axis=0, tiled=True)

    streams, filters = pl.pallas_call(
        functools.partial(spectral_kernel, inv_root),
        in_specs=[in_vmem] * (1 + len(consts)),
        out_specs=[in_vmem] * 2,
        out_shape=[jax.ShapeDtypeStruct((ctx, n, halves, own, LANES), BF) for n in (2, 1)],
        compiler_params=params(),
        name="spectral",
    )(arrived, *consts)
    streams = lax.all_to_all(streams, "ctx", split_axis=0, concat_axis=0, tiled=True)
    filters = lax.all_to_all(filters, "ctx", split_axis=0, concat_axis=0, tiled=True)

    wide = jax.ShapeDtypeStruct((rows, channels), BF)
    message = pl.BlockSpec((per_step, 2, halves, own, LANES), lambda j: (j, 0, 0, 0, 0))
    local_specs = [block()] * 4 + [row_block(16), w_block(), message]
    local_args = (query_in, key_in, value_in, cotangent, halo, short_weight, streams)
    sums = pl.pallas_call(
        sums_kernel,
        in_specs=[in_vmem] * len(local_args),
        out_specs=in_vmem,
        out_shape=jax.ShapeDtypeStruct((16, channels), BF),
        scratch_shapes=[pltpu.VMEM((rows + 8, LANES), F32)] * 3,
        compiler_params=params(),
        name="sums",
    )(*local_args)
    block_out, grad_q, grad_k, grad_v, last = pl.pallas_call(
        finish_kernel,
        grid=(steps,),
        in_specs=local_specs,
        out_specs=[block()] * 4 + [row_block(8)],
        out_shape=[wide] * 4 + [jax.ShapeDtypeStruct((8, channels), F32)],
        scratch_shapes=[pltpu.VMEM((rows + 8, LANES), F32)] * 4,
        compiler_params=params(),
        name="finish",
    )(*local_args)

    grad_filter = pl.pallas_call(
        unpack_kernel,
        grid=(steps,),
        in_specs=[pl.BlockSpec((per_step, 1, halves, own, LANES), lambda j: (j, 0, 0, 0, 0))],
        out_specs=block(),
        out_shape=wide,
        compiler_params=params(),
        name="unpack_filter",
    )(filters)

    mine, other, beyond, last = sum_over_ctx(sums, last)
    all_taps = lambda: pl.BlockSpec((3, taps, channels), lambda j: (0, 0, 0))
    grad_short, grad_q, grad_k, grad_v = pl.pallas_call(
        functools.partial(close_kernel, inv_root),
        grid=(1,),
        in_specs=[small(16)] * 3 + [small(8), all_taps()] + [end_block()] * 3,
        out_specs=[all_taps()] + [end_block()] * 3,
        out_shape=[jax.ShapeDtypeStruct((3, taps, channels), F32)] + [wide] * 3,
        input_output_aliases={5: 1, 6: 2, 7: 3},
        compiler_params=params(),
        name="close",
    )(mine, other, beyond, last, short_weight, grad_q, grad_k, grad_v)
    return (block_out, grad_q, grad_k, grad_v, grad_short, grad_filter)


def solution(mesh):
    wide = P("ctx", "tp")
    taps = P(None, None, "tp")
    return jax.shard_map(
        on_device,
        mesh=mesh,
        in_specs=(wide, wide, wide, wide, taps, wide),
        out_specs=(wide, wide, wide, wide, taps, wide),
        check_vma=False,
    )
```

time: 131 us -> 128 us (0.977)
  starting transfers between devices: 24 us -> 20.2 us
  local copies, waits for them, and re-layouts: 3.13 us -> 1.1 us
    ppermute x1, starting transfers between devices: 3.26 us -> 0.38 us  [sum_over_ctx(): lax.ppermute(jnp.where(summed, total, heads).astype(BF), 'ctx', [(i, i ^...]
    ppermute x7 -> x6, starting transfers between devices: 11.4 us -> 9.85 us  [moved(): lax.ppermute(x.astype(BF), 'ctx', [(i, to(i)) for i in range(ctx)])]
    unnamed x26 -> x24, local copies, waits for them, and re-layouts: 2.49 us -> 1.1 us
    ppermute x7 -> x6, waiting for transfers between devices: 2.66 us -> 3.78 us  [moved(): lax.ppermute(x.astype(BF), 'ctx', [(i, to(i)) for i in range(ctx)])]
    pallas_call x6 -> x7, Pallas kernels: 14.7 us -> 15.3 us  [the longest x1 4.9 us: on_device(): pl.pallas_call(functools.partial(spectral_kernel, inv_root), in_specs=[in...]
  transfers between devices with their start and end apart: 10 -> 9, of which waited for: 3 -> 5; matrix products, arithmetic and copies ran while one was open for 0% -> 0% of each run, Pallas kernels for 6% -> 6%
where the time goes in v3:
time: 128 us; the launch traced here: 127 us
  blocking collectives  83.3 us (65%)
  starting transfers between devices  20.2 us (16%)
  Pallas kernels  16.9 us (13%)
  waiting for transfers between devices  4.36 us (3%)
    all_to_all x1, blocking collectives, on_device(): lax.all_to_all(packed, 'ctx', split_axis=0, concat_axis=0, tiled=True)  51.4 us
    all_to_all x1, blocking collectives, on_device(): lax.all_to_all(streams, 'ctx', split_axis=0, concat_axis=0, tiled=True)  31.9 us
    ppermute x6, starting transfers between devices, moved(): lax.ppermute(x.astype(BF), 'ctx', [(i, to(i)) for i in range(ctx)])  9.85 us
    all_to_all x1, starting transfers between devices, on_device(): lax.all_to_all(filters, 'ctx', split_axis=0, concat_axis=0, tiled=True)  5.41 us
    pallas_call x1, Pallas kernels, on_device(): pl.pallas_call(functools.partial(spectral_kernel, inv_root), in_specs=[in...  4.9 us
    ppermute x1, starting transfers between devices, on_device(): halo = lax.ppermute(tails, 'ctx', up)  4.58 us
    ppermute x6, waiting for transfers between devices, moved(): lax.ppermute(x.astype(BF), 'ctx', [(i, to(i)) for i in range(ctx)])  3.78 us
    pallas_call x1, Pallas kernels, on_device(): pl.pallas_call(finish_kernel, grid=(steps,), in_specs=local_specs, out_sp...  3.69 us
  transfers between devices with their start and end apart: 9, of which 5 were waited for; matrix products, arithmetic and copies ran while one was open for 0% of the time, Pallas kernels for 6%

profile of v3, /device:TPU:1, one launch (start us, length us, event | category | flops | bytes accessed | tf_op | source)
XLA Modules:
  0.0 126.8 jit_solution(12624073486722881528)
XLA Ops:
  0.7 1.6 %tails.1 = bf16[16,1024]{1,0:T(8,128)(2,1)} custom-call(bf16[256,1024]{1,0:T(8,128)(2,1)} %q_ref.7, bf16[256,1024]{1,0:T(8,128)(2,1)} %k_ref.7, bf16[256,1024]{1,0:T(8,128)(2,1)} %v_ref.7), custom_call_target="tpu_custom_call" | custom-call | tf_op jit(solution)/shard_map/tails/pallas_call | solution.py:311
  2.2 4.6 %collective-permute-start = (bf16[16,1024]{1,0:T(8,128)(2,1)}, bf16[16,1024]{1,0:T(8,128)(2,1)S(1)}, u32[]{:S(2)}, u32[]{:S(2)}) collective-permute-start(bf16[16,1024]{1,0:T(8,128)(2,1)} %tails.1), channel_id=1, source_target_pairs={{0,8},{8,16},{16,24},{24,32},{32,40},{40,48},{48,56},{56,64},{64,7... | collective-permute-start | bytes 98312 | tf_op jit(solution)/shard_map/ppermute | solution.py:319
  6.8 1.0 copy-done.6
  7.9 0.2 pack_filter.1.buf_ref
  8.2 1.2 pack_signals.1
  9.4 51.4 %all_to_all.15.in_ref = bf16[32,3,2,32,128]{4,3,2,1,0:T(8,128)(2,1)S(1)} all-to-all(bf16[32,3,2,32,128]{4,3,2,1,0:T(8,128)(2,1)S(1)} %pack_signals.1), channel_id=1, replica_groups=mesh['ctx'=32,'tp'=8] {'ctx'}, dimensions={0} | all-to-all | bytes 3145728 | tf_op jit(solution)/shard_map/all_to_all | solution.py:341
  60.8 4.9 %spectral.1 = (bf16[32,2,2,32,128]{4,3,2,1,0:T(8,128)(2,1)S(1)}, bf16[32,1,2,32,128]{4,3,2,1,0:T(8,128)(2,1)S(1)}) custom-call(bf16[32,3,2,32,128]{4,3,2,1,0:T(8,128)(2,1)S(1)} %all_to_all.15.in_ref, bf16[128,64]{1,0:T(8,128)(2,1)S(1)} %copy-done.10, bf16[64,128]{1,0:T(8,128)(2,1)S(1)} %copy-done.11, bf16[256,256]{1,0:T(8,128)(2,1)S(1)} %copy-done.8, ...), custom_call_target="tpu_custom_call" | custom-call | tf_op jit(solution)/shard_map/spectral/pallas_call | solution.py:343
  65.8 31.9 %all_to_all.16.in_ref = bf16[32,2,2,32,128]{4,3,2,1,0:T(8,128)(2,1)S(1)} all-to-all(bf16[32,2,2,32,128]{4,3,2,1,0:T(8,128)(2,1)S(1)} %get-tuple-element.20), channel_id=1, replica_groups=mesh['ctx'=32,'tp'=8] {'ctx'}, dimensions={0} | all-to-all | bytes 2097152 | tf_op jit(solution)/shard_map/all_to_all | solution.py:351
  97.6 5.4 %all-to-all-start.2 = ((bf16[32,1,2,32,128]{4,3,2,1,0:T(8,128)(2,1)}), bf16[32,1,2,32,128]{4,3,2,1,0:T(8,128)(2,1)}, u32[]{:S(2)}, u32[]{:S(2)}) async-start(bf16[32,1,2,32,128]{4,3,2,1,0:T(8,128)(2,1)} %copy-done.5), calls=%async_computation.2 | async-start | bytes 1048576 | tf_op jit(solution)/shard_map/all_to_all | solution.py:352
  103.1 2.0 %sums.1 = bf16[16,1024]{1,0:T(8,128)(2,1)S(1)} custom-call(bf16[256,1024]{1,0:T(8,128)(2,1)S(1)} %copy-done, bf16[256,1024]{1,0:T(8,128)(2,1)S(1)} %copy-done.1, bf16[256,1024]{1,0:T(8,128)(2,1)S(1)} %copy-done.2, bf16[256,1024]{1,0:T(8,128)(2,1)S(1)} %copy-done.3, bf16[16,1024]{1,0:T(8,128)(2,1)S(1)} %collective-permute-done.halo_ref, ...), custom_call_target="tpu_custom_call" | custom-call | tf_op jit(solution)/shard_map/sums/pallas_call | solution.py:358
  105.0 1.7 %collective-permute-start.3 = (bf16[16,1024]{1,0:T(8,128)(2,1)S(1)}, bf16[16,1024]{1,0:T(8,128)(2,1)S(1)}, u32[]{:S(2)}, u32[]{:S(2)}) collective-permute-start(bf16[16,1024]{1,0:T(8,128)(2,1)S(1)} %sums.1), channel_id=1, source_target_pairs={{0,24},{8,16},{16,8},{24,0},{32,56},{40,48},{48,40},{56,32},{64,88... | collective-permute-start | bytes 98312 | tf_op jit(solution)/shard_map/ppermute | solution.py:264
  106.7 0.1 collective-permute-start.2
  106.9 0.4 collective-permute-start.1
  107.3 3.7 %finish.1 = (bf16[256,1024]{1,0:T(8,128)(2,1)}, bf16[256,1024]{1,0:T(8,128)(2,1)}, bf16[256,1024]{1,0:T(8,128)(2,1)}, bf16[256,1024]{1,0:T(8,128)(2,1)}, f32[8,1024]{1,0:T(8,128)S(1)}) custom-call(bf16[256,1024]{1,0:T(8,128)(2,1)S(1)} %copy-done, bf16[256,1024]{1,0:T(8,128)(2,1)S(1)} %copy-done.1, bf16[256,1024]{1,0:T(8,128)(2,1)S(1)} %copy-done.2, ...), custom_call_target="tpu_custom_call" | custom-call | tf_op jit(solution)/shard_map/finish/pallas_call | solution.py:367
  110.9 0.2 collective-permute-done.2
  111.3 3.9 %collective-permute-start.6 = (bf16[16,1024]{1,0:T(8,128)(2,1)S(1)}, bf16[16,1024]{1,0:T(8,128)(2,1)S(1)}, u32[]{:S(2)}, u32[]{:S(2)}) collective-permute-start(bf16[16,1024]{1,0:T(8,128)(2,1)S(1)} %convert_element_type.36), channel_id=1, source_target_pairs={{0,192},{8,200},{16,208},{24,216},{32,224},{40,232},{48,240},{56,2... | collective-permute-start | bytes 98312 | tf_op jit(solution)/shard_map/ppermute | solution.py:264
  115.2 3.7 %collective-permute-start.4 = (bf16[16,1024]{1,0:T(8,128)(2,1)S(1)}, bf16[16,1024]{1,0:T(8,128)(2,1)S(1)}, u32[]{:S(2)}, u32[]{:S(2)}) collective-permute-start(bf16[16,1024]{1,0:T(8,128)(2,1)S(1)} %convert_element_type.36), channel_id=1, source_target_pairs={{0,128},{8,136},{16,144},{24,152},{32,160},{40,168},{48,176},{56,1... | collective-permute-start | bytes 98312 | tf_op jit(solution)/shard_map/ppermute | solution.py:264
  118.9 2.0 %collective-permute-done.5 = bf16[16,1024]{1,0:T(8,128)(2,1)S(1)} collective-permute-done((bf16[16,1024]{1,0:T(8,128)(2,1)S(1)}, bf16[16,1024]{1,0:T(8,128)(2,1)S(1)}, u32[]{:S(2)}, u32[]{:S(2)}) %collective-permute-start.5) | collective-permute-done | bytes 32800 | tf_op jit(solution)/shard_map/ppermute | solution.py:264
  120.9 1.6 %collective-permute-done.4 = bf16[16,1024]{1,0:T(8,128)(2,1)S(1)} collective-permute-done((bf16[16,1024]{1,0:T(8,128)(2,1)S(1)}, bf16[16,1024]{1,0:T(8,128)(2,1)S(1)}, u32[]{:S(2)}, u32[]{:S(2)}) %collective-permute-start.4) | collective-permute-done | bytes 32800 | tf_op jit(solution)/shard_map/ppermute | solution.py:264
  122.4 0.1 fusion.3
  122.5 0.4 collective-permute-start.7
  122.9 1.9 %unpack_filter.1 = bf16[256,1024]{1,0:T(8,128)(2,1)} custom-call(bf16[32,1,2,32,128]{4,3,2,1,0:T(8,128)(2,1)} %all-to-all-done.2.in_ref), custom_call_target="tpu_custom_call" | custom-call | tf_op jit(solution)/shard_map/unpack_filter/pallas_call | solution.py:378
  124.8 0.5 collective-permute-done.7.other_ref
  125.3 1.5 %close.1 = (f32[3,3,1024]{2,1,0:T(4,128)}, bf16[256,1024]{1,0:T(8,128)(2,1)}, bf16[256,1024]{1,0:T(8,128)(2,1)}, bf16[256,1024]{1,0:T(8,128)(2,1)}) custom-call(f32[16,1024]{1,0:T(8,128)S(1)} %get-tuple-element.35.mine_ref, bf16[16,1024]{1,0:T(8,128)(2,1)S(1)} %collective-permute-done.7.other_ref, ...), custom_call_target="tpu_custom_call", output_to_operand_aliasing={{1}: (5, {}), {2}: (6, {}), {3}: (7, {})} | custom-call | tf_op jit(solution)/shard_map/close/pallas_call | solution.py:390
  (32 shorter events, 0.2 us)
Async XLA Ops:
  0.6 7.5 %copy-start.2 = (bf16[256,1024]{1,0:T(8,128)(2,1)S(1)}, bf16[256,1024]{1,0:T(8,128)(2,1)}, u32[]{:S(2)}) copy-start(bf16[256,1024]{1,0:T(8,128)(2,1)} %v_ref.7) | copy-start | bytes 1572868
  0.6 7.5 %copy-start.1 = (bf16[256,1024]{1,0:T(8,128)(2,1)S(1)}, bf16[256,1024]{1,0:T(8,128)(2,1)}, u32[]{:S(2)}) copy-start(bf16[256,1024]{1,0:T(8,128)(2,1)} %k_ref.7) | copy-start | bytes 1572868
  0.7 7.5 %copy-start = (bf16[256,1024]{1,0:T(8,128)(2,1)S(1)}, bf16[256,1024]{1,0:T(8,128)(2,1)}, u32[]{:S(2)}) copy-start(bf16[256,1024]{1,0:T(8,128)(2,1)} %q_ref.7) | copy-start | bytes 1572868
  0.7 7.5 %copy-start.4 = (f32[3,3,1024]{2,1,0:T(4,128)S(1)}, f32[3,3,1024]{2,1,0:T(4,128)}, u32[]{:S(2)}) copy-start(f32[3,3,1024]{2,1,0:T(4,128)} %w_ref.8) | copy-start | bytes 110596
  0.7 7.5 %copy-start.3 = (bf16[256,1024]{1,0:T(8,128)(2,1)S(1)}, bf16[256,1024]{1,0:T(8,128)(2,1)}, u32[]{:S(2)}) copy-start(bf16[256,1024]{1,0:T(8,128)(2,1)} %cot_ref.5) | copy-start | bytes 1572868
  2.2 5.9 %collective-permute-start = (bf16[16,1024]{1,0:T(8,128)(2,1)}, bf16[16,1024]{1,0:T(8,128)(2,1)S(1)}, u32[]{:S(2)}, u32[]{:S(2)}) collective-permute-start(bf16[16,1024]{1,0:T(8,128)(2,1)} %tails.1), channel_id=1, source_target_pairs={{0,8},{8,16},{16,24},{24,32},{32,40},{40,48},{48,56},{56,64},{64,7... | collective-permute-start | bytes 98312 | tf_op jit(solution)/shard_map/ppermute | solution.py:319
  6.8 1.0 copy-start.6
  9.3 51.5 %copy-start.7 = (bf16[256,256]{1,0:T(8,128)(2,1)S(1)}, bf16[256,256]{1,0:T(8,128)(2,1)}, u32[]{:S(2)}) copy-start(bf16[256,256]{1,0:T(8,128)(2,1)} %constant.64.clone.wi_ref) | copy-start | bytes 393220
  9.4 51.5 %copy-start.8 = (bf16[256,256]{1,0:T(8,128)(2,1)S(1)}, bf16[256,256]{1,0:T(8,128)(2,1)}, u32[]{:S(2)}) copy-start(bf16[256,256]{1,0:T(8,128)(2,1)} %constant.63.clone.w_ref) | copy-start | bytes 393220
  9.4 51.5 %copy-start.9 = (f32[2,64,128]{2,1,0:T(8,128)S(1)}, f32[2,64,128]{2,1,0:T(8,128)}, u32[]{:S(2)}) copy-start(f32[2,64,128]{2,1,0:T(8,128)} %constant.65.clone.turn_ref) | copy-start | bytes 196612
  9.4 51.4 %copy-start.10 = (bf16[128,64]{1,0:T(8,128)(2,1)S(1)}, bf16[128,64]{1,0:T(8,128)(2,1)}, u32[]{:S(2)}) copy-start(bf16[128,64]{1,0:T(8,128)(2,1)} %constant.61.clone.a_ref) | copy-start | bytes 49156
  9.4 51.4 %copy-start.11 = (bf16[64,128]{1,0:T(8,128)(2,1)S(1)}, bf16[64,128]{1,0:T(8,128)(2,1)}, u32[]{:S(2)}) copy-start(bf16[64,128]{1,0:T(8,128)(2,1)} %constant.62.clone.b_ref) | copy-start | bytes 49156
  65.8 31.9 %copy-start.5 = (bf16[32,1,2,32,128]{4,3,2,1,0:T(8,128)(2,1)}, bf16[32,1,2,32,128]{4,3,2,1,0:T(8,128)(2,1)S(1)}, u32[]{:S(2)}) copy-start(bf16[32,1,2,32,128]{4,3,2,1,0:T(8,128)(2,1)S(1)} %get-tuple-element.33) | copy-start | bytes 1572868
  97.6 25.3 %all-to-all-start.2 = ((bf16[32,1,2,32,128]{4,3,2,1,0:T(8,128)(2,1)}), bf16[32,1,2,32,128]{4,3,2,1,0:T(8,128)(2,1)}, u32[]{:S(2)}, u32[]{:S(2)}) async-start(bf16[32,1,2,32,128]{4,3,2,1,0:T(8,128)(2,1)} %copy-done.5), calls=%async_computation.2 | async-start | bytes 1048576 | tf_op jit(solution)/shard_map/all_to_all | solution.py:352
  105.0 5.9 %collective-permute-start.3 = (bf16[16,1024]{1,0:T(8,128)(2,1)S(1)}, bf16[16,1024]{1,0:T(8,128)(2,1)S(1)}, u32[]{:S(2)}, u32[]{:S(2)}) collective-permute-start(bf16[16,1024]{1,0:T(8,128)(2,1)S(1)} %sums.1), channel_id=1, source_target_pairs={{0,24},{8,16},{16,8},{24,0},{32,56},{40,48},{48,40},{56,32},{64,88... | collective-permute-start | bytes 98312 | tf_op jit(solution)/shard_map/ppermute | solution.py:264
  106.7 4.4 %collective-permute-start.2 = (bf16[16,1024]{1,0:T(8,128)(2,1)S(1)}, bf16[16,1024]{1,0:T(8,128)(2,1)S(1)}, u32[]{:S(2)}, u32[]{:S(2)}) collective-permute-start(bf16[16,1024]{1,0:T(8,128)(2,1)S(1)} %sums.1), channel_id=1, source_target_pairs={{0,16},{8,24},{16,0},{24,8},{32,48},{40,56},{48,32},{56,40},{64,80... | collective-permute-start | bytes 98312 | tf_op jit(solution)/shard_map/ppermute | solution.py:264
  106.9 4.3 %collective-permute-start.1 = (bf16[16,1024]{1,0:T(8,128)(2,1)S(1)}, bf16[16,1024]{1,0:T(8,128)(2,1)S(1)}, u32[]{:S(2)}, u32[]{:S(2)}) collective-permute-start(bf16[16,1024]{1,0:T(8,128)(2,1)S(1)} %sums.1), channel_id=1, source_target_pairs={{0,8},{8,0},{16,24},{24,16},{32,40},{40,32},{48,56},{56,48},{64,72... | collective-permute-start | bytes 98312 | tf_op jit(solution)/shard_map/ppermute | solution.py:264
  111.3 7.6 %collective-permute-start.6 = (bf16[16,1024]{1,0:T(8,128)(2,1)S(1)}, bf16[16,1024]{1,0:T(8,128)(2,1)S(1)}, u32[]{:S(2)}, u32[]{:S(2)}) collective-permute-start(bf16[16,1024]{1,0:T(8,128)(2,1)S(1)} %convert_element_type.36), channel_id=1, source_target_pairs={{0,192},{8,200},{16,208},{24,216},{32,224},{40,232},{48,240},{56,2... | collective-permute-start | bytes 98312 | tf_op jit(solution)/shard_map/ppermute | solution.py:264
  115.2 5.7 %collective-permute-start.5 = (bf16[16,1024]{1,0:T(8,128)(2,1)S(1)}, bf16[16,1024]{1,0:T(8,128)(2,1)S(1)}, u32[]{:S(2)}, u32[]{:S(2)}) collective-permute-start(bf16[16,1024]{1,0:T(8,128)(2,1)S(1)} %convert_element_type.36), channel_id=1, source_target_pairs={{0,64},{8,72},{16,80},{24,88},{32,96},{40,104},{48,112},{56,120},{... | collective-permute-start | bytes 98312 | tf_op jit(solution)/shard_map/ppermute | solution.py:264
  115.2 7.3 %collective-permute-start.4 = (bf16[16,1024]{1,0:T(8,128)(2,1)S(1)}, bf16[16,1024]{1,0:T(8,128)(2,1)S(1)}, u32[]{:S(2)}, u32[]{:S(2)}) collective-permute-start(bf16[16,1024]{1,0:T(8,128)(2,1)S(1)} %convert_element_type.36), channel_id=1, source_target_pairs={{0,128},{8,136},{16,144},{24,152},{32,160},{40,168},{48,176},{56,1... | collective-permute-start | bytes 98312 | tf_op jit(solution)/shard_map/ppermute | solution.py:264
  122.5 2.8 %collective-permute-start.7 = (bf16[16,1024]{1,0:T(8,128)(2,1)S(1)}, bf16[16,1024]{1,0:T(8,128)(2,1)S(1)}, u32[]{:S(2)}, u32[]{:S(2)}) collective-permute-start(bf16[16,1024]{1,0:T(8,128)(2,1)S(1)} %get-tuple-element.34), channel_id=1, source_target_pairs={{0,32},{8,40},{16,48},{24,56},{32,0},{40,8},{48,16},{56,24},{64,96... | collective-permute-start | bytes 98312 | tf_op jit(solution)/shard_map/ppermute | solution.py:279

commit v4 on v3

--- a/solution.py
+++ b/solution.py
@@ -63,8 +63,17 @@
     return jnp.concatenate(blocks, axis=0)
 
 
-def tails_kernel(q_ref, k_ref, v_ref, out_ref):
-    rows = [ref[...].astype(F32)[14:, :] for ref in (q_ref, k_ref, v_ref)]
+def tails_kernel(q_ref, k_ref, v_ref, out_ref, buf, sems):
+    refs = (q_ref, k_ref, v_ref)
+    copies = [
+        pltpu.make_async_copy(ref.at[pl.ds(ref.shape[0] - 16, 16), :], buf.at[i], sems.at[i])
+        for i, ref in enumerate(refs)
+    ]
+    for copy in copies:
+        copy.start()
+    for copy in copies:
+        copy.wait()
+    rows = [buf[i].astype(F32)[14:, :] for i in range(3)]
     fill = jnp.zeros((10, out_ref.shape[1]), F32)
     out_ref[...] = jnp.concatenate(rows + [fill], axis=0).astype(BF)
 
@@ -128,7 +137,7 @@
     inv_root, in_ref, a_ref, b_ref, w_ref, wi_ref, turn_ref, streams_ref, filters_ref
 ):
     sources, _, halves, own, _ = in_ref.shape
-    chans = 16
+    chans = 32
     for first in range(0, own, chans):
         at = slice(first, first + chans)
 
@@ -204,16 +213,13 @@
     for t, at in enumerate(lane_tiles(q_ref)):
         w, conv, grads = local_terms(refs, halo_ref, w_ref, in_ref, (qs, ks, vs), t, at)
         out_ref[:, at] = (filter_taps(qs, 8, rows, w, 0) * conv).astype(BF)
-        lasts = []
         for i, (grad, out) in enumerate(zip(grads, (gq_ref, gk_ref, gv_ref))):
             gs[pl.ds(0, rows), :] = grad
             back = w[i, 0:1, :] * grad
             for lag in range(1, 3):
                 back = back + w[i, lag : lag + 1, :] * gs[pl.ds(lag, rows), :]
             out[:, at] = back.astype(BF)
-            lasts.append(back[rows - 2 :])
-        lasts.append(jnp.zeros((2, LANES), F32))
-        last_ref[:, at] = jnp.concatenate(lasts, axis=0)
+            last_ref[i, :, at] = back[rows - 16 :]
 
 
 def unpack_kernel(in_ref, out_ref):
@@ -235,23 +241,37 @@
     gq_out,
     gk_out,
     gv_out,
+    short,
+    ends,
+    sems,
 ):
+    del gq_in, gk_in, gv_in
     mine = mine_ref[...]
     other = other_ref[...].astype(F32)
     total = (mine + other) * inv_root
     ahead = jnp.where(mine > 0.0, other, near_ref[...])
     row = lax.broadcasted_iota(jnp.int32, mine.shape, 0)
-    streams = ((gq_in, gq_out), (gk_in, gk_out), (gv_in, gv_out))
-    for i, (before, after) in enumerate(streams):
-        short_ref[i] = total[3 * i : 3 * i + 3]
+    copies = []
+    for i, out in enumerate((gq_out, gk_out, gv_out)):
+        short[i] = total[3 * i : 3 * i + 3]
         w1 = w_ref[i, 1:2, :]
         w2 = w_ref[i, 2:3, :]
         next0 = ahead[10 + 2 * i : 11 + 2 * i]
         next1 = ahead[11 + 2 * i : 12 + 2 * i]
-        end0 = last_ref[2 * i : 2 * i + 1] + w2 * next0
-        end1 = last_ref[2 * i + 1 : 2 * i + 2] + w1 * next0 + w2 * next1
-        fixed = jnp.where(row == 14, end0, jnp.where(row == 15, end1, before[...].astype(F32)))
-        after[...] = fixed.astype(BF)
+        last = last_ref[i]
+        end1 = last + w1 * next0 + w2 * next1
+        fixed = jnp.where(row == 14, last + w2 * next0, jnp.where(row == 15, end1, last))
+        ends[i] = fixed.astype(BF)
+        copies.append(
+            pltpu.make_async_copy(
+                ends.at[i], out.at[pl.ds(out.shape[0] - 16, 16), :], sems.at[i]
+            )
+        )
+        copies[-1].start()
+    copies.append(pltpu.make_async_copy(short, short_ref, sems.at[3]))
+    copies[-1].start()
+    for copy in copies:
+        copy.wait()
 
 
 def sum_over_ctx(terms, beside):
@@ -305,21 +325,20 @@
     block = lambda: pl.BlockSpec((rows, wide_step), lambda j: (0, j))
     row_block = lambda n: pl.BlockSpec((n, wide_step), lambda j: (0, j))
     w_block = lambda: pl.BlockSpec((3, taps, wide_step), lambda j: (0, 0, j))
-    end_block = lambda: pl.BlockSpec((16, channels), lambda j: (rows // 16 - 1, 0))
-    small = lambda n: pl.BlockSpec((n, channels), lambda j: (0, 0))
-
+
+    in_vmem = pl.BlockSpec(memory_space=pltpu.VMEM)
+    anywhere = pl.BlockSpec(memory_space=pl.ANY)
     tails = pl.pallas_call(
         tails_kernel,
-        grid=(1,),
-        in_specs=[end_block()] * 3,
-        out_specs=small(16),
+        in_specs=[anywhere] * 3,
+        out_specs=in_vmem,
         out_shape=jax.ShapeDtypeStruct((16, channels), BF),
+        scratch_shapes=[pltpu.VMEM((3, 16, channels), BF), pltpu.SemaphoreType.DMA((3,))],
         name="tails",
     )(query_in, key_in, value_in)
     halo = lax.ppermute(tails, "ctx", up)
 
     buf_shape = jax.ShapeDtypeStruct((ctx, 3, halves, own, LANES), BF)
-    in_vmem = pl.BlockSpec(memory_space=pltpu.VMEM)
     packed = pl.pallas_call(
         pack_filter_kernel,
         in_specs=[in_vmem],
@@ -368,8 +387,8 @@
         finish_kernel,
         grid=(steps,),
         in_specs=local_specs,
-        out_specs=[block()] * 4 + [row_block(8)],
-        out_shape=[wide] * 4 + [jax.ShapeDtypeStruct((8, channels), F32)],
+        out_specs=[block()] * 4 + [pl.BlockSpec((3, 16, wide_step), lambda j: (0, 0, j))],
+        out_shape=[wide] * 4 + [jax.ShapeDtypeStruct((3, 16, channels), F32)],
         scratch_shapes=[pltpu.VMEM((rows + 8, LANES), F32)] * 4,
         compiler_params=params(),
         name="finish",
@@ -386,13 +405,16 @@
     )(filters)
 
     mine, other, beyond, last = sum_over_ctx(sums, last)
-    all_taps = lambda: pl.BlockSpec((3, taps, channels), lambda j: (0, 0, 0))
     grad_short, grad_q, grad_k, grad_v = pl.pallas_call(
         functools.partial(close_kernel, inv_root),
-        grid=(1,),
-        in_specs=[small(16)] * 3 + [small(8), all_taps()] + [end_block()] * 3,
-        out_specs=[all_taps()] + [end_block()] * 3,
+        in_specs=[in_vmem] * 5 + [anywhere] * 3,
+        out_specs=[anywhere] * 4,
         out_shape=[jax.ShapeDtypeStruct((3, taps, channels), F32)] + [wide] * 3,
+        scratch_shapes=[
+            pltpu.VMEM((3, taps, channels), F32),
+            pltpu.VMEM((3, 16, channels), BF),
+            pltpu.SemaphoreType.DMA((4,)),
+        ],
         input_output_aliases={5: 1, 6: 2, 7: 3},
         compiler_params=params(),
         name="close",

time: 128 us -> 129 us (level)
  transfers between devices with their start and end apart: 9 -> 9, of which waited for: 5 -> 4; matrix products, arithmetic and copies ran while one was open for 0% -> 1% of each run, Pallas kernels for 6% -> 6%
where the time goes in v4:
time: 129 us; the launch traced here: 127 us
  blocking collectives  83.3 us (65%)
  starting transfers between devices  20.6 us (16%)
  Pallas kernels  16 us (12%)
  waiting for transfers between devices  3.35 us (3%)
  other arithmetic  1.33 us (1%)
    all_to_all x1, blocking collectives, on_device(): lax.all_to_all(packed, 'ctx', split_axis=0, concat_axis=0, tiled=True)  51.4 us
    all_to_all x1, blocking collectives, on_device(): lax.all_to_all(streams, 'ctx', split_axis=0, concat_axis=0, tiled=True)  31.9 us
    ppermute x6, starting transfers between devices, moved(): lax.ppermute(x.astype(BF), 'ctx', [(i, to(i)) for i in range(ctx)])  10.1 us
    all_to_all x1, starting transfers between devices, on_device(): lax.all_to_all(filters, 'ctx', split_axis=0, concat_axis=0, tiled=True)  5.41 us
    pallas_call x1, Pallas kernels, on_device(): pl.pallas_call(functools.partial(spectral_kernel, inv_root), in_specs=[in...  4.76 us
    ppermute x1, starting transfers between devices, on_device(): halo = lax.ppermute(tails, 'ctx', up)  4.59 us
    pallas_call x1, Pallas kernels, on_device(): pl.pallas_call(finish_kernel, grid=(steps,), in_specs=local_specs, out_sp...  3.67 us
    ppermute x6, waiting for transfers between devices, moved(): lax.ppermute(x.astype(BF), 'ctx', [(i, to(i)) for i in range(ctx)])  2.92 us
  transfers between devices with their start and end apart: 9, of which 4 were waited for; matrix products, arithmetic and copies ran while one was open for 1% of the time, Pallas kernels for 6%

profile of v4, /device:TPU:1, one launch (start us, length us, event | category | flops | bytes accessed | tf_op | source)
XLA Modules:
  0.0 126.7 jit_solution(13858288931109867421)
XLA Ops:
  0.7 1.6 %tails.1 = bf16[16,1024]{1,0:T(8,128)(2,1)} custom-call(bf16[256,1024]{1,0:T(8,128)(2,1)} %q_ref.7, bf16[256,1024]{1,0:T(8,128)(2,1)} %k_ref.7, bf16[256,1024]{1,0:T(8,128)(2,1)} %v_ref.7), custom_call_target="tpu_custom_call" | custom-call | tf_op jit(solution)/shard_map/tails/pallas_call | solution.py:331
  2.3 4.6 %collective-permute-start = (bf16[16,1024]{1,0:T(8,128)(2,1)}, bf16[16,1024]{1,0:T(8,128)(2,1)S(1)}, u32[]{:S(2)}, u32[]{:S(2)}) collective-permute-start(bf16[16,1024]{1,0:T(8,128)(2,1)} %tails.1), channel_id=1, source_target_pairs={{0,8},{8,16},{16,24},{24,32},{32,40},{40,48},{48,56},{56,64},{64,7... | collective-permute-start | bytes 98312 | tf_op jit(solution)/shard_map/ppermute | solution.py:339
  6.9 1.0 copy-done.6
  7.9 0.2 pack_filter.1.buf_ref
  8.2 1.2 pack_signals.1
  9.5 51.4 %all_to_all.15.in_ref = bf16[32,3,2,32,128]{4,3,2,1,0:T(8,128)(2,1)S(1)} all-to-all(bf16[32,3,2,32,128]{4,3,2,1,0:T(8,128)(2,1)S(1)} %pack_signals.1), channel_id=1, replica_groups=mesh['ctx'=32,'tp'=8] {'ctx'}, dimensions={0} | all-to-all | bytes 3145728 | tf_op jit(solution)/shard_map/all_to_all | solution.py:360
  60.9 4.8 %spectral.1 = (bf16[32,2,2,32,128]{4,3,2,1,0:T(8,128)(2,1)S(1)}, bf16[32,1,2,32,128]{4,3,2,1,0:T(8,128)(2,1)S(1)}) custom-call(bf16[32,3,2,32,128]{4,3,2,1,0:T(8,128)(2,1)S(1)} %all_to_all.15.in_ref, bf16[128,64]{1,0:T(8,128)(2,1)S(1)} %copy-done.10, bf16[64,128]{1,0:T(8,128)(2,1)S(1)} %copy-done.11, bf16[256,256]{1,0:T(8,128)(2,1)S(1)} %copy-done.8, ...), custom_call_target="tpu_custom_call" | custom-call | tf_op jit(solution)/shard_map/spectral/pallas_call | solution.py:362
  65.7 31.9 %all_to_all.16.in_ref = bf16[32,2,2,32,128]{4,3,2,1,0:T(8,128)(2,1)S(1)} all-to-all(bf16[32,2,2,32,128]{4,3,2,1,0:T(8,128)(2,1)S(1)} %get-tuple-element.20), channel_id=1, replica_groups=mesh['ctx'=32,'tp'=8] {'ctx'}, dimensions={0} | all-to-all | bytes 2097152 | tf_op jit(solution)/shard_map/all_to_all | solution.py:370
  97.6 5.4 %all-to-all-start.2 = ((bf16[32,1,2,32,128]{4,3,2,1,0:T(8,128)(2,1)}), bf16[32,1,2,32,128]{4,3,2,1,0:T(8,128)(2,1)}, u32[]{:S(2)}, u32[]{:S(2)}) async-start(bf16[32,1,2,32,128]{4,3,2,1,0:T(8,128)(2,1)} %copy-done.5), calls=%async_computation.2 | async-start | bytes 1048576 | tf_op jit(solution)/shard_map/all_to_all | solution.py:371
  103.0 2.0 %sums.1 = bf16[16,1024]{1,0:T(8,128)(2,1)S(1)} custom-call(bf16[256,1024]{1,0:T(8,128)(2,1)S(1)} %copy-done, bf16[256,1024]{1,0:T(8,128)(2,1)S(1)} %copy-done.1, bf16[256,1024]{1,0:T(8,128)(2,1)S(1)} %copy-done.2, bf16[256,1024]{1,0:T(8,128)(2,1)S(1)} %copy-done.3, bf16[16,1024]{1,0:T(8,128)(2,1)S(1)} %collective-permute-done.halo_ref, ...), custom_call_target="tpu_custom_call" | custom-call | tf_op jit(solution)/shard_map/sums/pallas_call | solution.py:377
  104.9 1.7 %collective-permute-start.3 = (bf16[16,1024]{1,0:T(8,128)(2,1)S(1)}, bf16[16,1024]{1,0:T(8,128)(2,1)S(1)}, u32[]{:S(2)}, u32[]{:S(2)}) collective-permute-start(bf16[16,1024]{1,0:T(8,128)(2,1)S(1)} %sums.1), channel_id=1, source_target_pairs={{0,24},{8,16},{16,8},{24,0},{32,56},{40,48},{48,40},{56,32},{64,88... | collective-permute-start | bytes 98312 | tf_op jit(solution)/shard_map/ppermute | solution.py:284
  106.7 0.1 collective-permute-start.2
  106.8 0.4 collective-permute-start.1
  107.2 0.5 iota_compare_fusion
  107.7 3.7 %finish.1 = (bf16[256,1024]{1,0:T(8,128)(2,1)}, bf16[256,1024]{1,0:T(8,128)(2,1)}, bf16[256,1024]{1,0:T(8,128)(2,1)}, bf16[256,1024]{1,0:T(8,128)(2,1)}, f32[3,16,1024]{2,1,0:T(8,128)S(1)}) custom-call(bf16[256,1024]{1,0:T(8,128)(2,1)S(1)} %copy-done, bf16[256,1024]{1,0:T(8,128)(2,1)S(1)} %copy-done.1, bf16[256,1024]{1,0:T(8,128)(2,1)S(1)} %copy-done.2, ...), custom_call_target="tpu_custom_call" | custom-call | tf_op jit(solution)/shard_map/finish/pallas_call | solution.py:386
  111.5 3.7 %collective-permute-start.6 = (bf16[16,1024]{1,0:T(8,128)(2,1)S(1)}, bf16[16,1024]{1,0:T(8,128)(2,1)S(1)}, u32[]{:S(2)}, u32[]{:S(2)}) collective-permute-start(bf16[16,1024]{1,0:T(8,128)(2,1)S(1)} %convert_element_type.36), channel_id=1, source_target_pairs={{0,192},{8,200},{16,208},{24,216},{32,224},{40,232},{48,240},{56,2... | collective-permute-start | bytes 98312 | tf_op jit(solution)/shard_map/ppermute | solution.py:284
  115.2 4.1 %collective-permute-start.4 = (bf16[16,1024]{1,0:T(8,128)(2,1)S(1)}, bf16[16,1024]{1,0:T(8,128)(2,1)S(1)}, u32[]{:S(2)}, u32[]{:S(2)}) collective-permute-start(bf16[16,1024]{1,0:T(8,128)(2,1)S(1)} %convert_element_type.36), channel_id=1, source_target_pairs={{0,128},{8,136},{16,144},{24,152},{32,160},{40,168},{48,176},{56,1... | collective-permute-start | bytes 98312 | tf_op jit(solution)/shard_map/ppermute | solution.py:284
  119.3 1.4 %collective-permute-done.5 = bf16[16,1024]{1,0:T(8,128)(2,1)S(1)} collective-permute-done((bf16[16,1024]{1,0:T(8,128)(2,1)S(1)}, bf16[16,1024]{1,0:T(8,128)(2,1)S(1)}, u32[]{:S(2)}, u32[]{:S(2)}) %collective-permute-start.5) | collective-permute-done | bytes 32800 | tf_op jit(solution)/shard_map/ppermute | solution.py:284
  120.7 1.5 %collective-permute-done.4 = bf16[16,1024]{1,0:T(8,128)(2,1)S(1)} collective-permute-done((bf16[16,1024]{1,0:T(8,128)(2,1)S(1)}, bf16[16,1024]{1,0:T(8,128)(2,1)S(1)}, u32[]{:S(2)}, u32[]{:S(2)}) %collective-permute-start.4) | collective-permute-done | bytes 32800 | tf_op jit(solution)/shard_map/ppermute | solution.py:284
  122.2 0.7 fusion.3
  123.0 0.5 collective-permute-start.7
  123.5 1.9 %unpack_filter.1 = bf16[256,1024]{1,0:T(8,128)(2,1)} custom-call(bf16[32,1,2,32,128]{4,3,2,1,0:T(8,128)(2,1)} %all-to-all-done.2.in_ref), custom_call_target="tpu_custom_call" | custom-call | tf_op jit(solution)/shard_map/unpack_filter/pallas_call | solution.py:397
  125.4 0.4 collective-permute-done.7.other_ref
  125.8 0.7 close.1
  (34 shorter events, 0.2 us)
Async XLA Ops:
  0.6 7.6 %copy-start.2 = (bf16[256,1024]{1,0:T(8,128)(2,1)S(1)}, bf16[256,1024]{1,0:T(8,128)(2,1)}, u32[]{:S(2)}) copy-start(bf16[256,1024]{1,0:T(8,128)(2,1)} %v_ref.7) | copy-start | bytes 1572868
  0.6 7.6 %copy-start.1 = (bf16[256,1024]{1,0:T(8,128)(2,1)S(1)}, bf16[256,1024]{1,0:T(8,128)(2,1)}, u32[]{:S(2)}) copy-start(bf16[256,1024]{1,0:T(8,128)(2,1)} %k_ref.7) | copy-start | bytes 1572868
  0.7 7.5 %copy-start = (bf16[256,1024]{1,0:T(8,128)(2,1)S(1)}, bf16[256,1024]{1,0:T(8,128)(2,1)}, u32[]{:S(2)}) copy-start(bf16[256,1024]{1,0:T(8,128)(2,1)} %q_ref.7) | copy-start | bytes 1572868
  0.7 7.5 %copy-start.4 = (f32[3,3,1024]{2,1,0:T(4,128)S(1)}, f32[3,3,1024]{2,1,0:T(4,128)}, u32[]{:S(2)}) copy-start(f32[3,3,1024]{2,1,0:T(4,128)} %w_ref.8) | copy-start | bytes 110596
  0.7 7.5 %copy-start.3 = (bf16[256,1024]{1,0:T(8,128)(2,1)S(1)}, bf16[256,1024]{1,0:T(8,128)(2,1)}, u32[]{:S(2)}) copy-start(bf16[256,1024]{1,0:T(8,128)(2,1)} %cot_ref.5) | copy-start | bytes 1572868
  2.3 5.9 %collective-permute-start = (bf16[16,1024]{1,0:T(8,128)(2,1)}, bf16[16,1024]{1,0:T(8,128)(2,1)S(1)}, u32[]{:S(2)}, u32[]{:S(2)}) collective-permute-start(bf16[16,1024]{1,0:T(8,128)(2,1)} %tails.1), channel_id=1, source_target_pairs={{0,8},{8,16},{16,24},{24,32},{32,40},{40,48},{48,56},{56,64},{64,7... | collective-permute-start | bytes 98312 | tf_op jit(solution)/shard_map/ppermute | solution.py:339
  6.9 1.0 copy-start.6
  9.4 51.5 %copy-start.7 = (bf16[256,256]{1,0:T(8,128)(2,1)S(1)}, bf16[256,256]{1,0:T(8,128)(2,1)}, u32[]{:S(2)}) copy-start(bf16[256,256]{1,0:T(8,128)(2,1)} %constant.64.clone.wi_ref) | copy-start | bytes 393220
  9.4 51.5 %copy-start.8 = (bf16[256,256]{1,0:T(8,128)(2,1)S(1)}, bf16[256,256]{1,0:T(8,128)(2,1)}, u32[]{:S(2)}) copy-start(bf16[256,256]{1,0:T(8,128)(2,1)} %constant.63.clone.w_ref) | copy-start | bytes 393220
  9.4 51.5 %copy-start.9 = (f32[2,64,128]{2,1,0:T(8,128)S(1)}, f32[2,64,128]{2,1,0:T(8,128)}, u32[]{:S(2)}) copy-start(f32[2,64,128]{2,1,0:T(8,128)} %constant.65.clone.turn_ref) | copy-start | bytes 196612
  9.4 51.4 %copy-start.10 = (bf16[128,64]{1,0:T(8,128)(2,1)S(1)}, bf16[128,64]{1,0:T(8,128)(2,1)}, u32[]{:S(2)}) copy-start(bf16[128,64]{1,0:T(8,128)(2,1)} %constant.61.clone.a_ref) | copy-start | bytes 49156
  9.4 51.4 %copy-start.11 = (bf16[64,128]{1,0:T(8,128)(2,1)S(1)}, bf16[64,128]{1,0:T(8,128)(2,1)}, u32[]{:S(2)}) copy-start(bf16[64,128]{1,0:T(8,128)(2,1)} %constant.62.clone.b_ref) | copy-start | bytes 49156
  65.7 31.9 %copy-start.5 = (bf16[32,1,2,32,128]{4,3,2,1,0:T(8,128)(2,1)}, bf16[32,1,2,32,128]{4,3,2,1,0:T(8,128)(2,1)S(1)}, u32[]{:S(2)}) copy-start(bf16[32,1,2,32,128]{4,3,2,1,0:T(8,128)(2,1)S(1)} %get-tuple-element.33) | copy-start | bytes 1572868
  97.6 25.9 %all-to-all-start.2 = ((bf16[32,1,2,32,128]{4,3,2,1,0:T(8,128)(2,1)}), bf16[32,1,2,32,128]{4,3,2,1,0:T(8,128)(2,1)}, u32[]{:S(2)}, u32[]{:S(2)}) async-start(bf16[32,1,2,32,128]{4,3,2,1,0:T(8,128)(2,1)} %copy-done.5), calls=%async_computation.2 | async-start | bytes 1048576 | tf_op jit(solution)/shard_map/all_to_all | solution.py:371
  104.9 6.4 %collective-permute-start.3 = (bf16[16,1024]{1,0:T(8,128)(2,1)S(1)}, bf16[16,1024]{1,0:T(8,128)(2,1)S(1)}, u32[]{:S(2)}, u32[]{:S(2)}) collective-permute-start(bf16[16,1024]{1,0:T(8,128)(2,1)S(1)} %sums.1), channel_id=1, source_target_pairs={{0,24},{8,16},{16,8},{24,0},{32,56},{40,48},{48,40},{56,32},{64,88... | collective-permute-start | bytes 98312 | tf_op jit(solution)/shard_map/ppermute | solution.py:284
  106.7 4.7 %collective-permute-start.2 = (bf16[16,1024]{1,0:T(8,128)(2,1)S(1)}, bf16[16,1024]{1,0:T(8,128)(2,1)S(1)}, u32[]{:S(2)}, u32[]{:S(2)}) collective-permute-start(bf16[16,1024]{1,0:T(8,128)(2,1)S(1)} %sums.1), channel_id=1, source_target_pairs={{0,16},{8,24},{16,0},{24,8},{32,48},{40,56},{48,32},{56,40},{64,80... | collective-permute-start | bytes 98312 | tf_op jit(solution)/shard_map/ppermute | solution.py:284
  106.8 4.6 %collective-permute-start.1 = (bf16[16,1024]{1,0:T(8,128)(2,1)S(1)}, bf16[16,1024]{1,0:T(8,128)(2,1)S(1)}, u32[]{:S(2)}, u32[]{:S(2)}) collective-permute-start(bf16[16,1024]{1,0:T(8,128)(2,1)S(1)} %sums.1), channel_id=1, source_target_pairs={{0,8},{8,0},{16,24},{24,16},{32,40},{40,32},{48,56},{56,48},{64,72... | collective-permute-start | bytes 98312 | tf_op jit(solution)/shard_map/ppermute | solution.py:284
  107.7 3.7 %copy-start.12 = (pred[16]{0:T(512)(128)(4,1)S(1)}, pred[16]{0:T(512)(128)(4,1)}, u32[]{:S(2)}) copy-start(pred[16]{0:T(512)(128)(4,1)} %iota_compare_fusion) | copy-start | bytes 52
  111.5 7.9 %collective-permute-start.6 = (bf16[16,1024]{1,0:T(8,128)(2,1)S(1)}, bf16[16,1024]{1,0:T(8,128)(2,1)S(1)}, u32[]{:S(2)}, u32[]{:S(2)}) collective-permute-start(bf16[16,1024]{1,0:T(8,128)(2,1)S(1)} %convert_element_type.36), channel_id=1, source_target_pairs={{0,192},{8,200},{16,208},{24,216},{32,224},{40,232},{48,240},{56,2... | collective-permute-start | bytes 98312 | tf_op jit(solution)/shard_map/ppermute | solution.py:284
  115.2 5.5 %collective-permute-start.5 = (bf16[16,1024]{1,0:T(8,128)(2,1)S(1)}, bf16[16,1024]{1,0:T(8,128)(2,1)S(1)}, u32[]{:S(2)}, u32[]{:S(2)}) collective-permute-start(bf16[16,1024]{1,0:T(8,128)(2,1)S(1)} %convert_element_type.36), channel_id=1, source_target_pairs={{0,64},{8,72},{16,80},{24,88},{32,96},{40,104},{48,112},{56,120},{... | collective-permute-start | bytes 98312 | tf_op jit(solution)/shard_map/ppermute | solution.py:284
  115.2 7.0 %collective-permute-start.4 = (bf16[16,1024]{1,0:T(8,128)(2,1)S(1)}, bf16[16,1024]{1,0:T(8,128)(2,1)S(1)}, u32[]{:S(2)}, u32[]{:S(2)}) collective-permute-start(bf16[16,1024]{1,0:T(8,128)(2,1)S(1)} %convert_element_type.36), channel_id=1, source_target_pairs={{0,128},{8,136},{16,144},{24,152},{32,160},{40,168},{48,176},{56,1... | collective-permute-start | bytes 98312 | tf_op jit(solution)/shard_map/ppermute | solution.py:284
  123.0 2.8 %collective-permute-start.7 = (bf16[16,1024]{1,0:T(8,128)(2,1)S(1)}, bf16[16,1024]{1,0:T(8,128)(2,1)S(1)}, u32[]{:S(2)}, u32[]{:S(2)}) collective-permute-start(bf16[16,1024]{1,0:T(8,128)(2,1)S(1)} %get-tuple-element.34), channel_id=1, source_target_pairs={{0,32},{8,40},{16,48},{24,56},{32,0},{40,8},{48,16},{56,24},{64,96... | collective-permute-start | bytes 98312 | tf_op jit(solution)/shard_map/ppermute | solution.py:299

commit v5 on v3

--- a/solution.py
+++ b/solution.py
@@ -128,7 +128,7 @@
     inv_root, in_ref, a_ref, b_ref, w_ref, wi_ref, turn_ref, streams_ref, filters_ref
 ):
     sources, _, halves, own, _ = in_ref.shape
-    chans = 16
+    chans = 32
     for first in range(0, own, chans):
         at = slice(first, first + chans)
 

time: 128 us -> 128 us (level)
  no operation moved by 1% of the time
where the time goes in v5:
time: 128 us; the launch traced here: 127 us
  blocking collectives  83.3 us (65%)
  starting transfers between devices  20.2 us (16%)
  Pallas kernels  16.7 us (13%)
  waiting for transfers between devices  4.36 us (3%)
    all_to_all x1, blocking collectives, on_device(): lax.all_to_all(packed, 'ctx', split_axis=0, concat_axis=0, tiled=True)  51.4 us
    all_to_all x1, blocking collectives, on_device(): lax.all_to_all(streams, 'ctx', split_axis=0, concat_axis=0, tiled=True)  31.9 us
    ppermute x6, starting transfers between devices, moved(): lax.ppermute(x.astype(BF), 'ctx', [(i, to(i)) for i in range(ctx)])  9.85 us
    all_to_all x1, starting transfers between devices, on_device(): lax.all_to_all(filters, 'ctx', split_axis=0, concat_axis=0, tiled=True)  5.41 us
    pallas_call x1, Pallas kernels, on_device(): pl.pallas_call(functools.partial(spectral_kernel, inv_root), in_specs=[in...  4.76 us
    ppermute x1, starting transfers between devices, on_device(): halo = lax.ppermute(tails, 'ctx', up)  4.58 us
    ppermute x6, waiting for transfers between devices, moved(): lax.ppermute(x.astype(BF), 'ctx', [(i, to(i)) for i in range(ctx)])  3.78 us
    pallas_call x1, Pallas kernels, on_device(): pl.pallas_call(finish_kernel, grid=(steps,), in_specs=local_specs, out_sp...  3.69 us
  transfers between devices with their start and end apart: 9, of which 5 were waited for; matrix products, arithmetic and copies ran while one was open for 0% of the time, Pallas kernels for 6%

profile of v5, /device:TPU:1, one launch (start us, length us, event | category | flops | bytes accessed | tf_op | source)
XLA Modules:
  0.0 126.7 jit_solution(14516439502777963218)
XLA Ops:
  0.7 1.6 %tails.1 = bf16[16,1024]{1,0:T(8,128)(2,1)} custom-call(bf16[256,1024]{1,0:T(8,128)(2,1)} %q_ref.7, bf16[256,1024]{1,0:T(8,128)(2,1)} %k_ref.7, bf16[256,1024]{1,0:T(8,128)(2,1)} %v_ref.7), custom_call_target="tpu_custom_call" | custom-call | tf_op jit(solution)/shard_map/tails/pallas_call | solution.py:311
  2.2 4.6 %collective-permute-start = (bf16[16,1024]{1,0:T(8,128)(2,1)}, bf16[16,1024]{1,0:T(8,128)(2,1)S(1)}, u32[]{:S(2)}, u32[]{:S(2)}) collective-permute-start(bf16[16,1024]{1,0:T(8,128)(2,1)} %tails.1), channel_id=1, source_target_pairs={{0,8},{8,16},{16,24},{24,32},{32,40},{40,48},{48,56},{56,64},{64,7... | collective-permute-start | bytes 98312 | tf_op jit(solution)/shard_map/ppermute | solution.py:319
  6.8 1.0 copy-done.6
  7.9 0.2 pack_filter.1.buf_ref
  8.2 1.2 pack_signals.1
  9.4 51.4 %all_to_all.15.in_ref = bf16[32,3,2,32,128]{4,3,2,1,0:T(8,128)(2,1)S(1)} all-to-all(bf16[32,3,2,32,128]{4,3,2,1,0:T(8,128)(2,1)S(1)} %pack_signals.1), channel_id=1, replica_groups=mesh['ctx'=32,'tp'=8] {'ctx'}, dimensions={0} | all-to-all | bytes 3145728 | tf_op jit(solution)/shard_map/all_to_all | solution.py:341
  60.8 4.8 %spectral.1 = (bf16[32,2,2,32,128]{4,3,2,1,0:T(8,128)(2,1)S(1)}, bf16[32,1,2,32,128]{4,3,2,1,0:T(8,128)(2,1)S(1)}) custom-call(bf16[32,3,2,32,128]{4,3,2,1,0:T(8,128)(2,1)S(1)} %all_to_all.15.in_ref, bf16[128,64]{1,0:T(8,128)(2,1)S(1)} %copy-done.10, bf16[64,128]{1,0:T(8,128)(2,1)S(1)} %copy-done.11, bf16[256,256]{1,0:T(8,128)(2,1)S(1)} %copy-done.8, ...), custom_call_target="tpu_custom_call" | custom-call | tf_op jit(solution)/shard_map/spectral/pallas_call | solution.py:343
  65.6 31.9 %all_to_all.16.in_ref = bf16[32,2,2,32,128]{4,3,2,1,0:T(8,128)(2,1)S(1)} all-to-all(bf16[32,2,2,32,128]{4,3,2,1,0:T(8,128)(2,1)S(1)} %get-tuple-element.20), channel_id=1, replica_groups=mesh['ctx'=32,'tp'=8] {'ctx'}, dimensions={0} | all-to-all | bytes 2097152 | tf_op jit(solution)/shard_map/all_to_all | solution.py:351
  97.5 5.4 %all-to-all-start.2 = ((bf16[32,1,2,32,128]{4,3,2,1,0:T(8,128)(2,1)}), bf16[32,1,2,32,128]{4,3,2,1,0:T(8,128)(2,1)}, u32[]{:S(2)}, u32[]{:S(2)}) async-start(bf16[32,1,2,32,128]{4,3,2,1,0:T(8,128)(2,1)} %copy-done.5), calls=%async_computation.2 | async-start | bytes 1048576 | tf_op jit(solution)/shard_map/all_to_all | solution.py:352
  102.9 2.0 %sums.1 = bf16[16,1024]{1,0:T(8,128)(2,1)S(1)} custom-call(bf16[256,1024]{1,0:T(8,128)(2,1)S(1)} %copy-done, bf16[256,1024]{1,0:T(8,128)(2,1)S(1)} %copy-done.1, bf16[256,1024]{1,0:T(8,128)(2,1)S(1)} %copy-done.2, bf16[256,1024]{1,0:T(8,128)(2,1)S(1)} %copy-done.3, bf16[16,1024]{1,0:T(8,128)(2,1)S(1)} %collective-permute-done.halo_ref, ...), custom_call_target="tpu_custom_call" | custom-call | tf_op jit(solution)/shard_map/sums/pallas_call | solution.py:358
  104.9 1.7 %collective-permute-start.3 = (bf16[16,1024]{1,0:T(8,128)(2,1)S(1)}, bf16[16,1024]{1,0:T(8,128)(2,1)S(1)}, u32[]{:S(2)}, u32[]{:S(2)}) collective-permute-start(bf16[16,1024]{1,0:T(8,128)(2,1)S(1)} %sums.1), channel_id=1, source_target_pairs={{0,24},{8,16},{16,8},{24,0},{32,56},{40,48},{48,40},{56,32},{64,88... | collective-permute-start | bytes 98312 | tf_op jit(solution)/shard_map/ppermute | solution.py:264
  106.6 0.1 collective-permute-start.2
  106.8 0.4 collective-permute-start.1
  107.1 3.7 %finish.1 = (bf16[256,1024]{1,0:T(8,128)(2,1)}, bf16[256,1024]{1,0:T(8,128)(2,1)}, bf16[256,1024]{1,0:T(8,128)(2,1)}, bf16[256,1024]{1,0:T(8,128)(2,1)}, f32[8,1024]{1,0:T(8,128)S(1)}) custom-call(bf16[256,1024]{1,0:T(8,128)(2,1)S(1)} %copy-done, bf16[256,1024]{1,0:T(8,128)(2,1)S(1)} %copy-done.1, bf16[256,1024]{1,0:T(8,128)(2,1)S(1)} %copy-done.2, ...), custom_call_target="tpu_custom_call" | custom-call | tf_op jit(solution)/shard_map/finish/pallas_call | solution.py:367
  110.8 0.2 collective-permute-done.2
  111.1 3.9 %collective-permute-start.6 = (bf16[16,1024]{1,0:T(8,128)(2,1)S(1)}, bf16[16,1024]{1,0:T(8,128)(2,1)S(1)}, u32[]{:S(2)}, u32[]{:S(2)}) collective-permute-start(bf16[16,1024]{1,0:T(8,128)(2,1)S(1)} %convert_element_type.36), channel_id=1, source_target_pairs={{0,192},{8,200},{16,208},{24,216},{32,224},{40,232},{48,240},{56,2... | collective-permute-start | bytes 98312 | tf_op jit(solution)/shard_map/ppermute | solution.py:264
  115.0 3.7 %collective-permute-start.4 = (bf16[16,1024]{1,0:T(8,128)(2,1)S(1)}, bf16[16,1024]{1,0:T(8,128)(2,1)S(1)}, u32[]{:S(2)}, u32[]{:S(2)}) collective-permute-start(bf16[16,1024]{1,0:T(8,128)(2,1)S(1)} %convert_element_type.36), channel_id=1, source_target_pairs={{0,128},{8,136},{16,144},{24,152},{32,160},{40,168},{48,176},{56,1... | collective-permute-start | bytes 98312 | tf_op jit(solution)/shard_map/ppermute | solution.py:264
  118.8 2.0 %collective-permute-done.5 = bf16[16,1024]{1,0:T(8,128)(2,1)S(1)} collective-permute-done((bf16[16,1024]{1,0:T(8,128)(2,1)S(1)}, bf16[16,1024]{1,0:T(8,128)(2,1)S(1)}, u32[]{:S(2)}, u32[]{:S(2)}) %collective-permute-start.5) | collective-permute-done | bytes 32800 | tf_op jit(solution)/shard_map/ppermute | solution.py:264
  120.7 1.6 %collective-permute-done.4 = bf16[16,1024]{1,0:T(8,128)(2,1)S(1)} collective-permute-done((bf16[16,1024]{1,0:T(8,128)(2,1)S(1)}, bf16[16,1024]{1,0:T(8,128)(2,1)S(1)}, u32[]{:S(2)}, u32[]{:S(2)}) %collective-permute-start.4) | collective-permute-done | bytes 32800 | tf_op jit(solution)/shard_map/ppermute | solution.py:264
  122.3 0.1 fusion.3
  122.4 0.4 collective-permute-start.7
  122.8 1.9 %unpack_filter.1 = bf16[256,1024]{1,0:T(8,128)(2,1)} custom-call(bf16[32,1,2,32,128]{4,3,2,1,0:T(8,128)(2,1)} %all-to-all-done.2.in_ref), custom_call_target="tpu_custom_call" | custom-call | tf_op jit(solution)/shard_map/unpack_filter/pallas_call | solution.py:378
  124.7 0.5 collective-permute-done.7.other_ref
  125.2 1.5 %close.1 = (f32[3,3,1024]{2,1,0:T(4,128)}, bf16[256,1024]{1,0:T(8,128)(2,1)}, bf16[256,1024]{1,0:T(8,128)(2,1)}, bf16[256,1024]{1,0:T(8,128)(2,1)}) custom-call(f32[16,1024]{1,0:T(8,128)S(1)} %get-tuple-element.35.mine_ref, bf16[16,1024]{1,0:T(8,128)(2,1)S(1)} %collective-permute-done.7.other_ref, ...), custom_call_target="tpu_custom_call", output_to_operand_aliasing={{1}: (5, {}), {2}: (6, {}), {3}: (7, {})} | custom-call | tf_op jit(solution)/shard_map/close/pallas_call | solution.py:390
  (32 shorter events, 0.2 us)
Async XLA Ops:
  0.6 7.5 %copy-start.2 = (bf16[256,1024]{1,0:T(8,128)(2,1)S(1)}, bf16[256,1024]{1,0:T(8,128)(2,1)}, u32[]{:S(2)}) copy-start(bf16[256,1024]{1,0:T(8,128)(2,1)} %v_ref.7) | copy-start | bytes 1572868
  0.6 7.5 %copy-start.1 = (bf16[256,1024]{1,0:T(8,128)(2,1)S(1)}, bf16[256,1024]{1,0:T(8,128)(2,1)}, u32[]{:S(2)}) copy-start(bf16[256,1024]{1,0:T(8,128)(2,1)} %k_ref.7) | copy-start | bytes 1572868
  0.7 7.5 %copy-start = (bf16[256,1024]{1,0:T(8,128)(2,1)S(1)}, bf16[256,1024]{1,0:T(8,128)(2,1)}, u32[]{:S(2)}) copy-start(bf16[256,1024]{1,0:T(8,128)(2,1)} %q_ref.7) | copy-start | bytes 1572868
  0.7 7.5 %copy-start.4 = (f32[3,3,1024]{2,1,0:T(4,128)S(1)}, f32[3,3,1024]{2,1,0:T(4,128)}, u32[]{:S(2)}) copy-start(f32[3,3,1024]{2,1,0:T(4,128)} %w_ref.8) | copy-start | bytes 110596
  0.7 7.5 %copy-start.3 = (bf16[256,1024]{1,0:T(8,128)(2,1)S(1)}, bf16[256,1024]{1,0:T(8,128)(2,1)}, u32[]{:S(2)}) copy-start(bf16[256,1024]{1,0:T(8,128)(2,1)} %cot_ref.5) | copy-start | bytes 1572868
  2.2 5.9 %collective-permute-start = (bf16[16,1024]{1,0:T(8,128)(2,1)}, bf16[16,1024]{1,0:T(8,128)(2,1)S(1)}, u32[]{:S(2)}, u32[]{:S(2)}) collective-permute-start(bf16[16,1024]{1,0:T(8,128)(2,1)} %tails.1), channel_id=1, source_target_pairs={{0,8},{8,16},{16,24},{24,32},{32,40},{40,48},{48,56},{56,64},{64,7... | collective-permute-start | bytes 98312 | tf_op jit(solution)/shard_map/ppermute | solution.py:319
  6.8 1.0 copy-start.6
  9.3 51.5 %copy-start.7 = (bf16[256,256]{1,0:T(8,128)(2,1)S(1)}, bf16[256,256]{1,0:T(8,128)(2,1)}, u32[]{:S(2)}) copy-start(bf16[256,256]{1,0:T(8,128)(2,1)} %constant.64.clone.wi_ref) | copy-start | bytes 393220
  9.4 51.5 %copy-start.8 = (bf16[256,256]{1,0:T(8,128)(2,1)S(1)}, bf16[256,256]{1,0:T(8,128)(2,1)}, u32[]{:S(2)}) copy-start(bf16[256,256]{1,0:T(8,128)(2,1)} %constant.63.clone.w_ref) | copy-start | bytes 393220
  9.4 51.5 %copy-start.9 = (f32[2,64,128]{2,1,0:T(8,128)S(1)}, f32[2,64,128]{2,1,0:T(8,128)}, u32[]{:S(2)}) copy-start(f32[2,64,128]{2,1,0:T(8,128)} %constant.65.clone.turn_ref) | copy-start | bytes 196612
  9.4 51.4 %copy-start.10 = (bf16[128,64]{1,0:T(8,128)(2,1)S(1)}, bf16[128,64]{1,0:T(8,128)(2,1)}, u32[]{:S(2)}) copy-start(bf16[128,64]{1,0:T(8,128)(2,1)} %constant.61.clone.a_ref) | copy-start | bytes 49156
  9.4 51.4 %copy-start.11 = (bf16[64,128]{1,0:T(8,128)(2,1)S(1)}, bf16[64,128]{1,0:T(8,128)(2,1)}, u32[]{:S(2)}) copy-start(bf16[64,128]{1,0:T(8,128)(2,1)} %constant.62.clone.b_ref) | copy-start | bytes 49156
  65.6 31.9 %copy-start.5 = (bf16[32,1,2,32,128]{4,3,2,1,0:T(8,128)(2,1)}, bf16[32,1,2,32,128]{4,3,2,1,0:T(8,128)(2,1)S(1)}, u32[]{:S(2)}) copy-start(bf16[32,1,2,32,128]{4,3,2,1,0:T(8,128)(2,1)S(1)} %get-tuple-element.33) | copy-start | bytes 1572868
  97.5 25.3 %all-to-all-start.2 = ((bf16[32,1,2,32,128]{4,3,2,1,0:T(8,128)(2,1)}), bf16[32,1,2,32,128]{4,3,2,1,0:T(8,128)(2,1)}, u32[]{:S(2)}, u32[]{:S(2)}) async-start(bf16[32,1,2,32,128]{4,3,2,1,0:T(8,128)(2,1)} %copy-done.5), calls=%async_computation.2 | async-start | bytes 1048576 | tf_op jit(solution)/shard_map/all_to_all | solution.py:352
  104.9 5.9 %collective-permute-start.3 = (bf16[16,1024]{1,0:T(8,128)(2,1)S(1)}, bf16[16,1024]{1,0:T(8,128)(2,1)S(1)}, u32[]{:S(2)}, u32[]{:S(2)}) collective-permute-start(bf16[16,1024]{1,0:T(8,128)(2,1)S(1)} %sums.1), channel_id=1, source_target_pairs={{0,24},{8,16},{16,8},{24,0},{32,56},{40,48},{48,40},{56,32},{64,88... | collective-permute-start | bytes 98312 | tf_op jit(solution)/shard_map/ppermute | solution.py:264
  106.6 4.4 %collective-permute-start.2 = (bf16[16,1024]{1,0:T(8,128)(2,1)S(1)}, bf16[16,1024]{1,0:T(8,128)(2,1)S(1)}, u32[]{:S(2)}, u32[]{:S(2)}) collective-permute-start(bf16[16,1024]{1,0:T(8,128)(2,1)S(1)} %sums.1), channel_id=1, source_target_pairs={{0,16},{8,24},{16,0},{24,8},{32,48},{40,56},{48,32},{56,40},{64,80... | collective-permute-start | bytes 98312 | tf_op jit(solution)/shard_map/ppermute | solution.py:264
  106.8 4.3 %collective-permute-start.1 = (bf16[16,1024]{1,0:T(8,128)(2,1)S(1)}, bf16[16,1024]{1,0:T(8,128)(2,1)S(1)}, u32[]{:S(2)}, u32[]{:S(2)}) collective-permute-start(bf16[16,1024]{1,0:T(8,128)(2,1)S(1)} %sums.1), channel_id=1, source_target_pairs={{0,8},{8,0},{16,24},{24,16},{32,40},{40,32},{48,56},{56,48},{64,72... | collective-permute-start | bytes 98312 | tf_op jit(solution)/shard_map/ppermute | solution.py:264
  111.1 7.6 %collective-permute-start.6 = (bf16[16,1024]{1,0:T(8,128)(2,1)S(1)}, bf16[16,1024]{1,0:T(8,128)(2,1)S(1)}, u32[]{:S(2)}, u32[]{:S(2)}) collective-permute-start(bf16[16,1024]{1,0:T(8,128)(2,1)S(1)} %convert_element_type.36), channel_id=1, source_target_pairs={{0,192},{8,200},{16,208},{24,216},{32,224},{40,232},{48,240},{56,2... | collective-permute-start | bytes 98312 | tf_op jit(solution)/shard_map/ppermute | solution.py:264
  115.0 5.7 %collective-permute-start.5 = (bf16[16,1024]{1,0:T(8,128)(2,1)S(1)}, bf16[16,1024]{1,0:T(8,128)(2,1)S(1)}, u32[]{:S(2)}, u32[]{:S(2)}) collective-permute-start(bf16[16,1024]{1,0:T(8,128)(2,1)S(1)} %convert_element_type.36), channel_id=1, source_target_pairs={{0,64},{8,72},{16,80},{24,88},{32,96},{40,104},{48,112},{56,120},{... | collective-permute-start | bytes 98312 | tf_op jit(solution)/shard_map/ppermute | solution.py:264
  115.0 7.3 %collective-permute-start.4 = (bf16[16,1024]{1,0:T(8,128)(2,1)S(1)}, bf16[16,1024]{1,0:T(8,128)(2,1)S(1)}, u32[]{:S(2)}, u32[]{:S(2)}) collective-permute-start(bf16[16,1024]{1,0:T(8,128)(2,1)S(1)} %convert_element_type.36), channel_id=1, source_target_pairs={{0,128},{8,136},{16,144},{24,152},{32,160},{40,168},{48,176},{56,1... | collective-permute-start | bytes 98312 | tf_op jit(solution)/shard_map/ppermute | solution.py:264
  122.4 2.8 %collective-permute-start.7 = (bf16[16,1024]{1,0:T(8,128)(2,1)S(1)}, bf16[16,1024]{1,0:T(8,128)(2,1)S(1)}, u32[]{:S(2)}, u32[]{:S(2)}) collective-permute-start(bf16[16,1024]{1,0:T(8,128)(2,1)S(1)} %get-tuple-element.34), channel_id=1, source_target_pairs={{0,32},{8,40},{16,48},{24,56},{32,0},{40,8},{48,16},{56,24},{64,96... | collective-permute-start | bytes 98312 | tf_op jit(solution)/shard_map/ppermute | solution.py:279

commit v6 on v4

--- a/solution.py
+++ b/solution.py
@@ -63,17 +63,8 @@
     return jnp.concatenate(blocks, axis=0)
 
 
-def tails_kernel(q_ref, k_ref, v_ref, out_ref, buf, sems):
-    refs = (q_ref, k_ref, v_ref)
-    copies = [
-        pltpu.make_async_copy(ref.at[pl.ds(ref.shape[0] - 16, 16), :], buf.at[i], sems.at[i])
-        for i, ref in enumerate(refs)
-    ]
-    for copy in copies:
-        copy.start()
-    for copy in copies:
-        copy.wait()
-    rows = [buf[i].astype(F32)[14:, :] for i in range(3)]
+def tails_kernel(q_ref, k_ref, v_ref, out_ref):
+    rows = [ref[...].astype(F32)[14:, :] for ref in (q_ref, k_ref, v_ref)]
     fill = jnp.zeros((10, out_ref.shape[1]), F32)
     out_ref[...] = jnp.concatenate(rows + [fill], axis=0).astype(BF)
 
@@ -330,10 +321,10 @@
     anywhere = pl.BlockSpec(memory_space=pl.ANY)
     tails = pl.pallas_call(
         tails_kernel,
-        in_specs=[anywhere] * 3,
-        out_specs=in_vmem,
+        grid=(1,),
+        in_specs=[pl.BlockSpec((16, channels), lambda j: (rows // 16 - 1, 0))] * 3,
+        out_specs=pl.BlockSpec((16, channels), lambda j: (0, 0)),
         out_shape=jax.ShapeDtypeStruct((16, channels), BF),
-        scratch_shapes=[pltpu.VMEM((3, 16, channels), BF), pltpu.SemaphoreType.DMA((3,))],
         name="tails",
     )(query_in, key_in, value_in)
     halo = lax.ppermute(tails, "ctx", up)

time: 129 us -> 128 us (level)
  no operation moved by 1% of the time
where the time goes in v6:
time: 128 us; the launch traced here: 127 us
  blocking collectives  83.3 us (65%)
  starting transfers between devices  20.6 us (16%)
  Pallas kernels  16 us (12%)
  waiting for transfers between devices  3.35 us (3%)
  other arithmetic  1.33 us (1%)
    all_to_all x1, blocking collectives, on_device(): lax.all_to_all(packed, 'ctx', split_axis=0, concat_axis=0, tiled=True)  51.4 us
    all_to_all x1, blocking collectives, on_device(): lax.all_to_all(streams, 'ctx', split_axis=0, concat_axis=0, tiled=True)  31.9 us
    ppermute x6, starting transfers between devices, moved(): lax.ppermute(x.astype(BF), 'ctx', [(i, to(i)) for i in range(ctx)])  10.1 us
    all_to_all x1, starting transfers between devices, on_device(): lax.all_to_all(filters, 'ctx', split_axis=0, concat_axis=0, tiled=True)  5.41 us
    pallas_call x1, Pallas kernels, on_device(): pl.pallas_call(functools.partial(spectral_kernel, inv_root), in_specs=[in...  4.76 us
    ppermute x1, starting transfers between devices, on_device(): halo = lax.ppermute(tails, 'ctx', up)  4.58 us
    pallas_call x1, Pallas kernels, on_device(): pl.pallas_call(finish_kernel, grid=(steps,), in_specs=local_specs, out_sp...  3.67 us
    ppermute x6, waiting for transfers between devices, moved(): lax.ppermute(x.astype(BF), 'ctx', [(i, to(i)) for i in range(ctx)])  2.92 us
  transfers between devices with their start and end apart: 9, of which 4 were waited for; matrix products, arithmetic and copies ran while one was open for 1% of the time, Pallas kernels for 6%

profile of v6, /device:TPU:1, one launch (start us, length us, event | category | flops | bytes accessed | tf_op | source)
XLA Modules:
  0.0 126.6 jit_solution(9388905992530117084)
XLA Ops:
  0.7 1.6 %tails.1 = bf16[16,1024]{1,0:T(8,128)(2,1)} custom-call(bf16[256,1024]{1,0:T(8,128)(2,1)} %q_ref.7, bf16[256,1024]{1,0:T(8,128)(2,1)} %k_ref.7, bf16[256,1024]{1,0:T(8,128)(2,1)} %v_ref.7), custom_call_target="tpu_custom_call" | custom-call | tf_op jit(solution)/shard_map/tails/pallas_call | solution.py:322
  2.2 4.6 %collective-permute-start = (bf16[16,1024]{1,0:T(8,128)(2,1)}, bf16[16,1024]{1,0:T(8,128)(2,1)S(1)}, u32[]{:S(2)}, u32[]{:S(2)}) collective-permute-start(bf16[16,1024]{1,0:T(8,128)(2,1)} %tails.1), channel_id=1, source_target_pairs={{0,8},{8,16},{16,24},{24,32},{32,40},{40,48},{48,56},{56,64},{64,7... | collective-permute-start | bytes 98312 | tf_op jit(solution)/shard_map/ppermute | solution.py:330
  6.8 1.0 copy-done.6
  7.9 0.2 pack_filter.1.buf_ref
  8.2 1.2 pack_signals.1
  9.4 51.4 %all_to_all.15.in_ref = bf16[32,3,2,32,128]{4,3,2,1,0:T(8,128)(2,1)S(1)} all-to-all(bf16[32,3,2,32,128]{4,3,2,1,0:T(8,128)(2,1)S(1)} %pack_signals.1), channel_id=1, replica_groups=mesh['ctx'=32,'tp'=8] {'ctx'}, dimensions={0} | all-to-all | bytes 3145728 | tf_op jit(solution)/shard_map/all_to_all | solution.py:351
  60.8 4.8 %spectral.1 = (bf16[32,2,2,32,128]{4,3,2,1,0:T(8,128)(2,1)S(1)}, bf16[32,1,2,32,128]{4,3,2,1,0:T(8,128)(2,1)S(1)}) custom-call(bf16[32,3,2,32,128]{4,3,2,1,0:T(8,128)(2,1)S(1)} %all_to_all.15.in_ref, bf16[128,64]{1,0:T(8,128)(2,1)S(1)} %copy-done.10, bf16[64,128]{1,0:T(8,128)(2,1)S(1)} %copy-done.11, bf16[256,256]{1,0:T(8,128)(2,1)S(1)} %copy-done.8, ...), custom_call_target="tpu_custom_call" | custom-call | tf_op jit(solution)/shard_map/spectral/pallas_call | solution.py:353
  65.6 31.9 %all_to_all.16.in_ref = bf16[32,2,2,32,128]{4,3,2,1,0:T(8,128)(2,1)S(1)} all-to-all(bf16[32,2,2,32,128]{4,3,2,1,0:T(8,128)(2,1)S(1)} %get-tuple-element.20), channel_id=1, replica_groups=mesh['ctx'=32,'tp'=8] {'ctx'}, dimensions={0} | all-to-all | bytes 2097152 | tf_op jit(solution)/shard_map/all_to_all | solution.py:361
  97.5 5.4 %all-to-all-start.2 = ((bf16[32,1,2,32,128]{4,3,2,1,0:T(8,128)(2,1)}), bf16[32,1,2,32,128]{4,3,2,1,0:T(8,128)(2,1)}, u32[]{:S(2)}, u32[]{:S(2)}) async-start(bf16[32,1,2,32,128]{4,3,2,1,0:T(8,128)(2,1)} %copy-done.5), calls=%async_computation.2 | async-start | bytes 1048576 | tf_op jit(solution)/shard_map/all_to_all | solution.py:362
  102.9 2.0 %sums.1 = bf16[16,1024]{1,0:T(8,128)(2,1)S(1)} custom-call(bf16[256,1024]{1,0:T(8,128)(2,1)S(1)} %copy-done, bf16[256,1024]{1,0:T(8,128)(2,1)S(1)} %copy-done.1, bf16[256,1024]{1,0:T(8,128)(2,1)S(1)} %copy-done.2, bf16[256,1024]{1,0:T(8,128)(2,1)S(1)} %copy-done.3, bf16[16,1024]{1,0:T(8,128)(2,1)S(1)} %collective-permute-done.halo_ref, ...), custom_call_target="tpu_custom_call" | custom-call | tf_op jit(solution)/shard_map/sums/pallas_call | solution.py:368
  104.9 1.7 %collective-permute-start.3 = (bf16[16,1024]{1,0:T(8,128)(2,1)S(1)}, bf16[16,1024]{1,0:T(8,128)(2,1)S(1)}, u32[]{:S(2)}, u32[]{:S(2)}) collective-permute-start(bf16[16,1024]{1,0:T(8,128)(2,1)S(1)} %sums.1), channel_id=1, source_target_pairs={{0,24},{8,16},{16,8},{24,0},{32,56},{40,48},{48,40},{56,32},{64,88... | collective-permute-start | bytes 98312 | tf_op jit(solution)/shard_map/ppermute | solution.py:275
  106.6 0.1 collective-permute-start.2
  106.8 0.4 collective-permute-start.1
  107.1 0.5 iota_compare_fusion
  107.6 3.7 %finish.1 = (bf16[256,1024]{1,0:T(8,128)(2,1)}, bf16[256,1024]{1,0:T(8,128)(2,1)}, bf16[256,1024]{1,0:T(8,128)(2,1)}, bf16[256,1024]{1,0:T(8,128)(2,1)}, f32[3,16,1024]{2,1,0:T(8,128)S(1)}) custom-call(bf16[256,1024]{1,0:T(8,128)(2,1)S(1)} %copy-done, bf16[256,1024]{1,0:T(8,128)(2,1)S(1)} %copy-done.1, bf16[256,1024]{1,0:T(8,128)(2,1)S(1)} %copy-done.2, ...), custom_call_target="tpu_custom_call" | custom-call | tf_op jit(solution)/shard_map/finish/pallas_call | solution.py:377
  111.4 3.7 %collective-permute-start.6 = (bf16[16,1024]{1,0:T(8,128)(2,1)S(1)}, bf16[16,1024]{1,0:T(8,128)(2,1)S(1)}, u32[]{:S(2)}, u32[]{:S(2)}) collective-permute-start(bf16[16,1024]{1,0:T(8,128)(2,1)S(1)} %convert_element_type.36), channel_id=1, source_target_pairs={{0,192},{8,200},{16,208},{24,216},{32,224},{40,232},{48,240},{56,2... | collective-permute-start | bytes 98312 | tf_op jit(solution)/shard_map/ppermute | solution.py:275
  115.2 4.1 %collective-permute-start.4 = (bf16[16,1024]{1,0:T(8,128)(2,1)S(1)}, bf16[16,1024]{1,0:T(8,128)(2,1)S(1)}, u32[]{:S(2)}, u32[]{:S(2)}) collective-permute-start(bf16[16,1024]{1,0:T(8,128)(2,1)S(1)} %convert_element_type.36), channel_id=1, source_target_pairs={{0,128},{8,136},{16,144},{24,152},{32,160},{40,168},{48,176},{56,1... | collective-permute-start | bytes 98312 | tf_op jit(solution)/shard_map/ppermute | solution.py:275
  119.3 1.4 %collective-permute-done.5 = bf16[16,1024]{1,0:T(8,128)(2,1)S(1)} collective-permute-done((bf16[16,1024]{1,0:T(8,128)(2,1)S(1)}, bf16[16,1024]{1,0:T(8,128)(2,1)S(1)}, u32[]{:S(2)}, u32[]{:S(2)}) %collective-permute-start.5) | collective-permute-done | bytes 32800 | tf_op jit(solution)/shard_map/ppermute | solution.py:275
  120.6 1.5 %collective-permute-done.4 = bf16[16,1024]{1,0:T(8,128)(2,1)S(1)} collective-permute-done((bf16[16,1024]{1,0:T(8,128)(2,1)S(1)}, bf16[16,1024]{1,0:T(8,128)(2,1)S(1)}, u32[]{:S(2)}, u32[]{:S(2)}) %collective-permute-start.4) | collective-permute-done | bytes 32800 | tf_op jit(solution)/shard_map/ppermute | solution.py:275
  122.2 0.7 fusion.3
  122.9 0.5 collective-permute-start.7
  123.5 1.9 %unpack_filter.1 = bf16[256,1024]{1,0:T(8,128)(2,1)} custom-call(bf16[32,1,2,32,128]{4,3,2,1,0:T(8,128)(2,1)} %all-to-all-done.2.in_ref), custom_call_target="tpu_custom_call" | custom-call | tf_op jit(solution)/shard_map/unpack_filter/pallas_call | solution.py:388
  125.4 0.4 collective-permute-done.7.other_ref
  125.8 0.7 close.1
  (34 shorter events, 0.2 us)
Async XLA Ops:
  0.6 7.5 %copy-start.2 = (bf16[256,1024]{1,0:T(8,128)(2,1)S(1)}, bf16[256,1024]{1,0:T(8,128)(2,1)}, u32[]{:S(2)}) copy-start(bf16[256,1024]{1,0:T(8,128)(2,1)} %v_ref.7) | copy-start | bytes 1572868
  0.6 7.5 %copy-start.1 = (bf16[256,1024]{1,0:T(8,128)(2,1)S(1)}, bf16[256,1024]{1,0:T(8,128)(2,1)}, u32[]{:S(2)}) copy-start(bf16[256,1024]{1,0:T(8,128)(2,1)} %k_ref.7) | copy-start | bytes 1572868
  0.7 7.5 %copy-start = (bf16[256,1024]{1,0:T(8,128)(2,1)S(1)}, bf16[256,1024]{1,0:T(8,128)(2,1)}, u32[]{:S(2)}) copy-start(bf16[256,1024]{1,0:T(8,128)(2,1)} %q_ref.7) | copy-start | bytes 1572868
  0.7 7.5 %copy-start.4 = (f32[3,3,1024]{2,1,0:T(4,128)S(1)}, f32[3,3,1024]{2,1,0:T(4,128)}, u32[]{:S(2)}) copy-start(f32[3,3,1024]{2,1,0:T(4,128)} %w_ref.8) | copy-start | bytes 110596
  0.7 7.5 %copy-start.3 = (bf16[256,1024]{1,0:T(8,128)(2,1)S(1)}, bf16[256,1024]{1,0:T(8,128)(2,1)}, u32[]{:S(2)}) copy-start(bf16[256,1024]{1,0:T(8,128)(2,1)} %cot_ref.5) | copy-start | bytes 1572868
  2.2 5.9 %collective-permute-start = (bf16[16,1024]{1,0:T(8,128)(2,1)}, bf16[16,1024]{1,0:T(8,128)(2,1)S(1)}, u32[]{:S(2)}, u32[]{:S(2)}) collective-permute-start(bf16[16,1024]{1,0:T(8,128)(2,1)} %tails.1), channel_id=1, source_target_pairs={{0,8},{8,16},{16,24},{24,32},{32,40},{40,48},{48,56},{56,64},{64,7... | collective-permute-start | bytes 98312 | tf_op jit(solution)/shard_map/ppermute | solution.py:330
  6.8 1.0 copy-start.6
  9.3 51.5 %copy-start.7 = (bf16[256,256]{1,0:T(8,128)(2,1)S(1)}, bf16[256,256]{1,0:T(8,128)(2,1)}, u32[]{:S(2)}) copy-start(bf16[256,256]{1,0:T(8,128)(2,1)} %constant.64.clone.wi_ref) | copy-start | bytes 393220
  9.4 51.5 %copy-start.8 = (bf16[256,256]{1,0:T(8,128)(2,1)S(1)}, bf16[256,256]{1,0:T(8,128)(2,1)}, u32[]{:S(2)}) copy-start(bf16[256,256]{1,0:T(8,128)(2,1)} %constant.63.clone.w_ref) | copy-start | bytes 393220
  9.4 51.5 %copy-start.9 = (f32[2,64,128]{2,1,0:T(8,128)S(1)}, f32[2,64,128]{2,1,0:T(8,128)}, u32[]{:S(2)}) copy-start(f32[2,64,128]{2,1,0:T(8,128)} %constant.65.clone.turn_ref) | copy-start | bytes 196612
  9.4 51.4 %copy-start.10 = (bf16[128,64]{1,0:T(8,128)(2,1)S(1)}, bf16[128,64]{1,0:T(8,128)(2,1)}, u32[]{:S(2)}) copy-start(bf16[128,64]{1,0:T(8,128)(2,1)} %constant.61.clone.a_ref) | copy-start | bytes 49156
  9.4 51.4 %copy-start.11 = (bf16[64,128]{1,0:T(8,128)(2,1)S(1)}, bf16[64,128]{1,0:T(8,128)(2,1)}, u32[]{:S(2)}) copy-start(bf16[64,128]{1,0:T(8,128)(2,1)} %constant.62.clone.b_ref) | copy-start | bytes 49156
  65.6 31.9 %copy-start.5 = (bf16[32,1,2,32,128]{4,3,2,1,0:T(8,128)(2,1)}, bf16[32,1,2,32,128]{4,3,2,1,0:T(8,128)(2,1)S(1)}, u32[]{:S(2)}) copy-start(bf16[32,1,2,32,128]{4,3,2,1,0:T(8,128)(2,1)S(1)} %get-tuple-element.33) | copy-start | bytes 1572868
  97.5 25.9 %all-to-all-start.2 = ((bf16[32,1,2,32,128]{4,3,2,1,0:T(8,128)(2,1)}), bf16[32,1,2,32,128]{4,3,2,1,0:T(8,128)(2,1)}, u32[]{:S(2)}, u32[]{:S(2)}) async-start(bf16[32,1,2,32,128]{4,3,2,1,0:T(8,128)(2,1)} %copy-done.5), calls=%async_computation.2 | async-start | bytes 1048576 | tf_op jit(solution)/shard_map/all_to_all | solution.py:362
  104.9 6.4 %collective-permute-start.3 = (bf16[16,1024]{1,0:T(8,128)(2,1)S(1)}, bf16[16,1024]{1,0:T(8,128)(2,1)S(1)}, u32[]{:S(2)}, u32[]{:S(2)}) collective-permute-start(bf16[16,1024]{1,0:T(8,128)(2,1)S(1)} %sums.1), channel_id=1, source_target_pairs={{0,24},{8,16},{16,8},{24,0},{32,56},{40,48},{48,40},{56,32},{64,88... | collective-permute-start | bytes 98312 | tf_op jit(solution)/shard_map/ppermute | solution.py:275
  106.6 4.7 %collective-permute-start.2 = (bf16[16,1024]{1,0:T(8,128)(2,1)S(1)}, bf16[16,1024]{1,0:T(8,128)(2,1)S(1)}, u32[]{:S(2)}, u32[]{:S(2)}) collective-permute-start(bf16[16,1024]{1,0:T(8,128)(2,1)S(1)} %sums.1), channel_id=1, source_target_pairs={{0,16},{8,24},{16,0},{24,8},{32,48},{40,56},{48,32},{56,40},{64,80... | collective-permute-start | bytes 98312 | tf_op jit(solution)/shard_map/ppermute | solution.py:275
  106.8 4.6 %collective-permute-start.1 = (bf16[16,1024]{1,0:T(8,128)(2,1)S(1)}, bf16[16,1024]{1,0:T(8,128)(2,1)S(1)}, u32[]{:S(2)}, u32[]{:S(2)}) collective-permute-start(bf16[16,1024]{1,0:T(8,128)(2,1)S(1)} %sums.1), channel_id=1, source_target_pairs={{0,8},{8,0},{16,24},{24,16},{32,40},{40,32},{48,56},{56,48},{64,72... | collective-permute-start | bytes 98312 | tf_op jit(solution)/shard_map/ppermute | solution.py:275
  107.6 3.7 %copy-start.12 = (pred[16]{0:T(512)(128)(4,1)S(1)}, pred[16]{0:T(512)(128)(4,1)}, u32[]{:S(2)}) copy-start(pred[16]{0:T(512)(128)(4,1)} %iota_compare_fusion) | copy-start | bytes 52
  111.4 7.9 %collective-permute-start.6 = (bf16[16,1024]{1,0:T(8,128)(2,1)S(1)}, bf16[16,1024]{1,0:T(8,128)(2,1)S(1)}, u32[]{:S(2)}, u32[]{:S(2)}) collective-permute-start(bf16[16,1024]{1,0:T(8,128)(2,1)S(1)} %convert_element_type.36), channel_id=1, source_target_pairs={{0,192},{8,200},{16,208},{24,216},{32,224},{40,232},{48,240},{56,2... | collective-permute-start | bytes 98312 | tf_op jit(solution)/shard_map/ppermute | solution.py:275
  115.2 5.5 %collective-permute-start.5 = (bf16[16,1024]{1,0:T(8,128)(2,1)S(1)}, bf16[16,1024]{1,0:T(8,128)(2,1)S(1)}, u32[]{:S(2)}, u32[]{:S(2)}) collective-permute-start(bf16[16,1024]{1,0:T(8,128)(2,1)S(1)} %convert_element_type.36), channel_id=1, source_target_pairs={{0,64},{8,72},{16,80},{24,88},{32,96},{40,104},{48,112},{56,120},{... | collective-permute-start | bytes 98312 | tf_op jit(solution)/shard_map/ppermute | solution.py:275
  115.2 7.0 %collective-permute-start.4 = (bf16[16,1024]{1,0:T(8,128)(2,1)S(1)}, bf16[16,1024]{1,0:T(8,128)(2,1)S(1)}, u32[]{:S(2)}, u32[]{:S(2)}) collective-permute-start(bf16[16,1024]{1,0:T(8,128)(2,1)S(1)} %convert_element_type.36), channel_id=1, source_target_pairs={{0,128},{8,136},{16,144},{24,152},{32,160},{40,168},{48,176},{56,1... | collective-permute-start | bytes 98312 | tf_op jit(solution)/shard_map/ppermute | solution.py:275
  122.9 2.8 %collective-permute-start.7 = (bf16[16,1024]{1,0:T(8,128)(2,1)S(1)}, bf16[16,1024]{1,0:T(8,128)(2,1)S(1)}, u32[]{:S(2)}, u32[]{:S(2)}) collective-permute-start(bf16[16,1024]{1,0:T(8,128)(2,1)S(1)} %get-tuple-element.34), channel_id=1, source_target_pairs={{0,32},{8,40},{16,48},{24,56},{32,0},{40,8},{48,16},{56,24},{64,96... | collective-permute-start | bytes 98312 | tf_op jit(solution)/shard_map/ppermute | solution.py:290
